TPU v7x, 128 devices: a whole 4x4x4 slice. The times are simulated.
128 devices in a mesh: exp: 16 (over y, z_lo, core), fsdp: 8 (over z_hi, x).
Axes of the slice: x: 4, y: 4, z: 4 (z_hi: 2, z_lo: 2; z = z_hi * 2 + z_lo), core: 2. Of those that a mesh axis runs over, the one named last changes fastest.
Arguments:
- tokens: bfloat16 [16384, 2048], P(('exp', 'fsdp')), may hold values from -6 to 6
- cotangent: bfloat16 [16384, 2048], P(('exp', 'fsdp')), may hold values from -0.29882812 to 0.29882812
- routes: int32 [16384, 6], P(('exp', 'fsdp')), may hold values from 0 to 31, all different within a row; in each aligned block of 128 rows (0 to 127, 128 to 255, ...) at most 28 rows name the same one
- probs: float32 [16384, 6], P(('exp', 'fsdp')), may hold values from 0.1 to 1
- w_gate_up: bfloat16 [32, 2048, 1408], P('exp', 'fsdp'), may hold values from -0.125 to 0.125
- w_down: bfloat16 [32, 704, 2048], P('exp', None, 'fsdp'), may hold values from -0.21875 to 0.21875
Outputs:
- d_tokens: bfloat16 [16384, 2048], P(('exp', 'fsdp'))
- d_probs: float32 [16384, 6], P(('exp', 'fsdp'))
- grad_gate_up: bfloat16 [32, 2048, 1408], P('exp', 'fsdp')
- grad_down: bfloat16 [32, 704, 2048], P('exp', None, 'fsdp')
Inputs may be any that keep to these rules, and one draw needn't show every extreme that they name: `routes`: each row names 6 different experts; among the rows of one device no expert is named more than 28 times.
All inputs are finite; a program needn't handle non-finite values.
Results may differ from a plain program's by a relative error of at most 0.02.
Values may be sent and summed in bfloat16 or wider, within the bound.
No kernel may reach another device: no remote copies, remote signals or barrier semaphores. Data moves between devices by JAX's collectives and lax.ppermute only.
A program may use at most 128 MiB of HBM per device.

v0:
```python
import jax
import jax.numpy as jnp
from jax import lax
from jax.sharding import PartitionSpec as P

TOP = 6


def expert_rows(rows_in, cotan_rows, weights_in, gate_up_matrix, down_matrix):
    half = gate_up_matrix.shape[1] // 2
    both = jnp.dot(rows_in, gate_up_matrix, preferred_element_type=jnp.float32)
    gate_value = both[:, :half]
    up_value = both[:, half:]
    logistic = jax.nn.sigmoid(gate_value)
    activated = gate_value * logistic
    hidden = (activated * up_value).astype(jnp.bfloat16)
    back_proj = lax.dot_general(
        cotan_rows, down_matrix, (((1,), (1,)), ((), ())), preferred_element_type=jnp.float32
    )
    expert_out = jnp.dot(hidden, down_matrix, preferred_element_type=jnp.float32)
    prob_grad = jnp.sum(cotan_rows.astype(jnp.float32) * expert_out, axis=1)
    scaled = (weights_in[:, None] * cotan_rows.astype(jnp.float32)).astype(jnp.bfloat16)
    d_hidden = weights_in[:, None] * back_proj
    d_upper = (d_hidden * activated).astype(jnp.bfloat16)
    d_gating = (d_hidden * up_value * logistic * (1.0 + gate_value * (1.0 - logistic))).astype(
        jnp.bfloat16
    )
    d_both = jnp.concatenate([d_gating, d_upper], axis=1)
    part_gate_up = lax.dot_general(
        rows_in, d_both, (((0,), (0,)), ((), ())), preferred_element_type=jnp.float32
    )
    part_down = lax.dot_general(
        hidden, scaled, (((0,), (0,)), ((), ())), preferred_element_type=jnp.float32
    )
    copy_grad = lax.dot_general(
        d_both, gate_up_matrix, (((1,), (1,)), ((), ())), preferred_element_type=jnp.float32
    )
    return (part_gate_up, part_down, copy_grad.astype(jnp.bfloat16), prob_grad)


def body(tokens, cotangent, routes, probs, w_gate_up, w_down):
    tok_rows, model_width = tokens.shape
    local_count = w_gate_up.shape[0]
    groups = lax.axis_size("exp")
    experts = local_count * groups
    capacity = 7 * tok_rows * TOP // (6 * experts)
    copies = tok_rows * TOP
    flat_routes = routes.reshape(-1)
    flat_probs = probs.reshape(-1)
    onehot = (flat_routes[:, None] == jnp.arange(experts, dtype=jnp.int32)[None, :]).astype(
        jnp.int32
    )
    ranking = jnp.cumsum(onehot, axis=0) - 1
    slot_index = jnp.sum(ranking * onehot, axis=1)
    target = flat_routes * capacity + slot_index
    source = (
        jnp.full((experts * capacity,), copies, jnp.int32)
        .at[target]
        .set(jnp.arange(copies, dtype=jnp.int32))
    )
    filled = source < copies
    safe_index = jnp.minimum(source, copies - 1)
    token_index = safe_index // TOP
    x_send = jnp.where(filled[:, None], tokens[token_index], jnp.zeros((), jnp.bfloat16))
    x_send = x_send.reshape(groups, local_count, capacity, model_width)
    dy_send = jnp.where(filled[:, None], cotangent[token_index], jnp.zeros((), jnp.bfloat16))
    dy_send = dy_send.reshape(groups, local_count, capacity, model_width)
    p_send = jnp.where(filled, flat_probs[safe_index], jnp.zeros((), jnp.float32)).reshape(
        groups, local_count, capacity
    )
    x_recv, dy_recv, p_recv = (
        lax.all_to_all(x_send, "exp", split_axis=0, concat_axis=2, tiled=True),
        lax.all_to_all(dy_send, "exp", split_axis=0, concat_axis=2, tiled=True),
        lax.all_to_all(
            p_send.astype(jnp.bfloat16), "exp", split_axis=0, concat_axis=2, tiled=True
        ).astype(p_send.dtype),
    )
    results = []
    full_gate_up, full_down = (
        lax.all_gather(w_gate_up, "fsdp", axis=1, tiled=True),
        lax.all_gather(w_down, "fsdp", axis=2, tiled=True),
    )
    for index in range(local_count):
        results.append(
            expert_rows(
                x_recv[0, index],
                dy_recv[0, index],
                p_recv[0, index],
                full_gate_up[index],
                full_down[index],
            )
        )
    summed = (
        lax.psum_scatter(
            jnp.stack([member[0] for member in results]).astype(jnp.bfloat16),
            "fsdp",
            scatter_dimension=1,
            tiled=True,
        ).astype(jnp.float32),
        lax.psum_scatter(
            jnp.stack([member[1] for member in results]).astype(jnp.bfloat16),
            "fsdp",
            scatter_dimension=2,
            tiled=True,
        ).astype(jnp.float32),
    )
    grad_gate_up = summed[0].astype(jnp.bfloat16)
    grad_down = summed[1].astype(jnp.bfloat16)
    dx_all = jnp.stack([member[2] for member in results])[None]
    dprob_all = jnp.stack([member[3] for member in results])[None]
    dx_back, dprob_back = (
        lax.all_to_all(dx_all, "exp", split_axis=2, concat_axis=0, tiled=True),
        lax.all_to_all(
            dprob_all.astype(jnp.bfloat16), "exp", split_axis=2, concat_axis=0, tiled=True
        ).astype(dprob_all.dtype),
    )
    dx_rows = dx_back.reshape(experts * capacity, model_width)[target]
    d_tokens = jnp.sum(
        dx_rows.astype(jnp.float32).reshape(tok_rows, TOP, model_width), axis=1
    ).astype(jnp.bfloat16)
    d_probs = dprob_back.reshape(-1)[target].reshape(tok_rows, TOP)
    return (d_tokens, d_probs, grad_gate_up, grad_down)


def solution(mesh):
    placed = (
        P(("exp", "fsdp"), None),
        P(("exp", "fsdp"), None),
        P(("exp", "fsdp"), None),
        P(("exp", "fsdp"), None),
        P("exp", "fsdp", None),
        P("exp", None, "fsdp"),
    )
    return jax.shard_map(
        body,
        mesh=mesh,
        in_specs=placed,
        out_specs=(
            P(("exp", "fsdp"), None),
            P(("exp", "fsdp"), None),
            P("exp", "fsdp", None),
            P("exp", None, "fsdp"),
        ),
        check_vma=False,
    )
```

profile of v0, /device:TPU:1, one launch (start us, length us, event | category | flops | bytes accessed | tf_op | source)
XLA Modules:
  0.0 620.7 jit_solution(9275712233499451757)
XLA Ops:
  7.2 0.7 all-gather.5.cloned.1.call-update
  7.9 0.8 copy.71
  8.7 0.1 eq.29
  8.8 0.1 eq.25
  9.0 0.8 copy.74
  9.8 0.1 reshape.143
  9.9 0.7 broadcast_multiply_fusion
  10.8 0.1 mul.105
  10.9 1.7 reduce-window.6
  12.7 0.3 slice_reduce_fusion
  13.1 3.4 scatter_custom_fusion
  16.5 5.8 gather_fusion
  22.3 0.7 convert_element_type.102
  23.0 7.3 %all-to-all-start = ((bf16[16,2,28]{2,1,0:T(2,128)(2,1)}), bf16[16,2,28]{2,1,0:T(2,128)(2,1)S(1)}, u32[]{:S(2)}, u32[]{:S(2)}) async-start(bf16[16,2,28]{2,1,0:T(2,128)(2,1)} %convert_element_type.102), calls=%async_computation | async-start | bytes 16384 | tf_op jit(solution)/shard_map/all_to_all | solution.py:74
  30.4 0.7 all-gather.3.cloned.1.call-update
  31.3 5.0 gather_fusion.2
  36.3 5.9 gather.25
  42.2 5.0 gather_fusion.1
  47.1 5.9 gather.23
  53.0 5.2 broadcast_select_fusion
  58.2 6.1 copy.76
  64.3 6.1 all-to-all-start.1
  70.4 7.8 %copy.78 = bf16[16,2,28,2048]{3,1,2,0:T(2,128)(2,1)} copy(bf16[16,2,28,2048]{3,2,1,0:T(8,128)(2,1)} %get-tuple-element.36) | data formatting | bytes 7340032 | tf_op jit(solution)/shard_map/jit(_where)/select_n | solution.py:64
  78.2 44.5 %all-to-all-done.1 = bf16[16,2,28,2048]{3,1,2,0:T(2,128)(2,1)} async-done(((bf16[16,2,28,2048]{3,1,2,0:T(2,128)(2,1)}), bf16[16,2,28,2048]{3,1,2,0:T(2,128)(2,1)}, u32[]{:S(2)}, u32[]{:S(2)}) %all-to-all-start.1) | async-done | bytes 3670048 | tf_op jit(solution)/shard_map/all_to_all | solution.py:73
  122.7 4.7 all-to-all-start.2
  127.5 8.9 %fusion.46 = (bf16[1,1,448,2048]{3,1,2,0:T(2,128)(2,1)}, bf16[1,1,448,2048]{3,1,2,0:T(2,128)(2,1)}) fusion(bf16[1,2,448,2048]{3,1,2,0:T(2,128)(2,1)} %bitcast.6), kind=kLoop, calls=%fused_computation.98 | loop fusion | bytes 7340032 | tf_op jit(solution)/shard_map/slice | solution.py:87
  136.5 43.3 %all-to-all-done.2 = bf16[16,2,28,2048]{3,1,2,0:T(2,128)(2,1)} async-done(((bf16[16,2,28,2048]{3,1,2,0:T(2,128)(2,1)}), bf16[16,2,28,2048]{3,1,2,0:T(2,128)(2,1)}, u32[]{:S(2)}, u32[]{:S(2)}) %all-to-all-start.2) | async-done | bytes 3670048 | tf_op jit(solution)/shard_map/all_to_all | solution.py:72
  179.8 8.9 %fusion.45 = (bf16[1,1,448,2048]{3,1,2,0:T(2,128)(2,1)}, bf16[1,1,448,2048]{3,1,2,0:T(2,128)(2,1)}) fusion(bf16[1,2,448,2048]{3,1,2,0:T(2,128)(2,1)} %bitcast.11), kind=kLoop, calls=%fused_computation.97 | loop fusion | bytes 7340032 | tf_op jit(solution)/shard_map/slice | solution.py:86
  188.7 40.9 %all-gather.5.cloned.1.call-done = bf16[2,2048,1408]{2,1,0:T(8,128)(2,1)} async-done(((bf16[2,256,1408]{2,1,0:T(8,128)(2,1)}), bf16[2,2048,1408]{2,1,0:T(8,128)(2,1)}) %all-gather.5.cloned.1.call-update) | async-done | bytes 11534352 | tf_op jit(solution)/shard_map/all_gather | solution.py:80
  229.6 7.3 %fusion.3 = f32[448,1408]{1,0:T(8,128)S(1)} fusion(bf16[2,2048,1408]{2,1,0:T(8,128)(2,1)} %all-gather.5.cloned.1.call-done, bf16[1,1,448,2048]{3,1,2,0:T(2,128)(2,1)} %get-tuple-element.30), kind=kOutput, calls=%fused_computation.15 | convolution fusion | flops 2583691264 | bytes 11960320 | tf_op jit(solution)/shard_map/dot_general | solution.py:11
  237.0 86.2 %all-gather.3.cloned.1.call-done = bf16[2,704,2048]{2,1,0:T(8,128)(2,1)} async-done(((bf16[2,704,256]{2,1,0:T(8,128)(2,1)}), bf16[2,704,2048]{2,1,0:T(8,128)(2,1)}) %all-gather.3.cloned.1.call-update) | async-done | bytes 5767184 | tf_op jit(solution)/shard_map/all_gather | solution.py:81
  323.2 6.9 %multiply_convert_fusion.5 = (bf16[448,704]{1,0:T(8,128)(2,1)}, bf16[448,704]{1,0:T(8,128)(2,1)}, bf16[448,704]{1,0:T(8,128)(2,1)S(1)}) fusion(f32[448,1408]{1,0:T(8,128)S(1)} %fusion.3, bf16[2,704,2048]{2,1,0:T(8,128)(2,1)} %all-gather.3.cloned.1.call-done, bf16[1,1,448,2048]{3,1,2,0:T(2,128)(2,1)} %get-tuple-element.32, f32[448]{0:T(512)S(1)} %bitcast.128), kind=kOutput, calls=%fused_computation.58 | convolution fusion | flops 1296891904 | bytes 10970880 | tf_op jit(solution)/shard_map/dot_general | solution.py:17
  330.2 2.5 fusion.10
  332.7 0.7 slice-done.2
  333.4 3.3 fusion.5
  336.8 3.6 multiply_convert_fusion.3
  340.4 2.5 fusion.11
  342.9 3.2 pad_maximum_fusion.1
  346.1 1.0 copy-done.10
  347.2 0.2 copy-done.11
  347.4 8.3 %fusion = bf16[1,2048,1408]{2,1,0:T(8,128)(2,1)S(1)} fusion(bf16[448,704]{1,0:T(8,128)(2,1)S(1)} %copy-done.11, bf16[448,704]{1,0:T(8,128)(2,1)S(1)} %copy-done.10, bf16[1,1,448,2048]{3,1,2,0:T(2,128)(2,1)} %get-tuple-element.30), kind=kOutput, calls=%fused_computation.9 | convolution fusion | flops 2589097984 | bytes 8863744 | tf_op jit(solution)/shard_map/dot_general | solution.py:29
  355.7 4.7 fusion.1
  360.4 5.2 pad_maximum_fusion
  365.6 1.1 copy-done.9
  366.7 5.5 fusion.6
  372.2 4.3 fusion.8
  376.6 0.9 copy.82
  377.4 6.2 all-to-all-start.4
  383.7 6.0 fusion.14
  389.6 5.7 fusion.15
  395.3 0.3 maximum_bitcast_fusion
  395.7 5.6 copy.80
  401.2 6.3 %all-to-all-start.3 = ((bf16[1,2,448,2048]{3,1,0,2:T(2,128)(2,1)}), bf16[1,2,448,2048]{3,1,0,2:T(2,128)(2,1)}, u32[]{:S(2)}, u32[]{:S(2)}) async-start(bf16[1,2,448,2048]{3,1,0,2:T(2,128)(2,1)} %copy.80), calls=%async_computation.3 | async-start | bytes 7340032 | tf_op jit(solution)/shard_map/all_to_all | solution.py:112
  407.5 0.1 copy.83
  407.9 3.2 gather_fusion.4
  411.1 0.1 reshape.145
  411.2 0.7 copy.85
  411.9 41.7 %all-to-all-done.3 = bf16[1,2,448,2048]{3,1,0,2:T(2,128)(2,1)} async-done(((bf16[1,2,448,2048]{3,1,0,2:T(2,128)(2,1)}), bf16[1,2,448,2048]{3,1,0,2:T(2,128)(2,1)}, u32[]{:S(2)}, u32[]{:S(2)}) %all-to-all-start.3) | async-done | bytes 3670048 | tf_op jit(solution)/shard_map/all_to_all | solution.py:112
  453.6 5.9 copy.81
  459.5 5.9 reshape.144
  465.4 9.6 %gather_fusion.3 = bf16[768,2048]{1,0:T(8,128)(2,1)} fusion(bf16[896,2048]{1,0:T(8,128)(2,1)} %reshape.144, s32[1024]{0:T(1024)S(1)} %pad_clamp_fusion), kind=kCustom, calls=%fused_computation.3 | custom fusion | bytes 6294528 | tf_op jit(solution)/shard_map/gather | solution.py:117
  475.0 6.3 %gather.27 = bf16[128,6,2048]{2,1,0:T(8,128)(2,1)} reshape(bf16[768,2048]{1,0:T(8,128)(2,1)} %gather_fusion.3) | data formatting | bytes 6291456 | tf_op jit(solution)/shard_map/gather | solution.py:117
  481.3 5.8 reduce_sum.43
  487.1 126.6 %reduce-scatter.3.cloned.1.call-done = bf16[2,256,1408]{2,1,0:T(8,128)(2,1)} async-done(((bf16[2,2048,1408]{2,1,0:T(8,128)(2,1)}), bf16[2,256,1408]{2,1,0:T(8,128)(2,1)}) %reduce-scatter.3.cloned.1.call-update) | async-done | bytes 1441808 | tf_op jit(solution)/shard_map/reduce_scatter | solution.py:94
  (70 shorter events, 1.0 us)
Async XLA Ops:
  7.2 24.1 %copy-start = (bf16[128,2048]{1,0:T(8,128)(2,1)S(1)}, bf16[128,2048]{1,0:T(8,128)(2,1)}, u32[]{:S(2)}) copy-start(bf16[128,2048]{1,0:T(8,128)(2,1)} %param.6) | copy-start | bytes 1572868
  7.2 222.5 %all-gather.5.cloned.1.call-start = ((), (), s32[]{:S(2)}) async-start(), calls=%async_computation.8 | async-start | bytes 12976128 | tf_op jit(solution)/shard_map/all_gather | solution.py:80
  23.0 41.2 %all-to-all-start = ((bf16[16,2,28]{2,1,0:T(2,128)(2,1)}), bf16[16,2,28]{2,1,0:T(2,128)(2,1)S(1)}, u32[]{:S(2)}, u32[]{:S(2)}) async-start(bf16[16,2,28]{2,1,0:T(2,128)(2,1)} %convert_element_type.102), calls=%async_computation | async-start | bytes 16384 | tf_op jit(solution)/shard_map/all_to_all | solution.py:74
  30.4 292.9 %all-gather.3.cloned.1.call-start = ((), (), s32[]{:S(2)}) async-start(), calls=%async_computation.7 | async-start | bytes 6488064 | tf_op jit(solution)/shard_map/all_gather | solution.py:81
  36.3 5.9 copy-start.2
  64.3 58.4 %all-to-all-start.1 = ((bf16[16,2,28,2048]{3,1,2,0:T(2,128)(2,1)}), bf16[16,2,28,2048]{3,1,2,0:T(2,128)(2,1)}, u32[]{:S(2)}, u32[]{:S(2)}) async-start(bf16[16,2,28,2048]{3,1,2,0:T(2,128)(2,1)} %copy.76), calls=%async_computation.1 | async-start | bytes 7340032 | tf_op jit(solution)/shard_map/all_to_all | solution.py:73
  122.7 57.1 %all-to-all-start.2 = ((bf16[16,2,28,2048]{3,1,2,0:T(2,128)(2,1)}), bf16[16,2,28,2048]{3,1,2,0:T(2,128)(2,1)}, u32[]{:S(2)}, u32[]{:S(2)}) async-start(bf16[16,2,28,2048]{3,1,2,0:T(2,128)(2,1)} %copy.78), calls=%async_computation.2 | async-start | bytes 7340032 | tf_op jit(solution)/shard_map/all_to_all | solution.py:72
  127.3 359.8 %reduce-scatter.5.cloned.1.call-start = ((), (), s32[]{:S(2)}) async-start(), calls=%async_computation.10 | async-start | bytes 6488064 | tf_op jit(solution)/shard_map/reduce_scatter | solution.py:100
  323.2 6.9 %copy-start.5 = (bf16[1,1,448,2048]{3,1,2,0:T(2,128)(2,1)S(1)}, bf16[1,1,448,2048]{3,1,2,0:T(2,128)(2,1)}, u32[]{:S(2)}) copy-start(bf16[1,1,448,2048]{3,1,2,0:T(2,128)(2,1)} %get-tuple-element.32) | copy-start | bytes 5505028
  323.2 9.5 %slice-start = ((s8[11534336]{0:T(1024)(128)(4,1)}), s8[4194304]{0:T(1024)(128)(4,1)S(1)}, s32[]{:S(2)}) async-start(s8[11534336]{0:T(1024)(128)(4,1)} %bitcast.130), calls=%async_computation.11 | async-start | bytes 8388608
  323.2 9.5 %slice-start.1 = ((s8[11534336]{0:T(1024)(128)(4,1)}), s8[4194304]{0:T(1024)(128)(4,1)S(1)}, s32[]{:S(2)}) async-start(s8[11534336]{0:T(1024)(128)(4,1)} %bitcast.130), calls=%async_computation.12 | async-start | bytes 8388608
  330.2 2.5 copy-start.8
  330.2 2.5 copy-start.6
  330.2 3.2 slice-start.2
  330.2 6.6 %slice-start.3 = ((s8[5767168]{0:T(1024)(128)(4,1)}), s8[4194304]{0:T(1024)(128)(4,1)S(1)}, s32[]{:S(2)}) async-start(s8[5767168]{0:T(1024)(128)(4,1)} %bitcast.132), calls=%async_computation.14 | async-start | bytes 8388608
  333.4 3.4 copy-start.3
  333.4 3.4 slice-start.4
  340.4 15.2 %copy-start.12 = (bf16[448,704]{1,0:T(8,128)(2,1)}, bf16[448,704]{1,0:T(8,128)(2,1)S(1)}, u32[]{:S(2)}) copy-start(bf16[448,704]{1,0:T(8,128)(2,1)S(1)} %get-tuple-element.28) | copy-start | bytes 1892356
  346.1 1.1 copy-start.10
  346.1 1.3 copy-start.11
  346.1 267.6 %reduce-scatter.3.cloned.1.call-start = ((), (), s32[]{:S(2)}) async-start(), calls=%async_computation.9 | async-start | bytes 12976128 | tf_op jit(solution)/shard_map/reduce_scatter | solution.py:94
  347.4 8.3 %copy-start.7 = (bf16[1,1,448,2048]{3,1,2,0:T(2,128)(2,1)S(1)}, bf16[1,1,448,2048]{3,1,2,0:T(2,128)(2,1)}, u32[]{:S(2)}) copy-start(bf16[1,1,448,2048]{3,1,2,0:T(2,128)(2,1)} %get-tuple-element.31) | copy-start | bytes 5505028
  347.4 8.3 %copy-start.14 = (bf16[448,704]{1,0:T(8,128)(2,1)S(1)}, bf16[448,704]{1,0:T(8,128)(2,1)}, u32[]{:S(2)}) copy-start(bf16[448,704]{1,0:T(8,128)(2,1)} %get-tuple-element.29) | copy-start | bytes 1892356
  365.5 1.1 copy-start.9
  366.7 5.5 copy-start.4
  377.4 23.8 %all-to-all-start.4 = ((bf16[1,2,448]{1,0,2:T(2,128)(2,1)}), bf16[1,2,448]{1,0,2:T(2,128)(2,1)S(1)}, u32[]{:S(2)}, u32[]{:S(2)}) async-start(bf16[1,2,448]{1,0,2:T(2,128)(2,1)} %copy.82), calls=%async_computation.4 | async-start | bytes 458752 | tf_op jit(solution)/shard_map/all_to_all | solution.py:113
  383.6 6.0 copy-start.13
  383.6 6.0 copy-start.15
  401.2 52.4 %all-to-all-start.3 = ((bf16[1,2,448,2048]{3,1,0,2:T(2,128)(2,1)}), bf16[1,2,448,2048]{3,1,0,2:T(2,128)(2,1)}, u32[]{:S(2)}, u32[]{:S(2)}) async-start(bf16[1,2,448,2048]{3,1,0,2:T(2,128)(2,1)} %copy.80), calls=%async_computation.3 | async-start | bytes 7340032 | tf_op jit(solution)/shard_map/all_to_all | solution.py:112
  475.0 138.7 %copy-start.1 = (bf16[128,2048]{1,0:T(8,128)(2,1)S(1)}, bf16[128,2048]{1,0:T(8,128)(2,1)}, u32[]{:S(2)}) copy-start(bf16[128,2048]{1,0:T(8,128)(2,1)} %param.6) | copy-start | bytes 1572868
Sparse Core Ops, SparseCore 0:
  10.3 219.3 all-gather.4
  231.8 91.3 all-gather.2
  346.2 115.7 reduce-scatter.4
  466.9 146.8 reduce-scatter.2
where the time goes:
time: 629 us; the launch traced here: 621 us
  waiting for transfers between devices  385 us (61%)
  local copies, waits for them, and re-layouts  108 us (17%)
  matrix products  60.6 us (10%)
  starting transfers between devices  30.7 us (5%)
  other arithmetic  22.3 us (4%)
  between operations  14.7 us (2%)
    reduce_scatter x1, waiting for transfers between devices, body(): lax.psum_scatter(jnp.stack([member[0] for member in results]).astype(jnp....  127 us
    all_gather x1, waiting for transfers between devices, body(): lax.all_gather(w_down, 'fsdp', axis=2, tiled=True)  86.2 us
    all_to_all x1, waiting for transfers between devices, body(): lax.all_to_all(dy_send, 'exp', split_axis=0, concat_axis=2, tiled=True)  44.5 us
    all_to_all x1, waiting for transfers between devices, body(): lax.all_to_all(x_send, 'exp', split_axis=0, concat_axis=2, tiled=True)  43.3 us
    all_to_all x1, waiting for transfers between devices, body(): lax.all_to_all(dx_all, 'exp', split_axis=2, concat_axis=0, tiled=True)  41.7 us
    all_gather x1, waiting for transfers between devices, body(): lax.all_gather(w_gate_up, 'fsdp', axis=1, tiled=True)  40.9 us
    gather x2, local copies, waits for them, and re-layouts, body(): dx_rows = dx_back.reshape(experts * capacity, model_width)[target]  15.9 us
    dot_general x2, matrix products, expert_rows(): lax.dot_general(rows_in, d_both, (((0,), (0,)), ((), ())), preferred_elem...  13 us
  transfers between devices with their start and end apart: 9, of which 6 were waited for; matrix products, arithmetic and copies ran while one was open for 27% of the time, Pallas kernels for 0%

commit v1 on v0

v1 whole, which is shorter than its diff:
```python
import jax
import jax.numpy as jnp
from jax import lax
from jax.experimental import pallas as pl
from jax.experimental.pallas import tpu as pltpu
from jax.sharding import Mesh, PartitionSpec as P

TOP = 6
CAP = 28
D = 2048
F = 704
TOK = 128
WIDE = D + 128
ROWS = 8 * 4 * CAP
BLK = 4 * CAP
BF = jnp.bfloat16
F32 = jnp.float32
MIB = 1 << 20


def params(mib=48):
    return pltpu.CompilerParams(vmem_limit_bytes=mib * MIB)


def mm(a, b, ca=1, cb=0):
    return lax.dot_general(a, b, (((ca,), (cb,)), ((), ())), preferred_element_type=F32)


def whole(shape):
    return pl.BlockSpec(shape, lambda *_: (0,) * len(shape))


def cost(flops, moved):
    return pl.CostEstimate(flops=flops, bytes_accessed=moved, transcendentals=0)


def meta_kernel(tok, cot, routes, probs, out_tok, out_cot):
    lane = lax.broadcasted_iota(jnp.int32, (TOK, 128), 1)
    meta = jnp.zeros((TOK, 128), F32)
    chosen = routes[...].astype(F32)
    weight = probs[...]
    for k in range(TOP):
        meta = jnp.where(lane == k, chosen[:, k : k + 1], meta)
        meta = jnp.where(lane == 8 + k, weight[:, k : k + 1], meta)
    meta = meta.astype(BF)
    out_tok[:, :D] = tok[...]
    out_tok[:, D:] = meta
    out_cot[:, :D] = cot[...]
    out_cot[:, D:] = meta


def add_meta(tokens, cotangent, routes, probs):
    shape = jax.ShapeDtypeStruct((TOK, WIDE), BF)
    return pl.pallas_call(
        meta_kernel,
        out_shape=(shape, shape),
        compiler_params=params(16),
        cost_estimate=cost(0, 4 * TOK * WIDE * 2),
    )(tokens, cotangent, routes, probs)


def pick_matrix(metas, experts, bases, weighted, sel):
    earlier = (
        lax.broadcasted_iota(jnp.int32, (TOK, TOK), 0)
        < lax.broadcasted_iota(jnp.int32, (TOK, TOK), 1)
    ).astype(BF)
    places, weights = [], []
    for d in range(4):
        turned = metas[d][...].astype(F32).T
        mask = jnp.zeros((8, TOK), F32)
        weight = jnp.zeros((8, TOK), F32)
        for k in range(TOP):
            hit = turned[k : k + 1, :] == experts
            mask = jnp.where(hit, 1.0, mask)
            weight = jnp.where(hit, turned[8 + k : 9 + k, :], weight)
        rank = mm(mask.astype(BF), earlier)
        places.append(jnp.where(mask > 0.5, rank + bases[d], -1.0))
        weights.append(weight if weighted else mask)
    place = jnp.concatenate(places, axis=1)
    weight = jnp.concatenate(weights, axis=1)
    row = lax.broadcasted_iota(jnp.int32, (BLK, 4 * TOK), 0).astype(F32)
    for j in range(8):
        sel[j * BLK : (j + 1) * BLK, :] = jnp.where(
            row == place[j : j + 1, :], weight[j : j + 1, :], 0.0
        ).astype(BF)


def pick_tokens_kernel(sc, t0, t1, t2, t3, m0, m1, m2, m3, out, sel):
    y = sc[0]

    @pl.when(pl.program_id(0) == 0)
    def _():
        experts = (y * 8 + lax.broadcasted_iota(jnp.int32, (8, TOK), 0)).astype(F32)
        bases = [(((y - d) & 3) * CAP).astype(F32) for d in range(4)]
        pick_matrix((m0, m1, m2, m3), experts, bases, False, sel)

    table = jnp.concatenate([t0[...], t1[...], t2[...], t3[...]], axis=0)
    out[...] = mm(sel[...], table).astype(BF)


def pick_cotan_kernel(sc, t0, t1, t2, t3, m0, m1, m2, m3, *rest):
    outs, sel = rest[:8], rest[8]
    y, z_lo, core, z_hi = sc[0], sc[1], sc[2], sc[3]
    z = z_hi * 2 + z_lo

    @pl.when(pl.program_id(0) == 0)
    def _():
        index = lax.broadcasted_iota(jnp.int32, (8, TOK), 0)
        experts = jnp.zeros((8, TOK), jnp.int32)
        for j in range(8):
            to_y, to_core = (y + j % 4) & 3, core ^ (j // 4)
            experts = jnp.where(
                index == j, ((to_y * 2 + z_lo) * 2 + to_core) * 2 + z_hi, experts
            )
        bases = [(((z - d) & 3) * CAP).astype(F32) for d in range(4)]
        pick_matrix((m0, m1, m2, m3), experts.astype(F32), bases, True, sel)

    table = jnp.concatenate([t0[...], t1[...], t2[...], t3[...]], axis=0)
    rows = mm(sel[...], table).astype(BF)
    for j in range(8):
        outs[j][...] = rows[j * BLK : (j + 1) * BLK, :]


def pick(kernel, sc, sources, split):
    step = 512
    column = lambda n, sc: (0, n)
    last = lambda n, sc: (0, D // 128)
    if split:
        out_shape = [jax.ShapeDtypeStruct((BLK, D), BF)] * 8
        out_specs = [pl.BlockSpec((BLK, step), column)] * 8
        scratch = [pltpu.VMEM((ROWS, 4 * TOK), BF)]
    else:
        out_shape = [
            jax.ShapeDtypeStruct((ROWS, D), BF),
            jax.ShapeDtypeStruct((ROWS, 4 * TOK), BF),
        ]
        out_specs = [
            pl.BlockSpec((ROWS, step), column),
            pl.BlockSpec((ROWS, 4 * TOK), lambda n, sc: (0, 0)),
        ]
        scratch = []
    return pl.pallas_call(
        kernel,
        grid_spec=pltpu.PrefetchScalarGridSpec(
            num_scalar_prefetch=1,
            grid=(D // step,),
            in_specs=[pl.BlockSpec((TOK, step), column)] * 4
            + [pl.BlockSpec((TOK, 128), last)] * 4,
            out_specs=out_specs,
            scratch_shapes=scratch,
        ),
        out_shape=out_shape,
        compiler_params=params(),
        cost_estimate=cost(2 * ROWS * 512 * D, 6 * MIB),
    )(sc, *sources, *sources)


def forward_kernel(sc, rows, w_own, w_oth, hidden, act, slope):
    z_hi = sc[3]
    own = pl.multiple_of(z_hi * 1024, 1024)
    oth = pl.multiple_of((1 - z_hi) * 1024, 1024)
    both = mm(rows[:, pl.ds(own, 1024)], w_own[...]) + mm(
        rows[:, pl.ds(oth, 1024)], w_oth[...]
    )
    gate, up = both[:, :F], both[:, F:]
    logistic = jax.nn.sigmoid(gate)
    activated = gate * logistic
    hidden[...] = (activated * up).astype(BF)
    act[...] = activated
    slope[...] = up * logistic * (1.0 + gate * (1.0 - logistic))


def forward(sc, rows, w_own, w_oth):
    tile = ROWS // 2
    line = lambda m, sc: (m, 0)
    return pl.pallas_call(
        forward_kernel,
        grid_spec=pltpu.PrefetchScalarGridSpec(
            num_scalar_prefetch=1,
            grid=(2,),
            in_specs=[
                pl.BlockSpec((tile, D), line),
                whole((1024, 2 * F)),
                whole((1024, 2 * F)),
            ],
            out_specs=[pl.BlockSpec((tile, F), line)] * 3,
        ),
        out_shape=[
            jax.ShapeDtypeStruct((ROWS, F), BF),
            jax.ShapeDtypeStruct((ROWS, F), F32),
            jax.ShapeDtypeStruct((ROWS, F), F32),
        ],
        compiler_params=params(),
        cost_estimate=cost(2 * ROWS * D * 2 * F, 16 * MIB),
    )(sc, rows, w_own, w_oth)


def backward_kernel(sc, *refs):
    arrived, (w_own, w_oth, hidden, act, slope, scaled, d_both, q_out) = refs[:8], refs[8:]
    y, z_lo, core, z_hi = sc[0], sc[1], sc[2], sc[3]
    row = lax.broadcasted_iota(jnp.int32, (4 * BLK, 4 * BLK), 0)
    col = lax.broadcasted_iota(jnp.int32, (4 * BLK, 4 * BLK), 1)

    def split(v, size):
        major = sum([(v >= size * n).astype(jnp.int32) for n in range(1, 4)])
        return major, v - size * major

    row_z, row_rest = split(row, BLK)
    row_y, row_s = split(row_rest, CAP)
    col_d, col_rest = split(col, BLK)
    col_z, col_s = split(col_rest, CAP)
    turn = (
        (row_z == col_z) & (row_s == col_s) & (row_y == ((y - col_d) & 3))
    ).astype(F32).astype(BF)
    for dc in range(2):
        from_core = core ^ dc
        for n in range(0, D, 512):
            table = jnp.concatenate(
                [arrived[4 * dc + k][:, n : n + 512] for k in range(4)], axis=0
            )
            moved = mm(turn, table).astype(BF)
            for z in range(4):
                place = (z % 2) * 4 + from_core * 2 + z // 2
                start = pl.multiple_of(place * BLK, 16)
                scaled[pl.ds(start, BLK), n : n + 512] = moved[z * BLK : (z + 1) * BLK, :]
    tile = ROWS // 2
    lane = lax.broadcasted_iota(jnp.int32, (tile, 128), 1)
    expert = ((y * 2 + z_lo) * 2 + core) * 2 + z_hi
    for m in range(2):
        part = slice(m * tile, (m + 1) * tile)
        total = jnp.zeros((tile, F), F32)
        for half, w in ((z_hi, w_own), (1 - z_hi, w_oth)):
            for i in range(4):
                start = pl.multiple_of(half * 1024 + i * 256, 256)
                total = total + mm(scaled[part, pl.ds(start, 256)], w[i], 1, 1)
        d_both[part, :] = jnp.concatenate(
            [(total * slope[part, :]).astype(BF), (total * act[part, :]).astype(BF)], axis=1
        )
        q = jnp.sum(total * hidden[part, :].astype(F32), axis=1, keepdims=True)
        q_out[part, :] = jnp.where(lane == expert, q, 0.0).astype(BF)


def backward(sc, arrived, w_own, w_oth, hidden, act, slope):
    vmem = pl.BlockSpec(memory_space=pltpu.VMEM)
    return pl.pallas_call(
        backward_kernel,
        in_specs=[pl.BlockSpec(memory_space=pltpu.SMEM)] + [vmem] * 13,
        out_specs=[vmem] * 3,
        out_shape=[
            jax.ShapeDtypeStruct((ROWS, D), BF),
            jax.ShapeDtypeStruct((ROWS, 2 * F), BF),
            jax.ShapeDtypeStruct((ROWS, 128), BF),
        ],
        compiler_params=params(),
        cost_estimate=cost(2 * ROWS * (D * F + 448 * D), 20 * MIB),
    )(sc, *arrived, w_own, w_oth, hidden, act, slope)


def grads_kernel(sc, rows, scaled, d_both, hidden, gate_up, down):
    gate_up[...] = mm(rows[...], d_both[...], 0, 0).astype(BF)
    down[...] = mm(hidden[...], scaled[...], 0, 0).astype(BF)


def grads(sc, rows, scaled, d_both, hidden, own):
    def column(i, sc):
        half = sc[3] if own else 1 - sc[3]
        return (0, half * 4 + i)

    line = lambda i, sc: (i, 0)
    return pl.pallas_call(
        grads_kernel,
        grid_spec=pltpu.PrefetchScalarGridSpec(
            num_scalar_prefetch=1,
            grid=(4,),
            in_specs=[
                pl.BlockSpec((ROWS, 256), column),
                pl.BlockSpec((ROWS, 256), column),
                whole((ROWS, 2 * F)),
                whole((ROWS, F)),
            ],
            out_specs=[pl.BlockSpec((256, 2 * F), line), pl.BlockSpec((F, 256), line)],
        ),
        out_shape=[
            jax.ShapeDtypeStruct((1024, 2 * F), BF),
            jax.ShapeDtypeStruct((4 * F, 256), BF),
        ],
        compiler_params=params(),
        cost_estimate=cost(2 * ROWS * 1024 * 3 * F, 12 * MIB),
    )(sc, rows, scaled, d_both, hidden)


def inputs_kernel(sc, d_both, q, w_own, w_oth, out):
    z_hi = sc[3]
    own = pl.multiple_of(z_hi * 1024, 1024)
    oth = pl.multiple_of((1 - z_hi) * 1024, 1024)
    out[:, pl.ds(own, 1024)] = mm(d_both[...], w_own[...], 1, 1).astype(BF)
    out[:, pl.ds(oth, 1024)] = mm(d_both[...], w_oth[...], 1, 1).astype(BF)
    out[:, D:] = q[...]


def input_grads(sc, d_both, q, w_own, w_oth):
    tile = ROWS // 2
    line = lambda m, sc: (m, 0)
    return pl.pallas_call(
        inputs_kernel,
        grid_spec=pltpu.PrefetchScalarGridSpec(
            num_scalar_prefetch=1,
            grid=(2,),
            in_specs=[
                pl.BlockSpec((tile, 2 * F), line),
                pl.BlockSpec((tile, 128), line),
                whole((1024, 2 * F)),
                whole((1024, 2 * F)),
            ],
            out_specs=pl.BlockSpec((tile, WIDE), line),
        ),
        out_shape=jax.ShapeDtypeStruct((ROWS, WIDE), BF),
        compiler_params=params(),
        cost_estimate=cost(2 * ROWS * D * 2 * F, 16 * MIB),
    )(sc, d_both, q, w_own, w_oth)


def combine_kernel(sel, rows, *outs):
    for start in range(0, WIDE, 512):
        end = min(start + 512, WIDE)
        part = mm(sel[...], rows[:, start:end], 0, 0).astype(BF)
        for d in range(4):
            outs[d][:, start:end] = part[d * TOK : (d + 1) * TOK, :]


def combine(sel, rows):
    return pl.pallas_call(
        combine_kernel,
        out_shape=[jax.ShapeDtypeStruct((TOK, WIDE), BF)] * 4,
        compiler_params=params(),
        cost_estimate=cost(2 * ROWS * 512 * WIDE, 8 * MIB),
    )(sel, rows)


def final_kernel(a, b, c, d, routes, probs, out, out_probs):
    total = (a[...].astype(F32) + b[...].astype(F32)) + (
        c[...].astype(F32) + d[...].astype(F32)
    )
    out[...] = total[:, :D].astype(BF)
    table = total[:, D:]
    lane = lax.broadcasted_iota(jnp.int32, (TOK, 128), 1)
    chosen = routes[...]
    weight = probs[...].astype(BF).astype(F32)
    for k in range(TOP):
        value = jnp.sum(
            jnp.where(lane == chosen[:, k : k + 1], table, 0.0), axis=1, keepdims=True
        )
        out_probs[:, k : k + 1] = value / weight[:, k : k + 1]


def final(parts, routes, probs):
    return pl.pallas_call(
        final_kernel,
        out_shape=[
            jax.ShapeDtypeStruct((TOK, D), BF),
            jax.ShapeDtypeStruct((TOK, TOP), F32),
        ],
        compiler_params=params(16),
        cost_estimate=cost(0, 3 * MIB),
    )(*parts, routes, probs)


def z_index(z):
    return (z % 2) * 2 + z // 2


def along_y(k):
    return [(y, (y + k) % 4) for y in range(4)]


def along_z(k):
    return [(z_index(z), z_index((z + k) % 4)) for z in range(4)]


def along_yc(k, dc):
    return [(y * 2 + c, ((y + k) % 4) * 2 + (c ^ dc)) for y in range(4) for c in range(2)]


def body(tokens, cotangent, routes, probs, w_gate_up, w_down):
    names = ("y", "zl", "c", "zh", "x")
    sc = jnp.stack([lax.axis_index(n) for n in names]).astype(jnp.int32)
    z_hi = sc[3]
    tok, cot = add_meta(tokens, cotangent, routes, probs)
    toks, cots = [tok], [cot]
    for k in (1, 2, 3):
        toks.append(lax.ppermute(tok, "y", along_y(k)))
        cots.append(lax.ppermute(cot, ("zl", "zh"), along_z(k)))

    pick_half = lambda w, i: lax.dynamic_index_in_dim(w, i, 0, keepdims=False)
    swap = [(0, 1), (1, 0)]
    own_gu, own_dn = pick_half(w_gate_up, z_hi), pick_half(w_down, z_hi)
    oth_gu = lax.ppermute(pick_half(w_gate_up, 1 - z_hi), "zh", swap)
    oth_dn = lax.ppermute(pick_half(w_down, 1 - z_hi), "zh", swap)
    gather = lambda w, t: lax.all_gather(w, "x", axis=0, tiled=t)
    gu_own, gu_oth = gather(own_gu, True), gather(oth_gu, True)
    dn_own, dn_oth = gather(own_dn, False), gather(oth_dn, False)

    x_send, sel = pick(pick_tokens_kernel, sc, toks, False)
    x_rows = lax.all_to_all(
        x_send.reshape(8, BLK, D), ("zl", "c", "zh"), split_axis=0, concat_axis=0, tiled=True
    ).reshape(ROWS, D)
    sent = pick(pick_cotan_kernel, sc, cots, True)
    arrived = [
        sent[j] if j == 0 else lax.ppermute(sent[j], ("y", "c"), along_yc(j % 4, j // 4))
        for j in range(8)
    ]
    hidden, act, slope = forward(sc, x_rows, gu_own, gu_oth)
    scaled, d_both, q = backward(sc, arrived, dn_own, dn_oth, hidden, act, slope)

    scatter = lambda g: lax.psum_scatter(g, "x", scatter_dimension=0, tiled=True)
    oth_part = grads(sc, x_rows, scaled, d_both, hidden, False)
    own_part = grads(sc, x_rows, scaled, d_both, hidden, True)
    oth_sum = [lax.ppermute(scatter(g), "zh", swap) for g in oth_part]
    own_sum = [scatter(g) for g in own_part]
    grad_gu, grad_dn = [
        jnp.where(z_hi == 0, jnp.stack([a, b]), jnp.stack([b, a]))
        for a, b in zip(own_sum, oth_sum)
    ]

    dx = input_grads(sc, d_both, q, gu_own, gu_oth)
    back = lax.all_to_all(
        dx.reshape(8, BLK, WIDE), ("zl", "c", "zh"), split_axis=0, concat_axis=0, tiled=True
    ).reshape(ROWS, WIDE)
    parts = combine(sel, back)
    parts = [parts[0]] + [lax.ppermute(parts[k], "y", along_y(-k)) for k in (1, 2, 3)]
    d_tokens, d_probs = final(parts, routes, probs)
    return d_tokens, d_probs, grad_gu, grad_dn


def solution(mesh):
    fine = Mesh(mesh.devices.reshape(4, 2, 2, 2, 4), ("y", "zl", "c", "zh", "x"))
    exp, fsdp = ("y", "zl", "c"), ("zh", "x")
    row = P(exp + fsdp, None)
    gate_up, down = P(exp, fsdp, None), P(exp, None, fsdp)
    return jax.shard_map(
        body,
        mesh=fine,
        in_specs=(row, row, row, row, gate_up, down),
        out_specs=(row, row, gate_up, down),
        check_vma=False,
    )
```

time: 629 us -> 369 us (0.59); the launches traced: 621 us -> 369 us
  waiting for transfers between devices: 385 us -> 220 us
  local copies, waits for them, and re-layouts: 108 us -> 20.6 us
  Pallas kernels: 0 us -> 69.9 us
  matrix products: 60.6 us -> 0 us
  other arithmetic: 22.3 us -> 5.79 us
  starting transfers between devices: 30.7 us -> 38 us
    ppermute x0 -> x20, waiting for transfers between devices: none -> 157 us  [the longest x1 48.1 us: body(): oth_dn = lax.ppermute(pick_half(w_down, 1 - z_hi), 'zh', swap)]
    all_gather x2 -> x4, waiting for transfers between devices: 127 us -> 0.03 us  [body(): gather = lambda w, t: lax.all_gather(w, 'x', axis=0, tiled=t)]
    reduce_scatter x2 -> x4, waiting for transfers between devices: 127 us -> 23.7 us  [body(): lax.psum_scatter(g, 'x', scatter_dimension=0, tiled=True)]
    all_to_all x5 -> x2, waiting for transfers between devices: 130 us -> 37.7 us  [the longest x1 37.7 us: body(): lax.all_to_all(dx.reshape(8, BLK, WIDE), ('zl', 'c', 'zh'), split_axis=0,...]
    pallas_call x0 -> x10, Pallas kernels: none -> 69.9 us  [the longest x2 16.3 us: grads(): pl.pallas_call(grads_kernel, grid_spec=pltpu.PrefetchScalarGridSpec(num_s...]
    dot_general x12 -> x0, matrix products: 60.6 us -> none  [the longest x2 13 us: expert_rows(): lax.dot_general(rows_in, d_both, (((0,), (0,)), ((), ())), preferred_elem...]
    gather x8 -> x0, local copies, waits for them, and re-layouts: 46.6 us -> none  [the longest x2 15.9 us: body(): dx_rows = dx_back.reshape(experts * capacity, model_width)[target]]
    ppermute x0 -> x20, starting transfers between devices: none -> 26.4 us  [the longest x7 6.24 us: body(): lax.ppermute(sent[j], ('y', 'c'), along_yc(j % 4, j // 4))]
  transfers between devices with their start and end apart: 9 -> 30, of which waited for: 6 -> 16; matrix products, arithmetic and copies ran while one was open for 27% -> 1% of each run, Pallas kernels for 0% -> 13%
where the time goes in v1:
time: 369 us
  waiting for transfers between devices  220 us (60%)
  Pallas kernels  69.9 us (19%)
  starting transfers between devices  38 us (10%)
  local copies, waits for them, and re-layouts  20.6 us (6%)
  between operations  14.3 us (4%)
  other arithmetic  5.79 us (2%)
    ppermute x1, waiting for transfers between devices, body(): oth_dn = lax.ppermute(pick_half(w_down, 1 - z_hi), 'zh', swap)  48.1 us
    all_to_all x1, waiting for transfers between devices, body(): lax.all_to_all(dx.reshape(8, BLK, WIDE), ('zl', 'c', 'zh'), split_axis=0,...  37.7 us
    ppermute x3, waiting for transfers between devices, body(): cots.append(lax.ppermute(cot, ('zl', 'zh'), along_z(k)))  26.8 us
    ppermute x3, waiting for transfers between devices, body(): toks.append(lax.ppermute(tok, 'y', along_y(k)))  24.9 us
    reduce_scatter x4, waiting for transfers between devices, body(): lax.psum_scatter(g, 'x', scatter_dimension=0, tiled=True)  23.7 us
    ppermute x7, waiting for transfers between devices, body(): lax.ppermute(sent[j], ('y', 'c'), along_yc(j % 4, j // 4))  22.1 us
    unnamed x41, local copies, waits for them, and re-layouts  16.4 us
    pallas_call x2, Pallas kernels, grads(): pl.pallas_call(grads_kernel, grid_spec=pltpu.PrefetchScalarGridSpec(num_s...  16.3 us
  transfers between devices with their start and end apart: 30, of which 16 were waited for; matrix products, arithmetic and copies ran while one was open for 1% of the time, Pallas kernels for 13%

profile of v1, /device:TPU:1, one launch (start us, length us, event | category | flops | bytes accessed | tf_op | source)
XLA Modules:
  0.0 368.6 jit_solution(18111964935955699314)
XLA Ops:
  7.2 2.3 dynamic-slice_bitcast_fusion
  9.6 4.5 %collective-permute-start.14 = (bf16[256,1408]{1,0:T(8,128)(2,1)S(1)}, bf16[256,1408]{1,0:T(8,128)(2,1)S(1)}, u32[]{:S(2)}, u32[]{:S(2)}) collective-permute-start(bf16[256,1408]{1,0:T(8,128)(2,1)S(1)} %get-tuple-element.68), channel_id=1, source_target_pairs={{0,4},{4,0},{1,5},{5,1},{2,6},{6,2},{3,7},{7,3},{8,12},{12,8},{9,1... | collective-permute-start | bytes 2162696 | tf_op jit(solution)/shard_map/ppermute | solution.py:397
  14.1 15.9 %collective-permute-done.14 = bf16[256,1408]{1,0:T(8,128)(2,1)S(1)} collective-permute-done((bf16[256,1408]{1,0:T(8,128)(2,1)S(1)}, bf16[256,1408]{1,0:T(8,128)(2,1)S(1)}, u32[]{:S(2)}, u32[]{:S(2)}) %collective-permute-start.14) | collective-permute-done | bytes 720928 | tf_op jit(solution)/shard_map/ppermute | solution.py:397
  30.0 0.9 copy-done.15
  31.4 2.8 collective-permute-start.2
  34.2 0.3 collective-permute-start.1
  34.5 0.7 collective-permute-start
  35.2 1.9 dynamic-slice_bitcast_fusion.1
  37.2 8.7 %collective-permute-done.2.t3.m3 = bf16[128,2176]{1,0:T(8,128)(2,1)S(1)} collective-permute-done((bf16[128,2176]{1,0:T(8,128)(2,1)S(1)}, bf16[128,2176]{1,0:T(8,128)(2,1)S(1)}, u32[]{:S(2)}, u32[]{:S(2)}) %collective-permute-start.2) | collective-permute-done | bytes 557088 | tf_op jit(solution)/shard_map/ppermute | solution.py:391
  45.9 2.5 collective-permute-done.1.t2.m2
  48.4 13.8 %collective-permute-done.t1.m1 = bf16[128,2176]{1,0:T(8,128)(2,1)S(1)} collective-permute-done((bf16[128,2176]{1,0:T(8,128)(2,1)S(1)}, bf16[128,2176]{1,0:T(8,128)(2,1)S(1)}, u32[]{:S(2)}, u32[]{:S(2)}) %collective-permute-start) | collective-permute-done | bytes 557088 | tf_op jit(solution)/shard_map/ppermute | solution.py:391
  62.1 5.4 %shard_map.94 = (bf16[896,2048]{1,0:T(8,128)(2,1)}, bf16[896,512]{1,0:T(8,128)(2,1)S(1)}) custom-call(s32[5]{0:T(128)S(1)} %stack.51.sc, bf16[128,2176]{1,0:T(8,128)(2,1)S(1)} %get-tuple-element.32.t0.m0, bf16[128,2176]{1,0:T(8,128)(2,1)S(1)} %collective-permute-done.t1.m1, bf16[128,2176]{1,0:T(8,128)(2,1)S(1)} %collective-permute-done.1.t2.m2, ...), custom_call_target="tpu_custom_call" | custom-call | flops 1879048192 | bytes 6291456 | tf_op jit(solution)/shard_map/pallas_call | solution.py:142
  67.5 0.9 copy-done.11
  68.4 4.9 %all-to-all-start = ((bf16[8,112,2048]{2,1,0:T(8,128)(2,1)}), bf16[8,112,2048]{2,1,0:T(8,128)(2,1)}, u32[]{:S(2)}, u32[]{:S(2)}) async-start(bf16[8,112,2048]{2,1,0:T(8,128)(2,1)} %bitcast.22), calls=%async_computation | async-start | bytes 7340032 | tf_op jit(solution)/shard_map/all_to_all | solution.py:404
  73.3 2.9 collective-permute-start.13
  76.2 48.1 %collective-permute-done.13 = bf16[704,256]{1,0:T(8,128)(2,1)S(1)} collective-permute-done((bf16[704,256]{1,0:T(8,128)(2,1)S(1)}, bf16[704,256]{1,0:T(8,128)(2,1)S(1)}, u32[]{:S(2)}, u32[]{:S(2)}) %collective-permute-start.13) | collective-permute-done | bytes 360480 | tf_op jit(solution)/shard_map/ppermute | solution.py:398
  124.3 0.7 copy-done.16
  125.1 1.0 collective-permute-start.5
  126.1 1.2 collective-permute-start.4
  127.3 11.3 %collective-permute-done.5.t3.m3 = bf16[128,2176]{1,0:T(8,128)(2,1)S(1)} collective-permute-done((bf16[128,2176]{1,0:T(8,128)(2,1)S(1)}, bf16[128,2176]{1,0:T(8,128)(2,1)S(1)}, u32[]{:S(2)}, u32[]{:S(2)}) %collective-permute-start.5) | collective-permute-done | bytes 557088 | tf_op jit(solution)/shard_map/ppermute | solution.py:392
  138.6 2.0 collective-permute-done.4.t2.m2
  140.6 13.5 %collective-permute-done.3.t1.m1 = bf16[128,2176]{1,0:T(8,128)(2,1)S(1)} collective-permute-done((bf16[128,2176]{1,0:T(8,128)(2,1)S(1)}, bf16[128,2176]{1,0:T(8,128)(2,1)S(1)}, u32[]{:S(2)}, u32[]{:S(2)}) %collective-permute-start.3) | collective-permute-done | bytes 557088 | tf_op jit(solution)/shard_map/ppermute | solution.py:392
  154.1 5.3 %shard_map.95 = (bf16[112,2048]{1,0:T(8,128)(2,1)S(1)}, bf16[112,2048]{1,0:T(8,128)(2,1)S(1)}, bf16[112,2048]{1,0:T(8,128)(2,1)S(1)}, bf16[112,2048]{1,0:T(8,128...) custom-call(s32[5]{0:T(128)S(1)} %stack.51.sc, ...), custom_call_target="tpu_custom_call" | custom-call | flops 1879048192 | bytes 6291456 | tf_op jit(solution)/shard_map/pallas_call | solution.py:142
  159.4 0.8 copy-done.13
  160.2 1.5 collective-permute-start.7
  161.7 1.2 collective-permute-start.8
  162.8 1.1 collective-permute-start.9
  163.9 0.5 collective-permute-start.10
  164.4 17.7 %collective-permute-done.6.refs_1_ = bf16[112,2048]{1,0:T(8,128)(2,1)S(1)} collective-permute-done((bf16[112,2048]{1,0:T(8,128)(2,1)S(1)}, bf16[112,2048]{1,0:T(8,128)(2,1)S(1)}, u32[]{:S(2)}, u32[]{:S(2)}) %collective-permute-start.6) | collective-permute-done | bytes 458784 | tf_op jit(solution)/shard_map/ppermute | solution.py:409
  182.0 2.0 collective-permute-start.12
  184.1 12.0 %shard_map.96 = (bf16[896,704]{1,0:T(8,128)(2,1)S(1)}, f32[896,704]{1,0:T(8,128)S(1)}, f32[896,704]{1,0:T(8,128)}) custom-call(s32[5]{0:T(128)S(1)} %stack.51.sc, bf16[896,2048]{1,0:T(8,128)(2,1)} %bitcast.8.rows, bf16[1024,1408]{1,0:T(8,128)(2,1)} %bitcast.19, bf16[1024,1408]{1,0:T(8,128)(2,1)} %all-gather.9.cloned.1.call-done.w_oth), custom_call_target="tpu_custom_call" | custom-call | flops 5167382528 | bytes 16777216 | tf_op jit(solution)/shard_map/pallas_call | solution.py:176
  196.1 1.5 copy-done.3
  197.6 1.1 copy-done.7
  198.7 4.4 %collective-permute-done.10.refs_5_ = bf16[112,2048]{1,0:T(8,128)(2,1)S(1)} collective-permute-done((bf16[112,2048]{1,0:T(8,128)(2,1)}, bf16[112,2048]{1,0:T(8,128)(2,1)S(1)}, u32[]{:S(2)}, u32[]{:S(2)}) %collective-permute-start.10) | collective-permute-done | bytes 458784 | tf_op jit(solution)/shard_map/ppermute | solution.py:409
  203.2 1.3 copy-done.8
  204.5 1.0 copy-done.14
  205.5 13.6 %shard_map.97 = (bf16[896,2048]{1,0:T(8,128)(2,1)}, bf16[896,1408]{1,0:T(8,128)(2,1)}, bf16[896,128]{1,0:T(8,128)(2,1)S(1)}) custom-call(s32[5]{0:T(128)S(1)} %stack.51.sc, bf16[112,2048]{1,0:T(8,128)(2,1)S(1)} %copy-done.14, bf16[112,2048]{1,0:T(8,128)(2,1)S(1)} %collective-permute-done.6.refs_1_, bf16[112,2048]{1,0:T(8,128)(2,1)S(1)} %collective-permute-done.7.refs_2_, ...), custom_call_target="tpu_custom_call" | custom-call | flops 4227858432 | bytes 20971520 | tf_op jit(solution)/shard_map/pallas_call | solution.py:245
  219.1 1.7 copy-done.4
  220.9 8.1 %shard_map.102 = (bf16[1024,1408]{1,0:T(8,128)(2,1)}, bf16[2816,256]{1,0:T(8,128)(2,1)}) custom-call(s32[5]{0:T(128)S(1)} %stack.51.sc, bf16[896,2048]{1,0:T(8,128)(2,1)} %bitcast.8.rows, bf16[896,2048]{1,0:T(8,128)(2,1)} %get-tuple-element.55.scaled, bf16[896,1408]{1,0:T(8,128)(2,1)S(1)} %copy-done.4, bf16[896,704]{1,0:T(8,128)(2,1)S(1)} %copy-done.9), custom_call_target="tpu_custom_call" | custom-call | flops 3875536896 | bytes 12582912 | tf_op jit(solution)/shard_map/pallas_call | solution.py:270
  229.1 0.5 reduce-scatter.11.cloned.1.call-update
  229.6 1.1 copy-done.5
  230.7 1.3 copy-done.10
  232.0 8.1 %shard_map.101 = (bf16[1024,1408]{1,0:T(8,128)(2,1)}, bf16[2816,256]{1,0:T(8,128)(2,1)}) custom-call(s32[5]{0:T(128)S(1)} %stack.51.sc, bf16[896,2048]{1,0:T(8,128)(2,1)} %bitcast.8.rows, bf16[896,2048]{1,0:T(8,128)(2,1)} %get-tuple-element.55.scaled, bf16[896,1408]{1,0:T(8,128)(2,1)S(1)} %copy-done.5, bf16[896,704]{1,0:T(8,128)(2,1)S(1)} %copy-done.10), custom_call_target="tpu_custom_call" | custom-call | flops 3875536896 | bytes 12582912 | tf_op jit(solution)/shard_map/pallas_call | solution.py:270
  240.2 0.3 reduce-scatter.5.cloned.1.call-start
  240.5 0.5 reduce-scatter.5.cloned.1.call-update
  240.9 1.3 copy-done.2
  242.3 1.7 copy-done.6
  244.0 9.9 %shard_map.98 = bf16[896,2176]{1,0:T(8,128)(2,1)} custom-call(s32[5]{0:T(128)S(1)} %stack.51.sc, bf16[896,1408]{1,0:T(8,128)(2,1)S(1)} %copy-done.6, bf16[896,128]{1,0:T(8,128)(2,1)S(1)} %get-tuple-element.48.q, bf16[1024,1408]{1,0:T(8,128)(2,1)S(1)} %bitcast.20, bf16[1024,1408]{1,0:T(8,128)(2,1)} %all-gather.9.cloned.1.call-done.w_oth), custom_call_target="tpu_custom_call" | custom-call | flops 5167382528 | bytes 16777216 | tf_op jit(solution)/shard_map/pallas_call | solution.py:304
  253.9 6.1 %all-to-all-start.1 = ((bf16[8,112,2176]{2,1,0:T(8,128)(2,1)}), bf16[8,112,2176]{2,1,0:T(8,128)(2,1)}, u32[]{:S(2)}, u32[]{:S(2)}) async-start(bf16[8,112,2176]{2,1,0:T(8,128)(2,1)} %bitcast.21), calls=%async_computation.1 | async-start | bytes 7798784 | tf_op jit(solution)/shard_map/all_to_all | solution.py:426
  260.0 5.2 %reduce-scatter.7.cloned.1.call-done = bf16[256,1408]{1,0:T(8,128)(2,1)} async-done(((bf16[1024,1408]{1,0:T(8,128)(2,1)}), bf16[256,1408]{1,0:T(8,128)(2,1)}) %reduce-scatter.7.cloned.1.call-update) | async-done | bytes 720912 | tf_op jit(solution)/shard_map/reduce_scatter | solution.py:415
  265.2 2.9 collective-permute-start.18
  268.1 37.7 %all-to-all-done.1 = bf16[8,112,2176]{2,1,0:T(8,128)(2,1)} async-done(((bf16[8,112,2176]{2,1,0:T(8,128)(2,1)}), bf16[8,112,2176]{2,1,0:T(8,128)(2,1)}, u32[]{:S(2)}, u32[]{:S(2)}) %all-to-all-start.1) | async-done | bytes 3899424 | tf_op jit(solution)/shard_map/all_to_all | solution.py:426
  305.8 5.5 %shard_map.99 = (bf16[128,2176]{1,0:T(8,128)(2,1)S(1)}, bf16[128,2176]{1,0:T(8,128)(2,1)}, bf16[128,2176]{1,0:T(8,128)(2,1)S(1)}, bf16[128,2176]{1,0:T(8,128)(2,1)S(1)}) custom-call(bf16[896,512]{1,0:T(8,128)(2,1)S(1)} %copy-done.12, bf16[896,2176]{1,0:T(8,128)(2,1)} %bitcast.12.rows), custom_call_target="tpu_custom_call" | custom-call | flops 1996488704 | bytes 8388608 | tf_op jit(solution)/shard_map/pallas_call | solution.py:332
  311.3 2.2 collective-permute-start.15
  313.5 0.6 collective-permute-start.17
  314.1 1.1 collective-permute-start.19
  315.2 3.7 %reduce-scatter.9.cloned.1.call-done = bf16[704,256]{1,0:T(8,128)(2,1)} async-done(((bf16[2816,256]{1,0:T(8,128)(2,1)}), bf16[704,256]{1,0:T(8,128)(2,1)}) %reduce-scatter.9.cloned.1.call-update) | async-done | bytes 360464 | tf_op jit(solution)/shard_map/reduce_scatter | solution.py:415
  318.9 10.1 %collective-permute-done.19 = bf16[704,256]{1,0:T(8,128)(2,1)} collective-permute-done((bf16[704,256]{1,0:T(8,128)(2,1)}, bf16[704,256]{1,0:T(8,128)(2,1)}, u32[]{:S(2)}, u32[]{:S(2)}) %collective-permute-start.19) | collective-permute-done | bytes 360480 | tf_op jit(solution)/shard_map/ppermute | solution.py:418
  329.0 2.4 maximum_select_fusion.1
  331.5 9.5 %collective-permute-done.17.d = bf16[128,2176]{1,0:T(8,128)(2,1)S(1)} collective-permute-done((bf16[128,2176]{1,0:T(8,128)(2,1)S(1)}, bf16[128,2176]{1,0:T(8,128)(2,1)S(1)}, u32[]{:S(2)}, u32[]{:S(2)}) %collective-permute-start.17) | collective-permute-done | bytes 557088 | tf_op jit(solution)/shard_map/ppermute | solution.py:430
  341.0 1.9 shard_map.100
  342.9 0.7 copy.19
  343.6 14.8 %reduce-scatter.5.cloned.1.call-done = bf16[256,1408]{1,0:T(8,128)(2,1)} async-done(((bf16[1024,1408]{1,0:T(8,128)(2,1)}), bf16[256,1408]{1,0:T(8,128)(2,1)}) %reduce-scatter.5.cloned.1.call-update) | async-done | bytes 720912 | tf_op jit(solution)/shard_map/reduce_scatter | solution.py:415
  358.4 3.4 maximum_select_fusion
  (60 shorter events, 1.0 us)
Async XLA Ops:
  7.2 176.9 %all-gather.13.cloned.1.call-start = ((), (), s32[]{:S(2)}) async-start(), calls=%async_computation.13 | async-start | bytes 3604480 | tf_op jit(solution)/shard_map/all_gather | solution.py:399
  9.5 21.4 %copy-start.17 = (s32[128,6]{0,1:T(8,128)S(1)}, s32[128,6]{0,1:T(8,128)}, u32[]{:S(2)}) copy-start(s32[128,6]{0,1:T(8,128)} %param.8) | copy-start | bytes 9220
  9.5 21.5 %copy-start.18 = (f32[128,6]{0,1:T(8,128)S(1)}, f32[128,6]{0,1:T(8,128)}, u32[]{:S(2)}) copy-start(f32[128,6]{0,1:T(8,128)} %param.9) | copy-start | bytes 9220
  9.5 21.6 %copy-start = (bf16[128,2048]{1,0:T(8,128)(2,1)S(1)}, bf16[128,2048]{1,0:T(8,128)(2,1)}, u32[]{:S(2)}) copy-start(bf16[128,2048]{1,0:T(8,128)(2,1)} %tok.1) | copy-start | bytes 1572868
  9.5 21.6 %copy-start.1 = (bf16[128,2048]{1,0:T(8,128)(2,1)S(1)}, bf16[128,2048]{1,0:T(8,128)(2,1)}, u32[]{:S(2)}) copy-start(bf16[128,2048]{1,0:T(8,128)(2,1)} %cot.1) | copy-start | bytes 1572868
  9.6 174.5 %all-gather.9.cloned.1.call-start = ((), (), s32[]{:S(2)}) async-start(), calls=%async_computation.7 | async-start | bytes 3604480 | tf_op jit(solution)/shard_map/all_gather | solution.py:399
  9.6 20.4 %collective-permute-start.14 = (bf16[256,1408]{1,0:T(8,128)(2,1)S(1)}, bf16[256,1408]{1,0:T(8,128)(2,1)S(1)}, u32[]{:S(2)}, u32[]{:S(2)}) collective-permute-start(bf16[256,1408]{1,0:T(8,128)(2,1)S(1)} %get-tuple-element.68), channel_id=1, source_target_pairs={{0,4},{4,0},{1,5},{5,1},{2,6},{6,2},{3,7},{7,3},{8,12},{12,8},{9,1... | collective-permute-start | bytes 2162696 | tf_op jit(solution)/shard_map/ppermute | solution.py:397
  30.0 0.9 copy-start.15
  30.9 172.3 %all-gather.7.cloned.1.call-start = ((), (), s32[]{:S(2)}) async-start(), calls=%async_computation.6 | async-start | bytes 1802240 | tf_op jit(solution)/shard_map/all_gather | solution.py:399
  31.4 14.5 %collective-permute-start.2 = (bf16[128,2176]{1,0:T(8,128)(2,1)S(1)}, bf16[128,2176]{1,0:T(8,128)(2,1)S(1)}, u32[]{:S(2)}, u32[]{:S(2)}) collective-permute-start(bf16[128,2176]{1,0:T(8,128)(2,1)S(1)} %get-tuple-element.32.t0.m0), channel_id=1, source_target_pairs={{0,96},{32,0},{64,32},{96,64},{1,97},{33,1},{65,33},{97,65},{2,98}... | collective-permute-start | bytes 1671176 | tf_op jit(solution)/shard_map/ppermute | solution.py:391
  34.2 14.2 %collective-permute-start.1 = (bf16[128,2176]{1,0:T(8,128)(2,1)S(1)}, bf16[128,2176]{1,0:T(8,128)(2,1)S(1)}, u32[]{:S(2)}, u32[]{:S(2)}) collective-permute-start(bf16[128,2176]{1,0:T(8,128)(2,1)S(1)} %get-tuple-element.32.t0.m0), channel_id=1, source_target_pairs={{0,64},{32,96},{64,0},{96,32},{1,65},{33,97},{65,1},{97,33},{2,66}... | collective-permute-start | bytes 1671176 | tf_op jit(solution)/shard_map/ppermute | solution.py:391
  34.5 27.6 %collective-permute-start = (bf16[128,2176]{1,0:T(8,128)(2,1)S(1)}, bf16[128,2176]{1,0:T(8,128)(2,1)S(1)}, u32[]{:S(2)}, u32[]{:S(2)}) collective-permute-start(bf16[128,2176]{1,0:T(8,128)(2,1)S(1)} %get-tuple-element.32.t0.m0), channel_id=1, source_target_pairs={{0,32},{32,64},{64,96},{96,0},{1,33},{33,65},{65,97},{97,1},{2,34}... | collective-permute-start | bytes 1671176 | tf_op jit(solution)/shard_map/ppermute | solution.py:391
  67.5 0.9 copy-start.11
  68.4 115.6 %all-to-all-start = ((bf16[8,112,2048]{2,1,0:T(8,128)(2,1)}), bf16[8,112,2048]{2,1,0:T(8,128)(2,1)}, u32[]{:S(2)}, u32[]{:S(2)}) async-start(bf16[8,112,2048]{2,1,0:T(8,128)(2,1)} %bitcast.22), calls=%async_computation | async-start | bytes 7340032 | tf_op jit(solution)/shard_map/all_to_all | solution.py:404
  73.3 129.8 %all-gather.11.cloned.1.call-start = ((), (), s32[]{:S(2)}) async-start(), calls=%async_computation.12 | async-start | bytes 1802240 | tf_op jit(solution)/shard_map/all_gather | solution.py:399
  73.3 51.0 %collective-permute-start.13 = (bf16[704,256]{1,0:T(8,128)(2,1)S(1)}, bf16[704,256]{1,0:T(8,128)(2,1)S(1)}, u32[]{:S(2)}, u32[]{:S(2)}) collective-permute-start(bf16[704,256]{1,0:T(8,128)(2,1)S(1)} %get-tuple-element.70), channel_id=1, source_target_pairs={{0,4},{4,0},{1,5},{5,1},{2,6},{6,2},{3,7},{7,3},{8,12},{12,8},{9,1... | collective-permute-start | bytes 1081352 | tf_op jit(solution)/shard_map/ppermute | solution.py:398
  124.3 0.7 copy-start.16
  125.1 140.1 %reduce-scatter.7.cloned.1.call-start = ((), (), s32[]{:S(2)}) async-start(), calls=%async_computation.9 | async-start | bytes 3604480 | tf_op jit(solution)/shard_map/reduce_scatter | solution.py:415
  125.1 13.4 %collective-permute-start.5 = (bf16[128,2176]{1,0:T(8,128)(2,1)S(1)}, bf16[128,2176]{1,0:T(8,128)(2,1)S(1)}, u32[]{:S(2)}, u32[]{:S(2)}) collective-permute-start(bf16[128,2176]{1,0:T(8,128)(2,1)S(1)} %get-tuple-element.34.t0.m0), channel_id=1, source_target_pairs={{0,20},{16,0},{4,16},{20,4},{1,21},{17,1},{5,17},{21,5},{2,22},{18... | collective-permute-start | bytes 1671176 | tf_op jit(solution)/shard_map/ppermute | solution.py:392
  126.1 14.5 %collective-permute-start.4 = (bf16[128,2176]{1,0:T(8,128)(2,1)S(1)}, bf16[128,2176]{1,0:T(8,128)(2,1)S(1)}, u32[]{:S(2)}, u32[]{:S(2)}) collective-permute-start(bf16[128,2176]{1,0:T(8,128)(2,1)S(1)} %get-tuple-element.34.t0.m0), channel_id=1, source_target_pairs={{0,4},{16,20},{4,0},{20,16},{1,5},{17,21},{5,1},{21,17},{2,6},{18,... | collective-permute-start | bytes 1671176 | tf_op jit(solution)/shard_map/ppermute | solution.py:392
  127.3 26.8 %collective-permute-start.3 = (bf16[128,2176]{1,0:T(8,128)(2,1)S(1)}, bf16[128,2176]{1,0:T(8,128)(2,1)S(1)}, u32[]{:S(2)}, u32[]{:S(2)}) collective-permute-start(bf16[128,2176]{1,0:T(8,128)(2,1)S(1)} %get-tuple-element.34.t0.m0), channel_id=1, source_target_pairs={{0,16},{16,4},{4,20},{20,0},{1,17},{17,5},{5,21},{21,1},{2,18},{18... | collective-permute-start | bytes 1671176 | tf_op jit(solution)/shard_map/ppermute | solution.py:392
  159.4 0.8 copy-start.13
  160.2 21.9 %collective-permute-start.6 = (bf16[112,2048]{1,0:T(8,128)(2,1)S(1)}, bf16[112,2048]{1,0:T(8,128)(2,1)S(1)}, u32[]{:S(2)}, u32[]{:S(2)}) collective-permute-start(bf16[112,2048]{1,0:T(8,128)(2,1)S(1)} %get-tuple-element.36), channel_id=1, source_target_pairs={{0,32},{8,40},{32,64},{40,72},{64,96},{72,104},{96,0},{104,8},{1,3... | collective-permute-start | bytes 1376264 | tf_op jit(solution)/shard_map/ppermute | solution.py:409
  160.2 21.9 %collective-permute-start.7 = (bf16[112,2048]{1,0:T(8,128)(2,1)S(1)}, bf16[112,2048]{1,0:T(8,128)(2,1)S(1)}, u32[]{:S(2)}, u32[]{:S(2)}) collective-permute-start(bf16[112,2048]{1,0:T(8,128)(2,1)S(1)} %get-tuple-element.37), channel_id=1, source_target_pairs={{0,64},{8,72},{32,96},{40,104},{64,0},{72,8},{96,32},{104,40},{1,6... | collective-permute-start | bytes 1376264 | tf_op jit(solution)/shard_map/ppermute | solution.py:409
  161.7 37.0 %collective-permute-start.8 = (bf16[112,2048]{1,0:T(8,128)(2,1)}, bf16[112,2048]{1,0:T(8,128)(2,1)S(1)}, u32[]{:S(2)}, u32[]{:S(2)}) collective-permute-start(bf16[112,2048]{1,0:T(8,128)(2,1)} %get-tuple-element.38), channel_id=1, source_target_pairs={{0,96},{8,104},{32,0},{40,8},{64,32},{72,40},{96,64},{104,72},{1,9... | collective-permute-start | bytes 1376264 | tf_op jit(solution)/shard_map/ppermute | solution.py:409
  162.8 35.9 %collective-permute-start.9 = (bf16[112,2048]{1,0:T(8,128)(2,1)}, bf16[112,2048]{1,0:T(8,128)(2,1)S(1)}, u32[]{:S(2)}, u32[]{:S(2)}) collective-permute-start(bf16[112,2048]{1,0:T(8,128)(2,1)} %get-tuple-element.39), channel_id=1, source_target_pairs={{0,8},{8,0},{32,40},{40,32},{64,72},{72,64},{96,104},{104,96},{1,9... | collective-permute-start | bytes 1376264 | tf_op jit(solution)/shard_map/ppermute | solution.py:409
  163.9 39.2 %collective-permute-start.10 = (bf16[112,2048]{1,0:T(8,128)(2,1)}, bf16[112,2048]{1,0:T(8,128)(2,1)S(1)}, u32[]{:S(2)}, u32[]{:S(2)}) collective-permute-start(bf16[112,2048]{1,0:T(8,128)(2,1)} %get-tuple-element.40), channel_id=1, source_target_pairs={{0,40},{8,32},{32,72},{40,64},{64,104},{72,96},{96,8},{104,0},{1,4... | collective-permute-start | bytes 1376264 | tf_op jit(solution)/shard_map/ppermute | solution.py:409
  182.0 21.1 %collective-permute-start.11 = (bf16[112,2048]{1,0:T(8,128)(2,1)S(1)}, bf16[112,2048]{1,0:T(8,128)(2,1)}, u32[]{:S(2)}, u32[]{:S(2)}) collective-permute-start(bf16[112,2048]{1,0:T(8,128)(2,1)S(1)} %get-tuple-element.41), channel_id=1, source_target_pairs={{0,72},{8,64},{32,104},{40,96},{64,8},{72,0},{96,40},{104,32},{1,7... | collective-permute-start | bytes 1376264 | tf_op jit(solution)/shard_map/ppermute | solution.py:409
  182.0 21.1 %collective-permute-start.12 = (bf16[112,2048]{1,0:T(8,128)(2,1)S(1)}, bf16[112,2048]{1,0:T(8,128)(2,1)}, u32[]{:S(2)}, u32[]{:S(2)}) collective-permute-start(bf16[112,2048]{1,0:T(8,128)(2,1)S(1)} %get-tuple-element.42), channel_id=1, source_target_pairs={{0,104},{8,96},{32,8},{40,0},{64,40},{72,32},{96,72},{104,64},{1,1... | collective-permute-start | bytes 1376264 | tf_op jit(solution)/shard_map/ppermute | solution.py:409
  196.1 1.5 copy-start.3
  197.6 1.1 copy-start.7
  203.2 1.3 copy-start.8
  204.5 1.0 copy-start.14
  205.5 13.6 %copy-start.9 = (bf16[896,704]{1,0:T(8,128)(2,1)S(1)}, bf16[896,704]{1,0:T(8,128)(2,1)}, u32[]{:S(2)}) copy-start(bf16[896,704]{1,0:T(8,128)(2,1)} %copy-done.7) | copy-start | bytes 3784708
  219.1 1.7 copy-start.4
  229.0 1.7 copy-start.5
  229.0 85.1 %reduce-scatter.11.cloned.1.call-start = ((), (), s32[]{:S(2)}) async-start(), calls=%async_computation.11 | async-start | bytes 1802240 | tf_op jit(solution)/shard_map/reduce_scatter | solution.py:415
  229.6 89.3 %reduce-scatter.9.cloned.1.call-start = ((), (), s32[]{:S(2)}) async-start(), calls=%async_computation.10 | async-start | bytes 1802240 | tf_op jit(solution)/shard_map/reduce_scatter | solution.py:415
  230.7 1.3 copy-start.10
  240.2 118.2 %reduce-scatter.5.cloned.1.call-start = ((), (), s32[]{:S(2)}) async-start(), calls=%async_computation.8 | async-start | bytes 3604480 | tf_op jit(solution)/shard_map/reduce_scatter | solution.py:415
  240.5 1.8 copy-start.2
  242.3 1.7 copy-start.6
  253.9 51.9 %copy-start.12 = (bf16[896,512]{1,0:T(8,128)(2,1)S(1)}, bf16[896,512]{1,0:T(8,128)(2,1)}, u32[]{:S(2)}) copy-start(bf16[896,512]{1,0:T(8,128)(2,1)} %copy-done.11) | copy-start | bytes 2752516
  253.9 51.9 %all-to-all-start.1 = ((bf16[8,112,2176]{2,1,0:T(8,128)(2,1)}), bf16[8,112,2176]{2,1,0:T(8,128)(2,1)}, u32[]{:S(2)}, u32[]{:S(2)}) async-start(bf16[8,112,2176]{2,1,0:T(8,128)(2,1)} %bitcast.21), calls=%async_computation.1 | async-start | bytes 7798784 | tf_op jit(solution)/shard_map/all_to_all | solution.py:426
  265.2 93.2 %collective-permute-start.18 = (bf16[256,1408]{1,0:T(8,128)(2,1)}, bf16[256,1408]{1,0:T(8,128)(2,1)}, u32[]{:S(2)}, u32[]{:S(2)}) collective-permute-start(bf16[256,1408]{1,0:T(8,128)(2,1)} %reduce-scatter.7.cloned.1.call-done), channel_id=1, source_target_pairs={{0,4},{4,0},{1,5},{5,1},{2,6},{6,2},{3,7},{7,3},{8,12},{12,8},{9,1... | collective-permute-start | bytes 2162696 | tf_op jit(solution)/shard_map/ppermute | solution.py:418
  311.3 20.2 %collective-permute-start.15 = (bf16[128,2176]{1,0:T(8,128)(2,1)}, bf16[128,2176]{1,0:T(8,128)(2,1)S(1)}, u32[]{:S(2)}, u32[]{:S(2)}) collective-permute-start(bf16[128,2176]{1,0:T(8,128)(2,1)} %get-tuple-element.50), channel_id=1, source_target_pairs={{0,96},{32,0},{64,32},{96,64},{1,97},{33,1},{65,33},{97,65},{2,98}... | collective-permute-start | bytes 1671176 | tf_op jit(solution)/shard_map/ppermute | solution.py:430
  313.5 18.0 %collective-permute-start.16 = (bf16[128,2176]{1,0:T(8,128)(2,1)S(1)}, bf16[128,2176]{1,0:T(8,128)(2,1)S(1)}, u32[]{:S(2)}, u32[]{:S(2)}) collective-permute-start(bf16[128,2176]{1,0:T(8,128)(2,1)S(1)} %get-tuple-element.51), channel_id=1, source_target_pairs={{0,64},{32,96},{64,0},{96,32},{1,65},{33,97},{65,1},{97,33},{2,66}... | collective-permute-start | bytes 1671176 | tf_op jit(solution)/shard_map/ppermute | solution.py:430
  313.5 27.5 %collective-permute-start.17 = (bf16[128,2176]{1,0:T(8,128)(2,1)S(1)}, bf16[128,2176]{1,0:T(8,128)(2,1)S(1)}, u32[]{:S(2)}, u32[]{:S(2)}) collective-permute-start(bf16[128,2176]{1,0:T(8,128)(2,1)S(1)} %get-tuple-element.52), channel_id=1, source_target_pairs={{0,32},{32,64},{64,96},{96,0},{1,33},{33,65},{65,97},{97,1},{2,34}... | collective-permute-start | bytes 1671176 | tf_op jit(solution)/shard_map/ppermute | solution.py:430
  314.1 15.0 %collective-permute-start.19 = (bf16[704,256]{1,0:T(8,128)(2,1)}, bf16[704,256]{1,0:T(8,128)(2,1)}, u32[]{:S(2)}, u32[]{:S(2)}) collective-permute-start(bf16[704,256]{1,0:T(8,128)(2,1)} %reduce-scatter.11.cloned.1.call-done), channel_id=1, source_target_pairs={{0,4},{4,0},{1,5},{5,1},{2,6},{6,2},{3,7},{7,3},{8,12},{12,8},{9,1... | collective-permute-start | bytes 1081352 | tf_op jit(solution)/shard_map/ppermute | solution.py:418
Sparse Core Ops, SparseCore 0:
  10.2 40.5 all-gather.12
  53.1 37.4 all-gather.8
  92.2 25.3 all-gather.6
  125.2 22.3 all-gather.10
  229.1 36.0 reduce-scatter.6
  268.0 23.5 reduce-scatter.10
  294.1 24.7 reduce-scatter.8
  321.3 36.9 reduce-scatter.4

commit v2 on v1

v2 whole, which is shorter than its diff:
```python
import jax
import jax.numpy as jnp
from jax import lax
from jax.experimental import pallas as pl
from jax.experimental.pallas import tpu as pltpu
from jax.sharding import Mesh, PartitionSpec as P

TOP = 6
CAP = 28
SLOT = 32
EXPERTS = 32
D = 2048
F = 704
TOK = 128
WIDE = D + 128
PACK = 3 * F + 64
ROWS = 8 * 4 * CAP
BLK = 4 * CAP
BF = jnp.bfloat16
F32 = jnp.float32
MIB = 1 << 20
FINAL_FLOPS = 10**11


def params():
    return pltpu.CompilerParams(vmem_limit_bytes=60 * MIB)


def mm(a, b, ca=1, cb=0):
    return lax.dot_general(a, b, (((ca,), (cb,)), ((), ())), preferred_element_type=F32)


def whole(shape):
    return pl.BlockSpec(shape, lambda *_: (0,) * len(shape))


def cost(flops, moved):
    return pl.CostEstimate(flops=flops, bytes_accessed=moved, transcendentals=0)


def prepare_kernel(sc, tok, cot, routes, probs, gate_up, down, out_tok, out_cot, own, oth):
    z_hi = sc[3]
    line = lax.broadcasted_iota(jnp.int32, (128, TOK), 0)
    meta = jnp.zeros((128, TOK), F32)
    chosen = routes[...].astype(F32)
    weight = probs[...]
    for k in range(TOP):
        meta = jnp.where(line == k, chosen[k : k + 1, :], meta)
        meta = jnp.where(line == 8 + k, weight[k : k + 1, :], meta)
    meta = meta.T.astype(BF)
    for n in range(4):
        out_tok[n, :, :D] = tok[...]
        out_tok[n, :, D:] = meta
    out_cot[:, :D] = cot[...]
    out_cot[:, D:] = meta
    for out, which in ((own, z_hi), (oth, 1 - z_hi)):
        out[:, : 2 * F] = gate_up[which]
        out[:, 2 * F : 3 * F] = down[which].T
        out[:, 3 * F :] = jnp.zeros((256, PACK - 3 * F), BF)


def prepare(sc, tokens, cotangent, routes, probs, w_gate_up, w_down):
    vmem = pl.BlockSpec(memory_space=pltpu.VMEM)
    wide = jax.ShapeDtypeStruct((TOK, WIDE), BF)
    shard = jax.ShapeDtypeStruct((256, PACK), BF)
    return pl.pallas_call(
        prepare_kernel,
        in_specs=[pl.BlockSpec(memory_space=pltpu.SMEM)] + [vmem] * 6,
        out_specs=[vmem] * 4,
        out_shape=(jax.ShapeDtypeStruct((4, TOK, WIDE), BF), wide, shard, shard),
        compiler_params=params(),
        cost_estimate=cost(0, 8 * MIB),
    )(sc, tokens, cotangent, routes, probs, w_gate_up, w_down)


def pick_matrix(metas, experts, bases, weighted, sel):
    earlier = (
        lax.broadcasted_iota(jnp.int32, (TOK, TOK), 0)
        < lax.broadcasted_iota(jnp.int32, (TOK, TOK), 1)
    ).astype(BF)
    places, weights = [], []
    for d in range(4):
        turned = metas[d][...].astype(F32).T
        mask = jnp.zeros((8, TOK), F32)
        weight = jnp.zeros((8, TOK), F32)
        for k in range(TOP):
            hit = turned[k : k + 1, :] == experts
            mask = jnp.where(hit, 1.0, mask)
            weight = jnp.where(hit, turned[8 + k : 9 + k, :], weight)
        rank = mm(mask.astype(BF), earlier)
        places.append(jnp.where(mask > 0.5, rank + bases[d], -1.0))
        weights.append(weight if weighted else mask)
    place = jnp.concatenate(places, axis=1)
    weight = jnp.concatenate(weights, axis=1)
    row = lax.broadcasted_iota(jnp.int32, (BLK, 4 * TOK), 0).astype(F32)
    for j in range(8):
        sel[j * BLK : (j + 1) * BLK, :] = jnp.where(
            row == place[j : j + 1, :], weight[j : j + 1, :], 0.0
        ).astype(BF)


def pick_kernel(sc, *refs):
    x_tab, x_meta, c_tabs, c_metas = refs[0], refs[1], refs[2:6], refs[6:10]
    shard, x_out, shard_out = refs[10:13]
    c_outs, x_sel, c_sel = refs[13:21], refs[21], refs[22]
    y, z_lo, core, z_hi = sc[0], sc[1], sc[2], sc[3]
    z = z_hi * 2 + z_lo

    @pl.when(pl.program_id(0) == 0)
    def _():
        index = lax.broadcasted_iota(jnp.int32, (8, TOK), 0)
        bases = [float(n * CAP) for n in range(4)]
        x_metas = [x_meta.at[n] for n in range(4)]
        pick_matrix(x_metas, (y * 8 + index).astype(F32), bases, False, x_sel)
        experts = jnp.zeros((8, TOK), jnp.int32)
        for j in range(8):
            to_y, to_core = (y + j % 4) & 3, core ^ (j // 4)
            experts = jnp.where(
                index == j, ((to_y * 2 + z_lo) * 2 + to_core) * 2 + z_hi, experts
            )
        bases = [(((z - d) & 3) * CAP).astype(F32) for d in range(4)]
        pick_matrix(c_metas, experts.astype(F32), bases, True, c_sel)

    shard_out[...] = shard[...]
    x_out[...] = mm(x_sel[...], x_tab[...].reshape(4 * TOK, -1)).astype(BF)
    rows = mm(c_sel[...], jnp.concatenate([t[...] for t in c_tabs], axis=0)).astype(BF)
    for j in range(8):
        c_outs[j][...] = rows[j * BLK : (j + 1) * BLK, :]


def pick(sc, toks, cots, shard):
    step = 512
    column = lambda n, sc: (0, n)
    line = lambda n, sc: (n, 0)
    tables = [
        pl.BlockSpec((4, TOK, step), lambda n, sc: (0, 0, n)),
        pl.BlockSpec((4, TOK, 128), lambda n, sc: (0, 0, D // 128)),
    ]
    tables += [pl.BlockSpec((TOK, step), column)] * 4
    tables += [pl.BlockSpec((TOK, 128), lambda n, sc: (0, D // 128))] * 4
    outs = pl.pallas_call(
        pick_kernel,
        grid_spec=pltpu.PrefetchScalarGridSpec(
            num_scalar_prefetch=1,
            grid=(D // step,),
            in_specs=tables + [pl.BlockSpec((64, PACK), line)],
            out_specs=[
                pl.BlockSpec((ROWS, step), column),
                pl.BlockSpec((64, PACK), line),
            ]
            + [pl.BlockSpec((BLK, step), column)] * 8,
            scratch_shapes=[pltpu.VMEM((ROWS, 4 * TOK), BF)] * 2,
        ),
        out_shape=[
            jax.ShapeDtypeStruct((ROWS, D), BF),
            jax.ShapeDtypeStruct((256, PACK), BF),
        ]
        + [jax.ShapeDtypeStruct((BLK, D), BF)] * 8,
        compiler_params=params(),
        cost_estimate=cost(4 * ROWS * 512 * D, 16 * MIB),
    )(sc, toks, toks, *cots, *cots, shard)
    return outs[0], outs[1], outs[2:]


def expert_kernel(sc, *refs):
    arrived, (x_in, w_own, w_oth) = refs[:8], refs[8:11]
    scaled_out, d_both_out, hidden_out, q_out, grad_out = refs[11:16]
    x, table, w, scaled, d_both, hidden, act, slope, q_rows, grad = refs[16:26]
    sem_in, sem_out = refs[26:]
    y, z_lo, core, z_hi = sc[0], sc[1], sc[2], sc[3]
    tile = ROWS // 2
    loads, stores = [], []

    def fetch(src, dst):
        copy = pltpu.make_async_copy(src, dst, sem_in.at[len(loads)])
        copy.start()
        loads.append(copy)
        return copy

    def put(src, dst):
        copy = pltpu.make_async_copy(src, dst, sem_out.at[len(stores)])
        copy.start()
        stores.append(copy)

    own = pl.multiple_of(z_hi * 1024, 1024)
    oth = pl.multiple_of((1 - z_hi) * 1024, 1024)
    w_copies = [
        fetch(w_own, w.at[pl.ds(own, 1024)]),
        fetch(w_oth, w.at[pl.ds(oth, 1024)]),
    ]
    fetch_x = lambda m: fetch(
        x_in.at[pl.ds(m * tile, tile)], x.at[pl.ds(m * tile, tile)]
    )
    x_copies = [fetch_x(0)]
    lane = lax.broadcasted_iota(jnp.int32, (tile, 128), 1)
    expert = ((y * 2 + z_lo) * 2 + core) * 2 + z_hi

    for m in range(2):
        part = slice(m * tile, (m + 1) * tile)
        if m == 0:
            w_copies[0].wait()
            w_copies[1].wait()
            x_copies.append(fetch_x(1))
            c_copies = [
                fetch(arrived[j], table.at[pl.ds(j * BLK, BLK)]) for j in range(8)
            ]
        x_copies[m].wait()
        both = mm(x[part, :], w[:, : 2 * F])
        gate, up = both[:, :F], both[:, F:]
        logistic = jax.nn.sigmoid(gate)
        activated = gate * logistic
        hidden[part, :] = (activated * up).astype(BF)
        act[part, :] = activated
        slope[part, :] = up * logistic * (1.0 + gate * (1.0 - logistic))
    put(hidden, hidden_out)

    row = lax.broadcasted_iota(jnp.int32, (4 * BLK, 4 * BLK), 0)
    col = lax.broadcasted_iota(jnp.int32, (4 * BLK, 4 * BLK), 1)

    def split(v, size):
        major = sum([(v >= size * n).astype(jnp.int32) for n in range(1, 4)])
        return major, v - size * major

    row_z, row_rest = split(row, BLK)
    row_y, row_s = split(row_rest, CAP)
    col_d, col_rest = split(col, BLK)
    col_z, col_s = split(col_rest, CAP)
    turn = (
        (row_z == col_z) & (row_s == col_s) & (row_y == ((y - col_d) & 3))
    ).astype(F32).astype(BF)
    for copy in c_copies:
        copy.wait()
    for dc in range(2):
        from_core = core ^ dc
        for n in range(0, D, 512):
            moved = mm(turn, table[dc * 4 * BLK : (dc + 1) * 4 * BLK, n : n + 512]).astype(BF)
            for z in range(4):
                place = (z % 2) * 4 + from_core * 2 + z // 2
                start = pl.multiple_of(place * BLK, 16)
                scaled[pl.ds(start, BLK), n : n + 512] = moved[z * BLK : (z + 1) * BLK, :]
    put(scaled, scaled_out)

    for m in range(2):
        part = slice(m * tile, (m + 1) * tile)
        total = mm(scaled[part, :], w[:, 2 * F : 3 * F])
        d_both[part, :] = jnp.concatenate(
            [(total * slope[part, :]).astype(BF), (total * act[part, :]).astype(BF)], axis=1
        )
        q = jnp.sum(total * hidden[part, :].astype(F32), axis=1, keepdims=True)
        q_rows[part, :] = jnp.where(lane == expert, q, 0.0).astype(BF)
    put(d_both, d_both_out)
    put(q_rows, q_out)

    for i in range(4):
        start = pl.multiple_of(oth + i * 256, 256)
        line = slice(i * 256, (i + 1) * 256)
        grad[line, : 2 * F] = mm(x[:, pl.ds(start, 256)], d_both[...], 0, 0).astype(BF)
        grad[line, 2 * F : 3 * F] = mm(scaled[:, pl.ds(start, 256)], hidden[...], 0, 0).astype(BF)
        grad[line, 3 * F :] = jnp.zeros((256, PACK - 3 * F), BF)
        put(grad.at[pl.ds(i * 256, 256)], grad_out.at[pl.ds(i * 256, 256)])
    for copy in stores:
        copy.wait()


def expert_pass(sc, x_rows, arrived, w_own, w_oth):
    anywhere = pl.BlockSpec(memory_space=pl.ANY)
    shapes = [(ROWS, D), (ROWS, 2 * F), (ROWS, F), (ROWS, 128), (1024, PACK)]
    scratch = [
        ((ROWS, D), BF),
        ((ROWS, D), BF),
        ((D, PACK), BF),
        ((ROWS, D), BF),
        ((ROWS, 2 * F), BF),
        ((ROWS, F), BF),
        ((ROWS, F), F32),
        ((ROWS, F), F32),
        ((ROWS, 128), BF),
        ((1024, PACK), BF),
    ]
    return pl.pallas_call(
        expert_kernel,
        in_specs=[pl.BlockSpec(memory_space=pltpu.SMEM)] + [anywhere] * 11,
        out_specs=[anywhere] * 5,
        out_shape=[jax.ShapeDtypeStruct(shape, BF) for shape in shapes],
        scratch_shapes=[pltpu.VMEM(*item) for item in scratch]
        + [pltpu.SemaphoreType.DMA((12,)), pltpu.SemaphoreType.DMA((8,))],
        compiler_params=params(),
        cost_estimate=cost(2 * ROWS * D * 6 * F, 32 * MIB),
    )(sc, *arrived, x_rows, w_own, w_oth)


def inputs_kernel(sc, d_both_in, q, w_own, w_oth, dx_out, d_both, w, dx, sem_in, sem_out):
    z_hi = sc[3]
    tile = ROWS // 2
    own = pl.multiple_of(z_hi * 1024, 1024)
    oth = pl.multiple_of((1 - z_hi) * 1024, 1024)
    pairs = (
        (d_both_in, d_both),
        (w_own.at[:, pl.ds(0, 2 * F)], w.at[pl.ds(own, 1024)]),
        (w_oth.at[:, pl.ds(0, 2 * F)], w.at[pl.ds(oth, 1024)]),
    )
    loads = [pltpu.make_async_copy(*pair, sem_in.at[i]) for i, pair in enumerate(pairs)]
    stores = []
    for copy in loads:
        copy.start()
    extra = q[...].astype(F32)
    for copy in loads:
        copy.wait()
    for m in range(2):
        part = slice(m * tile, (m + 1) * tile)
        rows = mm(d_both[part, :], w[...], 1, 1)
        for to_y in range(4):
            for j in range(4):
                first, block = j * BLK + to_y * CAP, to_y * 8 + m * 4 + j
                dx[block, :, :D] = rows[first : first + CAP, :].astype(BF)
                first += m * tile
                dx[block, :, D:] = extra[first : first + CAP, :].astype(BF)
            span = pl.ds(to_y * 8 + m * 4, 4)
            copy = pltpu.make_async_copy(dx.at[span], dx_out.at[span], sem_out.at[len(stores)])
            copy.start()
            stores.append(copy)
    for copy in stores:
        copy.wait()


def input_grads(sc, d_both, q, w_own, w_oth):
    anywhere = pl.BlockSpec(memory_space=pl.ANY)
    scratch = [(ROWS, 2 * F), (D, 2 * F), (EXPERTS, CAP, WIDE)]
    return pl.pallas_call(
        inputs_kernel,
        in_specs=[
            pl.BlockSpec(memory_space=pltpu.SMEM),
            anywhere,
            pl.BlockSpec(memory_space=pltpu.VMEM),
            anywhere,
            anywhere,
        ],
        out_specs=anywhere,
        out_shape=jax.ShapeDtypeStruct((EXPERTS, CAP, WIDE), BF),
        scratch_shapes=[pltpu.VMEM(shape, BF) for shape in scratch]
        + [pltpu.SemaphoreType.DMA((3,)), pltpu.SemaphoreType.DMA((8,))],
        compiler_params=params(),
        cost_estimate=cost(2 * ROWS * D * 2 * F, 16 * MIB),
    )(sc, d_both, q, w_own, w_oth)


def grads_kernel(sc, x_in, scaled_in, d_both_in, hidden_in, grad_out, *refs):
    x, scaled, d_both, hidden, grad, sem_in, sem_out = refs
    own = pl.multiple_of(sc[3] * 1024, 1024)
    pairs = (
        (d_both_in, d_both),
        (x_in.at[:, pl.ds(own, 1024)], x),
        (hidden_in, hidden),
        (scaled_in.at[:, pl.ds(own, 1024)], scaled),
    )
    loads = [pltpu.make_async_copy(*pair, sem_in.at[i]) for i, pair in enumerate(pairs)]
    stores = []
    for copy in loads:
        copy.start()
    for copy in loads:
        copy.wait()
    for i in range(4):
        line = slice(i * 256, (i + 1) * 256)
        grad[line, : 2 * F] = mm(x[:, line], d_both[...], 0, 0).astype(BF)
        grad[line, 2 * F : 3 * F] = mm(scaled[:, line], hidden[...], 0, 0).astype(BF)
        grad[line, 3 * F :] = jnp.zeros((256, PACK - 3 * F), BF)
        span = pl.ds(i * 256, 256)
        copy = pltpu.make_async_copy(grad.at[span], grad_out.at[span], sem_out.at[i])
        copy.start()
        stores.append(copy)
    for copy in stores:
        copy.wait()


def own_grads(sc, x_rows, scaled, d_both, hidden):
    anywhere = pl.BlockSpec(memory_space=pl.ANY)
    scratch = [(ROWS, 1024), (ROWS, 1024), (ROWS, 2 * F), (ROWS, F), (1024, PACK)]
    return pl.pallas_call(
        grads_kernel,
        in_specs=[pl.BlockSpec(memory_space=pltpu.SMEM)] + [anywhere] * 4,
        out_specs=anywhere,
        out_shape=jax.ShapeDtypeStruct((1024, PACK), BF),
        scratch_shapes=[pltpu.VMEM(shape, BF) for shape in scratch]
        + [pltpu.SemaphoreType.DMA((4,)), pltpu.SemaphoreType.DMA((4,))],
        compiler_params=params(),
        cost_estimate=cost(2 * ROWS * 1024 * 3 * F, 12 * MIB),
    )(sc, x_rows, scaled, d_both, hidden)


def final_kernel(back, routes, probs, out, out_probs, sel, rows):
    experts = lax.broadcasted_iota(jnp.int32, (EXPERTS, TOK), 0)
    mask = jnp.zeros((EXPERTS, TOK), F32)
    for k in range(TOP):
        mask = jnp.where(routes[k : k + 1, :] == experts, 1.0, mask)
    earlier = (
        lax.broadcasted_iota(jnp.int32, (TOK, TOK), 0)
        < lax.broadcasted_iota(jnp.int32, (TOK, TOK), 1)
    ).astype(BF)
    place = jnp.where(mask > 0.5, mm(mask.astype(BF), earlier), -1.0)
    slot = lax.broadcasted_iota(jnp.int32, (SLOT, TOK), 0).astype(F32)
    for e in range(EXPERTS):
        line = slice(e * SLOT, (e + 1) * SLOT)
        sel[line, :] = (slot == place[e : e + 1, :]).astype(F32).astype(BF)
        rows[e, :CAP, :] = back[e]
        rows[e, CAP:, :] = jnp.zeros((SLOT - CAP, WIDE), BF)
    table = rows[...].reshape(EXPERTS * SLOT, WIDE)
    for n in range(0, D, 512):
        out[:, n : n + 512] = mm(sel[...], table[:, n : n + 512], 0, 0).astype(BF)
    values = mm(table[:, D:], sel[...], 0, 0)
    weight = probs[...].astype(BF).astype(F32)
    line = lax.broadcasted_iota(jnp.int32, (128, TOK), 0)
    for k in range(TOP):
        value = jnp.sum(
            jnp.where(line == routes[k : k + 1, :], values, 0.0), axis=0, keepdims=True
        )
        out_probs[k : k + 1, :] = value / weight[k : k + 1, :]


def final(back, routes, probs):
    return pl.pallas_call(
        final_kernel,
        out_shape=[
            jax.ShapeDtypeStruct((TOK, D), BF),
            jax.ShapeDtypeStruct((TOP, TOK), F32),
        ],
        scratch_shapes=[
            pltpu.VMEM((EXPERTS * SLOT, TOK), BF),
            pltpu.VMEM((EXPERTS, SLOT, WIDE), BF),
        ],
        compiler_params=params(),
        cost_estimate=cost(FINAL_FLOPS, 8 * MIB),
    )(back, routes, probs)


def place_kernel(sc, own, oth, gate_up, down, turned, sems):
    copies = []
    for i, (part, which) in enumerate(((oth, 1 - sc[3]), (own, sc[3]))):
        copy = pltpu.make_async_copy(
            part.at[:, pl.ds(0, 2 * F)], gate_up.at[which], sems.at[2 * i]
        )
        copy.start()
        turned[i] = part[:, 2 * F : 3 * F].T
        after = pltpu.make_async_copy(turned.at[i], down.at[which], sems.at[2 * i + 1])
        after.start()
        copies += [copy, after]
    for copy in copies:
        copy.wait()


def place(sc, own, oth):
    vmem = pl.BlockSpec(memory_space=pltpu.VMEM)
    return pl.pallas_call(
        place_kernel,
        in_specs=[pl.BlockSpec(memory_space=pltpu.SMEM), vmem, vmem],
        out_specs=[pl.BlockSpec(memory_space=pl.ANY)] * 2,
        out_shape=[
            jax.ShapeDtypeStruct((2, 256, 2 * F), BF),
            jax.ShapeDtypeStruct((2, F, 256), BF),
        ],
        scratch_shapes=[pltpu.VMEM((2, F, 256), BF), pltpu.SemaphoreType.DMA((4,))],
        compiler_params=params(),
        cost_estimate=cost(0, 5 * MIB),
    )(sc, own, oth)


def z_index(z):
    return (z % 2) * 2 + z // 2


def along_y(k):
    return [(y, (y + k) % 4) for y in range(4)]


def along_z(k):
    return [(z_index(z), z_index((z + k) % 4)) for z in range(4)]


def along_yc(k, dc):
    return [(y * 2 + c, ((y + k) % 4) * 2 + (c ^ dc)) for y in range(4) for c in range(2)]


def body(tokens, cotangent, routes, probs, w_gate_up, w_down):
    names = ("y", "zl", "c", "zh", "x")
    sc = jnp.stack([lax.axis_index(n) for n in names]).astype(jnp.int32)
    tok, cot, own, oth = prepare(
        sc, tokens, cotangent, routes.T, probs.T, w_gate_up, w_down
    )
    cots = [cot] + [lax.ppermute(cot, ("zl", "zh"), along_z(k)) for k in (1, 2, 3)]
    toks = lax.all_to_all(tok, "y", split_axis=0, concat_axis=0, tiled=True)
    swap = [(0, 1), (1, 0)]
    gather = lambda w: lax.all_gather(w, "x", axis=0, tiled=True)
    x_send, oth, sent = pick(sc, toks, cots, lax.ppermute(oth, "zh", swap))
    w_own, w_oth = gather(own), gather(oth)

    x_rows = lax.all_to_all(
        x_send.reshape(8, BLK, D), ("zl", "c", "zh"), split_axis=0, concat_axis=0, tiled=True
    ).reshape(ROWS, D)
    arrived = [
        sent[j] if j == 0 else lax.ppermute(sent[j], ("y", "c"), along_yc(j % 4, j // 4))
        for j in range(8)
    ]
    scaled, d_both, hidden, q, oth_part = expert_pass(sc, x_rows, arrived, w_own, w_oth)

    scatter = lambda g: lax.psum_scatter(g, "x", scatter_dimension=0, tiled=True)
    oth_sum = lax.ppermute(scatter(oth_part), "zh", swap)
    dx = input_grads(sc, d_both, q, w_own, w_oth)
    own_sum = scatter(own_grads(sc, x_rows, scaled, d_both, hidden))
    back = lax.all_to_all(
        dx, ("y", "zl", "c", "zh"), split_axis=0, concat_axis=0, tiled=True
    )
    d_tokens, d_probs = final(back, routes.T, probs.T)
    grad_gu, grad_dn = place(sc, own_sum, oth_sum)
    return d_tokens, d_probs.T, grad_gu, grad_dn


def solution(mesh):
    fine = Mesh(mesh.devices.reshape(4, 2, 2, 2, 4), ("y", "zl", "c", "zh", "x"))
    exp, fsdp = ("y", "zl", "c"), ("zh", "x")
    row = P(exp + fsdp, None)
    gate_up, down = P(exp, fsdp, None), P(exp, None, fsdp)
    return jax.shard_map(
        body,
        mesh=fine,
        in_specs=(row, row, row, row, gate_up, down),
        out_specs=(row, row, gate_up, down),
        check_vma=False,
    )
```

time: 369 us -> 272 us (0.74)
  waiting for transfers between devices: 220 us -> 138 us
  local copies, waits for them, and re-layouts: 20.6 us -> 4.71 us
  starting transfers between devices: 38 us -> 47.3 us
  other arithmetic: 5.79 us -> 0 us
    ppermute x13 -> x5, waiting for transfers between devices: 135 us -> 47.9 us  [the longest x3 46.4 us: body(): lax.ppermute(cot, ('zl', 'zh'), along_z(k))]
    reduce_scatter x4 -> x2, waiting for transfers between devices: 23.7 us -> 38.1 us  [body(): lax.psum_scatter(g, 'x', scatter_dimension=0, tiled=True)]
    ppermute x7, starting transfers between devices: 6.24 us -> 19 us  [body(): lax.ppermute(sent[j], ('y', 'c'), along_yc(j % 4, j // 4))]
    unnamed x41 -> x32, local copies, waits for them, and re-layouts: 16.4 us -> 4.09 us
    all_to_all x1 -> x2, waiting for transfers between devices: 37.7 us -> 25.5 us  [the longest x1 25.5 us: body(): lax.all_to_all(dx, ('y', 'zl', 'c', 'zh'), split_axis=0, concat_axis=0, t...]
    ppermute x13 -> x5, starting transfers between devices: 20.2 us -> 9.07 us  [the longest x1 3.67 us: body(): x_send, oth, sent = pick(sc, toks, cots, lax.ppermute(oth, 'zh', swap))]
    all_to_all x1 -> x2, starting transfers between devices: 6.15 us -> 12.9 us  [the longest x1 7.76 us: body(): lax.all_to_all(dx, ('y', 'zl', 'c', 'zh'), split_axis=0, concat_axis=0, t...]
    select_n x2 -> x0, other arithmetic: 5.79 us -> none  [body(): jnp.where(z_hi == 0, jnp.stack([a, b]), jnp.stack([b, a]))]
  transfers between devices with their start and end apart: 30 -> 19, of which waited for: 16 -> 10; matrix products, arithmetic and copies ran while one was open for 1% -> 0% of each run, Pallas kernels for 13% -> 13%
where the time goes in v2:
time: 272 us; the launch traced here: 271 us
  waiting for transfers between devices  138 us (51%)
  Pallas kernels  66.7 us (25%)
  starting transfers between devices  47.3 us (17%)
  between operations  13.9 us (5%)
  local copies, waits for them, and re-layouts  4.71 us (2%)
    ppermute x3, waiting for transfers between devices, body(): lax.ppermute(cot, ('zl', 'zh'), along_z(k))  46.4 us
    reduce_scatter x2, waiting for transfers between devices, body(): lax.psum_scatter(g, 'x', scatter_dimension=0, tiled=True)  38.1 us
    all_to_all x1, waiting for transfers between devices, body(): lax.all_to_all(dx, ('y', 'zl', 'c', 'zh'), split_axis=0, concat_axis=0, t...  25.5 us
    ppermute x7, waiting for transfers between devices, body(): lax.ppermute(sent[j], ('y', 'c'), along_yc(j % 4, j // 4))  25.3 us
    pallas_call x1, Pallas kernels, expert_pass(): pl.pallas_call(expert_kernel, in_specs=[pl.BlockSpec(memory_space=pltpu.S...  23.8 us
    ppermute x7, starting transfers between devices, body(): lax.ppermute(sent[j], ('y', 'c'), along_yc(j % 4, j // 4))  19 us
    pallas_call x1, Pallas kernels, input_grads(): pl.pallas_call(inputs_kernel, in_specs=[pl.BlockSpec(memory_space=pltpu.S...  11.8 us
    pallas_call x1, Pallas kernels, own_grads(): pl.pallas_call(grads_kernel, in_specs=[pl.BlockSpec(memory_space=pltpu.SM...  10.2 us
  transfers between devices with their start and end apart: 19, of which 10 were waited for; matrix products, arithmetic and copies ran while one was open for 0% of the time, Pallas kernels for 13%

profile of v2, /device:TPU:1, one launch (start us, length us, event | category | flops | bytes accessed | tf_op | source)
XLA Modules:
  0.0 271.0 jit_solution(17575935286963274398)
XLA Ops:
  7.2 0.0 all-gather.3.cloned.1.call-start
  7.2 0.6 stack.23.sc
  7.8 4.5 %shard_map.93 = (bf16[4,128,2176]{2,1,0:T(8,128)(2,1)}, bf16[128,2176]{1,0:T(8,128)(2,1)}, bf16[256,2176]{1,0:T(8,128)(2,1)}, bf16[256,2176]{1,0:T(8,128)(2,1)}) custom-call(s32[5]{0:T(128)} %stack.23.sc, bf16[128,2048]{1,0:T(8,128)(2,1)} %tok.1, bf16[128,2048]{1,0:T(8,128)(2,1)} %cot.1, s32[6,128]{1,0:T(8,128)} %bitcast.11, f32[6,128]{1,0:T(8,128)} %bitcast.13, ...), custom_call_target="tpu_custom_call" | custom-call | bytes 8388608 | tf_op jit(solution)/shard_map/pallas_call | solution.py:66
  12.3 0.0 all-gather.3.cloned.1.call-update
  12.3 0.0 copy-start.2
  12.4 5.2 %all-to-all-start = ((bf16[4,128,2176]{2,1,0:T(8,128)(2,1)}), bf16[4,128,2176]{2,1,0:T(8,128)(2,1)S(1)}, u32[]{:S(2)}, u32[]{:S(2)}) async-start(bf16[4,128,2176]{2,1,0:T(8,128)(2,1)} %get-tuple-element.27), calls=%async_computation | async-start | bytes 4456448 | tf_op jit(solution)/shard_map/all_to_all | solution.py:489
  17.5 0.0 all-gather.5.cloned.1.call-start
  17.5 0.0 copy-done.2
  17.5 3.7 %collective-permute-start.3 = (bf16[256,2176]{1,0:T(8,128)(2,1)S(1)}, bf16[256,2176]{1,0:T(8,128)(2,1)}, u32[]{:S(2)}, u32[]{:S(2)}) collective-permute-start(bf16[256,2176]{1,0:T(8,128)(2,1)S(1)} %copy-done.2), channel_id=1, source_target_pairs={{0,4},{4,0},{1,5},{5,1},{2,6},{6,2},{3,7},{7,3},{8,12},{12,8},{9,1... | collective-permute-start | bytes 3342344 | tf_op jit(solution)/shard_map/ppermute | solution.py:492
  21.2 0.4 collective-permute-start.2
  21.6 2.1 collective-permute-start.1
  23.7 0.0 collective-permute-start
  23.7 35.1 %collective-permute-done.2.refs_5_.refs_9_ = bf16[128,2176]{1,0:T(8,128)(2,1)S(1)} collective-permute-done((bf16[128,2176]{1,0:T(8,128)(2,1)}, bf16[128,2176]{1,0:T(8,128)(2,1)S(1)}, u32[]{:S(2)}, u32[]{:S(2)}) %collective-permute-start.2) | collective-permute-done | bytes 557088 | tf_op jit(solution)/shard_map/ppermute | solution.py:488
  58.8 0.0 collective-permute-done.1.refs_4_.refs_8_
  58.8 11.3 %collective-permute-done.refs_3_.refs_7_ = bf16[128,2176]{1,0:T(8,128)(2,1)S(1)} collective-permute-done((bf16[128,2176]{1,0:T(8,128)(2,1)}, bf16[128,2176]{1,0:T(8,128)(2,1)S(1)}, u32[]{:S(2)}, u32[]{:S(2)}) %collective-permute-start) | collective-permute-done | bytes 557088 | tf_op jit(solution)/shard_map/ppermute | solution.py:488
  70.1 0.0 copy-done.3
  70.1 0.0 copy-done.4
  70.1 0.8 copy-done.5
  70.9 0.0 collective-permute-done.3.refs_10_
  70.9 0.0 all-to-all-done.refs_0_.refs_1_
  70.9 1.4 copy-done
  72.4 9.3 %shard_map.94 = (bf16[896,2048]{1,0:T(8,128)(2,1)}, bf16[256,2176]{1,0:T(8,128)(2,1)}, bf16[112,2048]{1,0:T(8,128)(2,1)}, bf16[112,2048]{1,0:T(8,128)(2,1)}, bf1...) custom-call(s32[5]{0:T(128)} %stack.23.sc, ...), custom_call_target="tpu_custom_call" | custom-call | flops 3758096384 | bytes 16777216 | tf_op jit(solution)/shard_map/pallas_call | solution.py:141
  81.7 0.0 all-gather.5.cloned.1.call-update
  81.7 0.0 copy-start.11
  81.7 0.0 copy-start.9
  81.7 0.0 copy-start.7
  81.7 0.0 copy-start.6
  81.8 6.2 %all-to-all-start.1 = ((bf16[8,112,2048]{2,1,0:T(8,128)(2,1)}), bf16[8,112,2048]{2,1,0:T(8,128)(2,1)}, u32[]{:S(2)}, u32[]{:S(2)}) async-start(bf16[8,112,2048]{2,1,0:T(8,128)(2,1)} %bitcast.10), calls=%async_computation.1 | async-start | bytes 7340032 | tf_op jit(solution)/shard_map/all_to_all | solution.py:495
  88.0 0.0 reduce-scatter.5.cloned.1.call-start
  88.0 1.4 collective-permute-start.4
  89.4 2.4 collective-permute-start.5
  91.8 1.2 collective-permute-start.6
  93.0 0.9 collective-permute-start.7
  93.9 0.2 collective-permute-start.8
  94.1 7.5 %collective-permute-done.4.refs_1_ = bf16[112,2048]{1,0:T(8,128)(2,1)S(1)} collective-permute-done((bf16[112,2048]{1,0:T(8,128)(2,1)}, bf16[112,2048]{1,0:T(8,128)(2,1)S(1)}, u32[]{:S(2)}, u32[]{:S(2)}) %collective-permute-start.4) | collective-permute-done | bytes 458784 | tf_op jit(solution)/shard_map/ppermute | solution.py:499
  101.6 12.6 %collective-permute-start.9 = (bf16[112,2048]{1,0:T(8,128)(2,1)S(1)}, bf16[112,2048]{1,0:T(8,128)(2,1)S(1)}, u32[]{:S(2)}, u32[]{:S(2)}) collective-permute-start(bf16[112,2048]{1,0:T(8,128)(2,1)S(1)} %copy-done.7), channel_id=1, source_target_pairs={{0,72},{8,64},{32,104},{40,96},{64,8},{72,0},{96,40},{104,32},{1,7... | collective-permute-start | bytes 1376264 | tf_op jit(solution)/shard_map/ppermute | solution.py:499
  114.2 0.0 collective-permute-done.5.refs_2_
  114.2 0.0 copy-done.6
  114.2 0.3 collective-permute-start.10
  114.4 0.0 collective-permute-done.6.refs_3_
  114.5 0.0 collective-permute-done.7.refs_4_
  114.5 7.2 %collective-permute-done.8.refs_5_ = bf16[112,2048]{1,0:T(8,128)(2,1)S(1)} collective-permute-done((bf16[112,2048]{1,0:T(8,128)(2,1)S(1)}, bf16[112,2048]{1,0:T(8,128)(2,1)S(1)}, u32[]{:S(2)}, u32[]{:S(2)}) %collective-permute-start.8) | collective-permute-done | bytes 458784 | tf_op jit(solution)/shard_map/ppermute | solution.py:499
  121.7 10.6 %collective-permute-done.9.refs_6_ = bf16[112,2048]{1,0:T(8,128)(2,1)S(1)} collective-permute-done((bf16[112,2048]{1,0:T(8,128)(2,1)S(1)}, bf16[112,2048]{1,0:T(8,128)(2,1)S(1)}, u32[]{:S(2)}, u32[]{:S(2)}) %collective-permute-start.9) | collective-permute-done | bytes 458784 | tf_op jit(solution)/shard_map/ppermute | solution.py:499
  132.3 0.0 copy-done.13
  132.4 0.8 copy-done.15
  133.1 0.0 collective-permute-done.10.refs_7_
  133.1 0.0 all-to-all-done.1
  133.1 1.6 all-gather.5.cloned.1.call-done.refs_10_.w_oth
  134.7 0.0 copy-done.10
  134.7 23.8 %shard_map.95 = (bf16[896,2048]{1,0:T(8,128)(2,1)}, bf16[896,1408]{1,0:T(8,128)(2,1)}, bf16[896,704]{1,0:T(8,128)(2,1)}, bf16[896,128]{1,0:T(8,128)(2,1)}, bf16[1024,2176]{1,0:T(8,128)(2,1)}) custom-call(s32[5]{0:T(128)} %stack.23.sc, bf16[112,2048]{1,0:T(8,128)(2,1)} %get-tuple-element.30.refs_0_, bf16[112,2048]{1,0:T(8,128)(2,1)} %copy-done.8, ...), custom_call_target="tpu_custom_call" | custom-call | flops 15502147584 | bytes 33554432 | tf_op jit(solution)/shard_map/pallas_call | solution.py:280
  158.5 0.0 reduce-scatter.5.cloned.1.call-update
  158.5 11.8 %shard_map.96 = bf16[32,28,2176]{2,1,0:T(8,128)(2,1)} custom-call(s32[5]{0:T(128)} %stack.23.sc, bf16[896,1408]{1,0:T(8,128)(2,1)} %get-tuple-element.41.d_both_in, bf16[896,128]{1,0:T(8,128)(2,1)} %get-tuple-element.42.q, bf16[1024,2176]{1,0:T(8,128)(2,1)} %all-gather.3.cloned.1.call-done.refs_9_.w_own, ...), custom_call_target="tpu_custom_call" | custom-call | flops 5167382528 | bytes 16777216 | tf_op jit(solution)/shard_map/pallas_call | solution.py:329
  170.4 7.8 %all-to-all-start.2 = ((bf16[32,28,2176]{2,1,0:T(8,128)(2,1)}), bf16[32,28,2176]{2,1,0:T(8,128)(2,1)}, u32[]{:S(2)}, u32[]{:S(2)}) async-start(bf16[32,28,2176]{2,1,0:T(8,128)(2,1)} %shard_map.96), calls=%async_computation.2 | async-start | bytes 8912896 | tf_op jit(solution)/shard_map/all_to_all | solution.py:508
  178.1 0.0 reduce-scatter.3.cloned.1.call-start
  178.2 10.2 %shard_map.98 = bf16[1024,2176]{1,0:T(8,128)(2,1)} custom-call(s32[5]{0:T(128)} %stack.23.sc, bf16[896,2048]{1,0:T(8,128)(2,1)} %bitcast.8.refs_8_.x_in, bf16[896,2048]{1,0:T(8,128)(2,1)} %get-tuple-element.45.scaled_in, bf16[896,1408]{1,0:T(8,128)(2,1)} %get-tuple-element.41.d_both_in, bf16[896,704]{1,0:T(8,128)(2,1)} %get-tuple-element.46.hidden_in), custom_call_target="tpu_custom_call" | custom-call | flops 3875536896 | bytes 12582912 | tf_op jit(solution)/shard_map/pallas_call | solution.py:378
  188.4 0.0 reduce-scatter.3.cloned.1.call-update
  188.4 19.6 %reduce-scatter.5.cloned.1.call-done = bf16[256,2176]{1,0:T(8,128)(2,1)} async-done(((bf16[1024,2176]{1,0:T(8,128)(2,1)}), bf16[256,2176]{1,0:T(8,128)(2,1)}) %reduce-scatter.5.cloned.1.call-update) | async-done | bytes 1114128 | tf_op jit(solution)/shard_map/reduce_scatter | solution.py:504
  208.0 2.9 %collective-permute-start.11 = (bf16[256,2176]{1,0:T(8,128)(2,1)}, bf16[256,2176]{1,0:T(8,128)(2,1)S(1)}, u32[]{:S(2)}, u32[]{:S(2)}) collective-permute-start(bf16[256,2176]{1,0:T(8,128)(2,1)} %reduce-scatter.5.cloned.1.call-done), channel_id=1, source_target_pairs={{0,4},{4,0},{1,5},{5,1},{2,6},{6,2},{3,7},{7,3},{8,12},{12,8},{9,1... | collective-permute-start | bytes 3342344 | tf_op jit(solution)/shard_map/ppermute | solution.py:505
  210.9 25.5 %all-to-all-done.2.back = bf16[32,28,2176]{2,1,0:T(8,128)(2,1)} async-done(((bf16[32,28,2176]{2,1,0:T(8,128)(2,1)}), bf16[32,28,2176]{2,1,0:T(8,128)(2,1)}, u32[]{:S(2)}, u32[]{:S(2)}) %all-to-all-start.2) | async-done | bytes 3899424 | tf_op jit(solution)/shard_map/all_to_all | solution.py:508
  236.4 4.1 %shard_map.97 = (bf16[128,2048]{1,0:T(8,128)(2,1)}, f32[6,128]{1,0:T(8,128)}) custom-call(bf16[32,28,2176]{2,1,0:T(8,128)(2,1)} %all-to-all-done.2.back, s32[6,128]{1,0:T(8,128)} %bitcast.12, f32[6,128]{1,0:T(8,128)} %bitcast.14), custom_call_target="tpu_custom_call" | custom-call | flops 99999997952 | bytes 8388608 | tf_op jit(solution)/shard_map/pallas_call | solution.py:420
  240.5 18.5 %reduce-scatter.3.cloned.1.call-done.own = bf16[256,2176]{1,0:T(8,128)(2,1)} async-done(((bf16[1024,2176]{1,0:T(8,128)(2,1)}), bf16[256,2176]{1,0:T(8,128)(2,1)}) %reduce-scatter.3.cloned.1.call-update) | async-done | bytes 1114128 | tf_op jit(solution)/shard_map/reduce_scatter | solution.py:504
  259.0 1.5 collective-permute-done.11.oth
  260.5 1.0 copy-done.1
  261.5 3.0 %shard_map.99 = (bf16[2,256,1408]{2,1,0:T(8,128)(2,1)}, bf16[2,704,256]{2,1,0:T(8,128)(2,1)}) custom-call(s32[5]{0:T(128)} %stack.23.sc, bf16[256,2176]{1,0:T(8,128)(2,1)} %reduce-scatter.3.cloned.1.call-done.own, bf16[256,2176]{1,0:T(8,128)(2,1)} %copy-done.1), custom_call_target="tpu_custom_call" | custom-call | bytes 5242880 | tf_op jit(solution)/shard_map/pallas_call | solution.py:452
  (18 shorter events, 0.0 us)
Async XLA Ops:
  7.2 126.0 %all-gather.3.cloned.1.call-start = ((), (), s32[]{:S(2)}) async-start(), calls=%async_computation.5 | async-start | bytes 5570560 | tf_op jit(solution)/shard_map/all_gather | solution.py:491
  12.3 5.2 %copy-start.2 = (bf16[256,2176]{1,0:T(8,128)(2,1)S(1)}, bf16[256,2176]{1,0:T(8,128)(2,1)}, u32[]{:S(2)}) copy-start(bf16[256,2176]{1,0:T(8,128)(2,1)} %get-tuple-element.29) | copy-start | bytes 3342340
  12.4 58.6 %all-to-all-start = ((bf16[4,128,2176]{2,1,0:T(8,128)(2,1)}), bf16[4,128,2176]{2,1,0:T(8,128)(2,1)S(1)}, u32[]{:S(2)}, u32[]{:S(2)}) async-start(bf16[4,128,2176]{2,1,0:T(8,128)(2,1)} %get-tuple-element.27), calls=%async_computation | async-start | bytes 4456448 | tf_op jit(solution)/shard_map/all_to_all | solution.py:489
  17.5 117.2 %all-gather.5.cloned.1.call-start = ((), (), s32[]{:S(2)}) async-start(), calls=%async_computation.6 | async-start | bytes 5570560 | tf_op jit(solution)/shard_map/all_gather | solution.py:491
  17.5 53.4 %collective-permute-start.3 = (bf16[256,2176]{1,0:T(8,128)(2,1)S(1)}, bf16[256,2176]{1,0:T(8,128)(2,1)}, u32[]{:S(2)}, u32[]{:S(2)}) collective-permute-start(bf16[256,2176]{1,0:T(8,128)(2,1)S(1)} %copy-done.2), channel_id=1, source_target_pairs={{0,4},{4,0},{1,5},{5,1},{2,6},{6,2},{3,7},{7,3},{8,12},{12,8},{9,1... | collective-permute-start | bytes 3342344 | tf_op jit(solution)/shard_map/ppermute | solution.py:492
  21.2 37.6 %collective-permute-start.2 = (bf16[128,2176]{1,0:T(8,128)(2,1)}, bf16[128,2176]{1,0:T(8,128)(2,1)S(1)}, u32[]{:S(2)}, u32[]{:S(2)}) collective-permute-start(bf16[128,2176]{1,0:T(8,128)(2,1)} %get-tuple-element.28.refs_2_.refs_6_), channel_id=1, source_target_pairs={{0,20},{16,0},{4,16},{20,4},{1,21},{17,1},{5,17},{21,5},{2,22},{18... | collective-permute-start | bytes 1671176 | tf_op jit(solution)/shard_map/ppermute | solution.py:488
  21.6 37.2 %collective-permute-start.1 = (bf16[128,2176]{1,0:T(8,128)(2,1)}, bf16[128,2176]{1,0:T(8,128)(2,1)S(1)}, u32[]{:S(2)}, u32[]{:S(2)}) collective-permute-start(bf16[128,2176]{1,0:T(8,128)(2,1)} %get-tuple-element.28.refs_2_.refs_6_), channel_id=1, source_target_pairs={{0,4},{16,20},{4,0},{20,16},{1,5},{17,21},{5,1},{21,17},{2,6},{18,... | collective-permute-start | bytes 1671176 | tf_op jit(solution)/shard_map/ppermute | solution.py:488
  23.7 46.4 %collective-permute-start = (bf16[128,2176]{1,0:T(8,128)(2,1)}, bf16[128,2176]{1,0:T(8,128)(2,1)S(1)}, u32[]{:S(2)}, u32[]{:S(2)}) collective-permute-start(bf16[128,2176]{1,0:T(8,128)(2,1)} %get-tuple-element.28.refs_2_.refs_6_), channel_id=1, source_target_pairs={{0,16},{16,4},{4,20},{20,0},{1,17},{17,5},{5,21},{21,1},{2,18},{18... | collective-permute-start | bytes 1671176 | tf_op jit(solution)/shard_map/ppermute | solution.py:488
  58.8 11.3 %copy-start.3 = (bf16[128,2176]{1,0:T(8,128)(2,1)}, bf16[128,2176]{1,0:T(8,128)(2,1)S(1)}, u32[]{:S(2)}) copy-start(bf16[128,2176]{1,0:T(8,128)(2,1)S(1)} %collective-permute-done.2.refs_5_.refs_9_) | copy-start | bytes 1671172
  58.8 11.3 %copy-start.4 = (bf16[128,2176]{1,0:T(8,128)(2,1)}, bf16[128,2176]{1,0:T(8,128)(2,1)S(1)}, u32[]{:S(2)}) copy-start(bf16[128,2176]{1,0:T(8,128)(2,1)S(1)} %collective-permute-done.1.refs_4_.refs_8_) | copy-start | bytes 1671172
  70.1 0.8 copy-start.5
  70.9 1.4 copy-start
  81.7 11.2 %copy-start.11 = (bf16[112,2048]{1,0:T(8,128)(2,1)S(1)}, bf16[112,2048]{1,0:T(8,128)(2,1)}, u32[]{:S(2)}) copy-start(bf16[112,2048]{1,0:T(8,128)(2,1)} %get-tuple-element.34) | copy-start | bytes 1376260
  81.7 12.2 %copy-start.9 = (bf16[112,2048]{1,0:T(8,128)(2,1)S(1)}, bf16[112,2048]{1,0:T(8,128)(2,1)}, u32[]{:S(2)}) copy-start(bf16[112,2048]{1,0:T(8,128)(2,1)} %get-tuple-element.35) | copy-start | bytes 1376260
  81.7 19.9 %copy-start.7 = (bf16[112,2048]{1,0:T(8,128)(2,1)S(1)}, bf16[112,2048]{1,0:T(8,128)(2,1)}, u32[]{:S(2)}) copy-start(bf16[112,2048]{1,0:T(8,128)(2,1)} %get-tuple-element.36) | copy-start | bytes 1376260
  81.7 32.4 %copy-start.6 = (bf16[112,2048]{1,0:T(8,128)(2,1)S(1)}, bf16[112,2048]{1,0:T(8,128)(2,1)}, u32[]{:S(2)}) copy-start(bf16[112,2048]{1,0:T(8,128)(2,1)} %get-tuple-element.37) | copy-start | bytes 1376260
  81.8 51.4 %all-to-all-start.1 = ((bf16[8,112,2048]{2,1,0:T(8,128)(2,1)}), bf16[8,112,2048]{2,1,0:T(8,128)(2,1)}, u32[]{:S(2)}, u32[]{:S(2)}) async-start(bf16[8,112,2048]{2,1,0:T(8,128)(2,1)} %bitcast.10), calls=%async_computation.1 | async-start | bytes 7340032 | tf_op jit(solution)/shard_map/all_to_all | solution.py:495
  88.0 120.1 %reduce-scatter.5.cloned.1.call-start = ((), (), s32[]{:S(2)}) async-start(), calls=%async_computation.8 | async-start | bytes 5570560 | tf_op jit(solution)/shard_map/reduce_scatter | solution.py:504
  88.0 13.6 %collective-permute-start.4 = (bf16[112,2048]{1,0:T(8,128)(2,1)}, bf16[112,2048]{1,0:T(8,128)(2,1)S(1)}, u32[]{:S(2)}, u32[]{:S(2)}) collective-permute-start(bf16[112,2048]{1,0:T(8,128)(2,1)} %get-tuple-element.31), channel_id=1, source_target_pairs={{0,32},{8,40},{32,64},{40,72},{64,96},{72,104},{96,0},{104,8},{1,3... | collective-permute-start | bytes 1376264 | tf_op jit(solution)/shard_map/ppermute | solution.py:499
  89.4 24.8 %collective-permute-start.5 = (bf16[112,2048]{1,0:T(8,128)(2,1)}, bf16[112,2048]{1,0:T(8,128)(2,1)S(1)}, u32[]{:S(2)}, u32[]{:S(2)}) collective-permute-start(bf16[112,2048]{1,0:T(8,128)(2,1)} %get-tuple-element.32), channel_id=1, source_target_pairs={{0,64},{8,72},{32,96},{40,104},{64,0},{72,8},{96,32},{104,40},{1,6... | collective-permute-start | bytes 1376264 | tf_op jit(solution)/shard_map/ppermute | solution.py:499
  91.8 22.7 %collective-permute-start.6 = (bf16[112,2048]{1,0:T(8,128)(2,1)}, bf16[112,2048]{1,0:T(8,128)(2,1)S(1)}, u32[]{:S(2)}, u32[]{:S(2)}) collective-permute-start(bf16[112,2048]{1,0:T(8,128)(2,1)} %get-tuple-element.33), channel_id=1, source_target_pairs={{0,96},{8,104},{32,0},{40,8},{64,32},{72,40},{96,64},{104,72},{1,9... | collective-permute-start | bytes 1376264 | tf_op jit(solution)/shard_map/ppermute | solution.py:499
  93.0 21.5 %collective-permute-start.7 = (bf16[112,2048]{1,0:T(8,128)(2,1)S(1)}, bf16[112,2048]{1,0:T(8,128)(2,1)S(1)}, u32[]{:S(2)}, u32[]{:S(2)}) collective-permute-start(bf16[112,2048]{1,0:T(8,128)(2,1)S(1)} %copy-done.11), channel_id=1, source_target_pairs={{0,8},{8,0},{32,40},{40,32},{64,72},{72,64},{96,104},{104,96},{1,9... | collective-permute-start | bytes 1376264 | tf_op jit(solution)/shard_map/ppermute | solution.py:499
  93.9 27.8 %collective-permute-start.8 = (bf16[112,2048]{1,0:T(8,128)(2,1)S(1)}, bf16[112,2048]{1,0:T(8,128)(2,1)S(1)}, u32[]{:S(2)}, u32[]{:S(2)}) collective-permute-start(bf16[112,2048]{1,0:T(8,128)(2,1)S(1)} %copy-done.9), channel_id=1, source_target_pairs={{0,40},{8,32},{32,72},{40,64},{64,104},{72,96},{96,8},{104,0},{1,4... | collective-permute-start | bytes 1376264 | tf_op jit(solution)/shard_map/ppermute | solution.py:499
  101.6 33.1 %copy-start.8 = (bf16[112,2048]{1,0:T(8,128)(2,1)}, bf16[112,2048]{1,0:T(8,128)(2,1)S(1)}, u32[]{:S(2)}) copy-start(bf16[112,2048]{1,0:T(8,128)(2,1)S(1)} %collective-permute-done.4.refs_1_) | copy-start | bytes 1376260
  101.6 30.8 %collective-permute-start.9 = (bf16[112,2048]{1,0:T(8,128)(2,1)S(1)}, bf16[112,2048]{1,0:T(8,128)(2,1)S(1)}, u32[]{:S(2)}, u32[]{:S(2)}) collective-permute-start(bf16[112,2048]{1,0:T(8,128)(2,1)S(1)} %copy-done.7), channel_id=1, source_target_pairs={{0,72},{8,64},{32,104},{40,96},{64,8},{72,0},{96,40},{104,32},{1,7... | collective-permute-start | bytes 1376264 | tf_op jit(solution)/shard_map/ppermute | solution.py:499
  114.2 20.5 %copy-start.10 = (bf16[112,2048]{1,0:T(8,128)(2,1)}, bf16[112,2048]{1,0:T(8,128)(2,1)S(1)}, u32[]{:S(2)}) copy-start(bf16[112,2048]{1,0:T(8,128)(2,1)S(1)} %collective-permute-done.5.refs_2_) | copy-start | bytes 1376260
  114.2 18.9 %collective-permute-start.10 = (bf16[112,2048]{1,0:T(8,128)(2,1)S(1)}, bf16[112,2048]{1,0:T(8,128)(2,1)}, u32[]{:S(2)}, u32[]{:S(2)}) collective-permute-start(bf16[112,2048]{1,0:T(8,128)(2,1)S(1)} %copy-done.6), channel_id=1, source_target_pairs={{0,104},{8,96},{32,8},{40,0},{64,40},{72,32},{96,72},{104,64},{1,1... | collective-permute-start | bytes 1376264 | tf_op jit(solution)/shard_map/ppermute | solution.py:499
  114.5 20.3 %copy-start.12 = (bf16[112,2048]{1,0:T(8,128)(2,1)}, bf16[112,2048]{1,0:T(8,128)(2,1)S(1)}, u32[]{:S(2)}) copy-start(bf16[112,2048]{1,0:T(8,128)(2,1)S(1)} %collective-permute-done.6.refs_3_) | copy-start | bytes 1376260
  114.5 17.9 %copy-start.13 = (bf16[112,2048]{1,0:T(8,128)(2,1)}, bf16[112,2048]{1,0:T(8,128)(2,1)S(1)}, u32[]{:S(2)}) copy-start(bf16[112,2048]{1,0:T(8,128)(2,1)S(1)} %collective-permute-done.7.refs_4_) | copy-start | bytes 1376260
  121.7 10.6 %copy-start.14 = (bf16[112,2048]{1,0:T(8,128)(2,1)}, bf16[112,2048]{1,0:T(8,128)(2,1)S(1)}, u32[]{:S(2)}) copy-start(bf16[112,2048]{1,0:T(8,128)(2,1)S(1)} %collective-permute-done.8.refs_5_) | copy-start | bytes 1376260
  132.4 0.8 copy-start.15
  170.4 66.1 %all-to-all-start.2 = ((bf16[32,28,2176]{2,1,0:T(8,128)(2,1)}), bf16[32,28,2176]{2,1,0:T(8,128)(2,1)}, u32[]{:S(2)}, u32[]{:S(2)}) async-start(bf16[32,28,2176]{2,1,0:T(8,128)(2,1)} %shard_map.96), calls=%async_computation.2 | async-start | bytes 8912896 | tf_op jit(solution)/shard_map/all_to_all | solution.py:508
  178.1 80.9 %reduce-scatter.3.cloned.1.call-start = ((), (), s32[]{:S(2)}) async-start(), calls=%async_computation.7 | async-start | bytes 5570560 | tf_op jit(solution)/shard_map/reduce_scatter | solution.py:504
  208.0 52.5 %collective-permute-start.11 = (bf16[256,2176]{1,0:T(8,128)(2,1)}, bf16[256,2176]{1,0:T(8,128)(2,1)S(1)}, u32[]{:S(2)}, u32[]{:S(2)}) collective-permute-start(bf16[256,2176]{1,0:T(8,128)(2,1)} %reduce-scatter.5.cloned.1.call-done), channel_id=1, source_target_pairs={{0,4},{4,0},{1,5},{5,1},{2,6},{6,2},{3,7},{7,3},{8,12},{12,8},{9,1... | collective-permute-start | bytes 3342344 | tf_op jit(solution)/shard_map/ppermute | solution.py:505
  260.5 1.0 copy-start.1
Sparse Core Ops, SparseCore 0:
  12.5 53.6 all-gather.2
  81.8 52.8 all-gather.4
  158.6 49.3 reduce-scatter.4
  210.3 48.6 reduce-scatter.2

commit v3 on v2

--- a/solution.py
+++ b/solution.py
@@ -23,7 +23,7 @@
 
 
 def params():
-    return pltpu.CompilerParams(vmem_limit_bytes=60 * MIB)
+    return pltpu.CompilerParams(vmem_limit_bytes=63 * MIB)
 
 
 def mm(a, b, ca=1, cb=0):
@@ -101,8 +101,7 @@
 
 def pick_kernel(sc, *refs):
     x_tab, x_meta, c_tabs, c_metas = refs[0], refs[1], refs[2:6], refs[6:10]
-    shard, x_out, shard_out = refs[10:13]
-    c_outs, x_sel, c_sel = refs[13:21], refs[21], refs[22]
+    x_out, c_outs, x_sel, c_sel = refs[10], refs[11:19], refs[19], refs[20]
     y, z_lo, core, z_hi = sc[0], sc[1], sc[2], sc[3]
     z = z_hi * 2 + z_lo
 
@@ -121,17 +120,15 @@
         bases = [(((z - d) & 3) * CAP).astype(F32) for d in range(4)]
         pick_matrix(c_metas, experts.astype(F32), bases, True, c_sel)
 
-    shard_out[...] = shard[...]
     x_out[...] = mm(x_sel[...], x_tab[...].reshape(4 * TOK, -1)).astype(BF)
     rows = mm(c_sel[...], jnp.concatenate([t[...] for t in c_tabs], axis=0)).astype(BF)
     for j in range(8):
         c_outs[j][...] = rows[j * BLK : (j + 1) * BLK, :]
 
 
-def pick(sc, toks, cots, shard):
+def pick(sc, toks, cots):
     step = 512
     column = lambda n, sc: (0, n)
-    line = lambda n, sc: (n, 0)
     tables = [
         pl.BlockSpec((4, TOK, step), lambda n, sc: (0, 0, n)),
         pl.BlockSpec((4, TOK, 128), lambda n, sc: (0, 0, D // 128)),
@@ -143,23 +140,21 @@
         grid_spec=pltpu.PrefetchScalarGridSpec(
             num_scalar_prefetch=1,
             grid=(D // step,),
-            in_specs=tables + [pl.BlockSpec((64, PACK), line)],
+            in_specs=tables,
             out_specs=[
                 pl.BlockSpec((ROWS, step), column),
-                pl.BlockSpec((64, PACK), line),
             ]
             + [pl.BlockSpec((BLK, step), column)] * 8,
             scratch_shapes=[pltpu.VMEM((ROWS, 4 * TOK), BF)] * 2,
         ),
         out_shape=[
             jax.ShapeDtypeStruct((ROWS, D), BF),
-            jax.ShapeDtypeStruct((256, PACK), BF),
         ]
         + [jax.ShapeDtypeStruct((BLK, D), BF)] * 8,
         compiler_params=params(),
         cost_estimate=cost(4 * ROWS * 512 * D, 16 * MIB),
-    )(sc, toks, toks, *cots, *cots, shard)
-    return outs[0], outs[1], outs[2:]
+    )(sc, toks, toks, *cots, *cots)
+    return outs[0], outs[1:]
 
 
 def expert_kernel(sc, *refs):
@@ -385,6 +380,22 @@
         compiler_params=params(),
         cost_estimate=cost(2 * ROWS * 1024 * 3 * F, 12 * MIB),
     )(sc, x_rows, scaled, d_both, hidden)
+
+
+def hold_kernel(value, *rest):
+    pass
+
+
+def hold(value, *after):
+    anywhere = pl.BlockSpec(memory_space=pl.ANY)
+    return pl.pallas_call(
+        hold_kernel,
+        in_specs=[anywhere] * (1 + len(after)),
+        out_specs=anywhere,
+        out_shape=jax.ShapeDtypeStruct(value.shape, value.dtype),
+        input_output_aliases={0: 0},
+        compiler_params=params(),
+    )(value, *after)
 
 
 def final_kernel(back, routes, probs, out, out_probs, sel, rows):
@@ -489,7 +500,8 @@
     toks = lax.all_to_all(tok, "y", split_axis=0, concat_axis=0, tiled=True)
     swap = [(0, 1), (1, 0)]
     gather = lambda w: lax.all_gather(w, "x", axis=0, tiled=True)
-    x_send, oth, sent = pick(sc, toks, cots, lax.ppermute(oth, "zh", swap))
+    oth = hold(lax.ppermute(oth, "zh", swap), toks, *cots[1:])
+    x_send, sent = pick(sc, toks, cots)
     w_own, w_oth = gather(own), gather(oth)
 
     x_rows = lax.all_to_all(

time: 272 us -> 265 us (0.974)
  local copies, waits for them, and re-layouts: 4.71 us -> 1.43 us
    unnamed x32 -> x24, local copies, waits for them, and re-layouts: 4.09 us -> 0.8 us
  transfers between devices with their start and end apart: 19 -> 19, of which waited for: 10 -> 9; matrix products, arithmetic and copies ran while one was open for 0% -> 0% of each run, Pallas kernels for 13% -> 13%
where the time goes in v3:
time: 265 us; the launch traced here: 264 us
  waiting for transfers between devices  137 us (52%)
  Pallas kernels  65.9 us (25%)
  starting transfers between devices  45.8 us (17%)
  between operations  14 us (5%)
    ppermute x3, waiting for transfers between devices, body(): lax.ppermute(cot, ('zl', 'zh'), along_z(k))  46.5 us
    reduce_scatter x2, waiting for transfers between devices, body(): lax.psum_scatter(g, 'x', scatter_dimension=0, tiled=True)  40 us
    ppermute x7, waiting for transfers between devices, body(): lax.ppermute(sent[j], ('y', 'c'), along_yc(j % 4, j // 4))  25.3 us
    all_to_all x1, waiting for transfers between devices, body(): lax.all_to_all(dx, ('y', 'zl', 'c', 'zh'), split_axis=0, concat_axis=0, t...  24.6 us
    pallas_call x1, Pallas kernels, expert_pass(): pl.pallas_call(expert_kernel, in_specs=[pl.BlockSpec(memory_space=pltpu.S...  23.8 us
    ppermute x7, starting transfers between devices, body(): lax.ppermute(sent[j], ('y', 'c'), along_yc(j % 4, j // 4))  19.1 us
    pallas_call x1, Pallas kernels, input_grads(): pl.pallas_call(inputs_kernel, in_specs=[pl.BlockSpec(memory_space=pltpu.S...  11.8 us
    pallas_call x1, Pallas kernels, own_grads(): pl.pallas_call(grads_kernel, in_specs=[pl.BlockSpec(memory_space=pltpu.SM...  10.1 us
  transfers between devices with their start and end apart: 19, of which 9 were waited for; matrix products, arithmetic and copies ran while one was open for 0% of the time, Pallas kernels for 13%

profile of v3, /device:TPU:1, one launch (start us, length us, event | category | flops | bytes accessed | tf_op | source)
XLA Modules:
  0.0 264.4 jit_solution(6757278747107470757)
XLA Ops:
  7.2 0.0 all-gather.3.cloned.1.call-start
  7.2 0.6 stack.23.sc
  7.8 4.5 %shard_map.93 = (bf16[4,128,2176]{2,1,0:T(8,128)(2,1)}, bf16[128,2176]{1,0:T(8,128)(2,1)}, bf16[256,2176]{1,0:T(8,128)(2,1)}, bf16[256,2176]{1,0:T(8,128)(2,1)}) custom-call(s32[5]{0:T(128)} %stack.23.sc, bf16[128,2048]{1,0:T(8,128)(2,1)} %tok.1, bf16[128,2048]{1,0:T(8,128)(2,1)} %cot.1, s32[6,128]{1,0:T(8,128)} %bitcast.11, f32[6,128]{1,0:T(8,128)} %bitcast.13, ...), custom_call_target="tpu_custom_call" | custom-call | bytes 8388608 | tf_op jit(solution)/shard_map/pallas_call | solution.py:66
  12.3 0.0 all-gather.3.cloned.1.call-update
  12.3 0.0 copy-start.1
  12.4 0.0 copy-start.2
  12.4 5.2 %all-to-all-start = ((bf16[4,128,2176]{2,1,0:T(8,128)(2,1)}), bf16[4,128,2176]{2,1,0:T(8,128)(2,1)}, u32[]{:S(2)}, u32[]{:S(2)}) async-start(bf16[4,128,2176]{2,1,0:T(8,128)(2,1)} %get-tuple-element.26), calls=%async_computation | async-start | bytes 4456448 | tf_op jit(solution)/shard_map/all_to_all | solution.py:500
  17.5 0.0 all-gather.5.cloned.1.call-start
  17.5 0.0 copy-done.1
  17.5 4.1 %collective-permute-start.10 = (bf16[256,2176]{1,0:T(8,128)(2,1)S(1)}, bf16[256,2176]{1,0:T(8,128)(2,1)}, u32[]{:S(2)}, u32[]{:S(2)}) collective-permute-start(bf16[256,2176]{1,0:T(8,128)(2,1)S(1)} %copy-done.1), channel_id=1, source_target_pairs={{0,4},{4,0},{1,5},{5,1},{2,6},{6,2},{3,7},{7,3},{8,12},{12,8},{9,1... | collective-permute-start | bytes 3342344 | tf_op jit(solution)/shard_map/ppermute | solution.py:503
  21.6 0.0 copy-done.2
  21.6 0.4 collective-permute-start.2
  22.0 2.1 collective-permute-start.1
  24.1 0.0 collective-permute-start
  24.1 34.5 %collective-permute-done.2.refs_5_.refs_9_.rest_3_ = bf16[128,2176]{1,0:T(8,128)(2,1)S(1)} collective-permute-done((bf16[128,2176]{1,0:T(8,128)(2,1)S(1)}, bf16[128,2176]{1,0:T(8,128)(2,1)S(1)}, u32[]{:S(2)}, u32[]{:S(2)}) %collective-permute-start.2) | collective-permute-done | bytes 557088 | tf_op jit(solution)/shard_map/ppermute | solution.py:499
  58.6 0.0 collective-permute-done.1.refs_4_.refs_8_.rest_2_
  58.6 11.9 %collective-permute-done.refs_3_.refs_7_.rest_1_ = bf16[128,2176]{1,0:T(8,128)(2,1)} collective-permute-done((bf16[128,2176]{1,0:T(8,128)(2,1)S(1)}, bf16[128,2176]{1,0:T(8,128)(2,1)}, u32[]{:S(2)}, u32[]{:S(2)}) %collective-permute-start) | collective-permute-done | bytes 557088 | tf_op jit(solution)/shard_map/ppermute | solution.py:499
  70.6 0.0 collective-permute-done.10.value
  70.6 0.0 all-to-all-done.refs_0_.refs_1_.rest_0_
  70.6 0.0 copy-done
  70.6 0.0 all-gather.5.cloned.1.call-update
  70.6 8.7 %shard_map.94 = (bf16[896,2048]{1,0:T(8,128)(2,1)}, bf16[112,2048]{1,0:T(8,128)(2,1)}, bf16[112,2048]{1,0:T(8,128)(2,1)}, bf16[112,2048]{1,0:T(8,128)(2,1)}, bf1...) custom-call(s32[5]{0:T(128)} %stack.23.sc, ...), custom_call_target="tpu_custom_call" | custom-call | flops 3758096384 | bytes 16777216 | tf_op jit(solution)/shard_map/pallas_call | solution.py:138
  79.3 0.0 copy-start.9
  79.3 0.0 copy-start.7
  79.4 0.0 copy-start.5
  79.4 5.4 %all-to-all-start.1 = ((bf16[8,112,2048]{2,1,0:T(8,128)(2,1)}), bf16[8,112,2048]{2,1,0:T(8,128)(2,1)}, u32[]{:S(2)}, u32[]{:S(2)}) async-start(bf16[8,112,2048]{2,1,0:T(8,128)(2,1)} %bitcast.10), calls=%async_computation.1 | async-start | bytes 7340032 | tf_op jit(solution)/shard_map/all_to_all | solution.py:507
  84.7 0.0 reduce-scatter.5.cloned.1.call-start
  84.7 1.3 collective-permute-start.3
  86.1 2.6 collective-permute-start.4
  88.7 1.1 collective-permute-start.5
  89.7 0.9 collective-permute-start.6
  90.6 0.0 copy-done.9
  90.6 0.3 collective-permute-start.7
  90.9 7.4 %collective-permute-done.3.refs_1_ = bf16[112,2048]{1,0:T(8,128)(2,1)S(1)} collective-permute-done((bf16[112,2048]{1,0:T(8,128)(2,1)}, bf16[112,2048]{1,0:T(8,128)(2,1)S(1)}, u32[]{:S(2)}, u32[]{:S(2)}) %collective-permute-start.3) | collective-permute-done | bytes 458784 | tf_op jit(solution)/shard_map/ppermute | solution.py:511
  98.4 0.0 copy-done.7
  98.4 12.6 %collective-permute-start.8 = (bf16[112,2048]{1,0:T(8,128)(2,1)S(1)}, bf16[112,2048]{1,0:T(8,128)(2,1)S(1)}, u32[]{:S(2)}, u32[]{:S(2)}) collective-permute-start(bf16[112,2048]{1,0:T(8,128)(2,1)S(1)} %copy-done.7), channel_id=1, source_target_pairs={{0,72},{8,64},{32,104},{40,96},{64,8},{72,0},{96,40},{104,32},{1,7... | collective-permute-start | bytes 1376264 | tf_op jit(solution)/shard_map/ppermute | solution.py:511
  111.0 0.0 collective-permute-done.4.refs_2_
  111.0 0.0 copy-done.5
  111.0 0.3 collective-permute-start.9
  111.3 0.0 collective-permute-done.5.refs_3_
  111.3 0.0 copy-start.6
  111.3 0.0 collective-permute-done.6.refs_4_
  111.3 0.0 copy-start.8
  111.3 7.2 %collective-permute-done.7.refs_5_ = bf16[112,2048]{1,0:T(8,128)(2,1)S(1)} collective-permute-done((bf16[112,2048]{1,0:T(8,128)(2,1)S(1)}, bf16[112,2048]{1,0:T(8,128)(2,1)S(1)}, u32[]{:S(2)}, u32[]{:S(2)}) %collective-permute-start.7) | collective-permute-done | bytes 458784 | tf_op jit(solution)/shard_map/ppermute | solution.py:511
  118.5 10.7 %collective-permute-done.8.refs_6_ = bf16[112,2048]{1,0:T(8,128)(2,1)S(1)} collective-permute-done((bf16[112,2048]{1,0:T(8,128)(2,1)S(1)}, bf16[112,2048]{1,0:T(8,128)(2,1)S(1)}, u32[]{:S(2)}, u32[]{:S(2)}) %collective-permute-start.8) | collective-permute-done | bytes 458784 | tf_op jit(solution)/shard_map/ppermute | solution.py:511
  129.2 0.8 copy-done.11
  129.9 0.0 collective-permute-done.9.refs_7_
  130.0 0.0 all-to-all-done.1
  130.0 0.0 all-gather.3.cloned.1.call-done.refs_9_.w_own
  130.0 0.0 all-gather.5.cloned.1.call-done.refs_10_.w_oth
  130.0 23.8 %shard_map.96 = (bf16[896,2048]{1,0:T(8,128)(2,1)}, bf16[896,1408]{1,0:T(8,128)(2,1)}, bf16[896,704]{1,0:T(8,128)(2,1)}, bf16[896,128]{1,0:T(8,128)(2,1)}, bf16[1024,2176]{1,0:T(8,128)(2,1)}) custom-call(s32[5]{0:T(128)} %stack.23.sc, bf16[112,2048]{1,0:T(8,128)(2,1)} %get-tuple-element.28.refs_0_, bf16[112,2048]{1,0:T(8,128)(2,1)} %copy-done.3, ...), custom_call_target="tpu_custom_call" | custom-call | flops 15502147584 | bytes 33554432 | tf_op jit(solution)/shard_map/pallas_call | solution.py:275
  153.9 0.0 reduce-scatter.5.cloned.1.call-update
  153.9 11.8 %shard_map.97 = bf16[32,28,2176]{2,1,0:T(8,128)(2,1)} custom-call(s32[5]{0:T(128)} %stack.23.sc, bf16[896,1408]{1,0:T(8,128)(2,1)} %get-tuple-element.39.d_both_in, bf16[896,128]{1,0:T(8,128)(2,1)} %get-tuple-element.40.q, bf16[1024,2176]{1,0:T(8,128)(2,1)} %all-gather.3.cloned.1.call-done.refs_9_.w_own, ...), custom_call_target="tpu_custom_call" | custom-call | flops 5167382528 | bytes 16777216 | tf_op jit(solution)/shard_map/pallas_call | solution.py:324
  165.7 6.7 %all-to-all-start.2 = ((bf16[32,28,2176]{2,1,0:T(8,128)(2,1)}), bf16[32,28,2176]{2,1,0:T(8,128)(2,1)}, u32[]{:S(2)}, u32[]{:S(2)}) async-start(bf16[32,28,2176]{2,1,0:T(8,128)(2,1)} %shard_map.97), calls=%async_computation.2 | async-start | bytes 8912896 | tf_op jit(solution)/shard_map/all_to_all | solution.py:520
  172.4 0.0 reduce-scatter.3.cloned.1.call-start
  172.5 10.1 %shard_map.99 = bf16[1024,2176]{1,0:T(8,128)(2,1)} custom-call(s32[5]{0:T(128)} %stack.23.sc, bf16[896,2048]{1,0:T(8,128)(2,1)} %bitcast.8.refs_8_.x_in, bf16[896,2048]{1,0:T(8,128)(2,1)} %get-tuple-element.43.scaled_in, bf16[896,1408]{1,0:T(8,128)(2,1)} %get-tuple-element.39.d_both_in, bf16[896,704]{1,0:T(8,128)(2,1)} %get-tuple-element.44.hidden_in), custom_call_target="tpu_custom_call" | custom-call | flops 3875536896 | bytes 12582912 | tf_op jit(solution)/shard_map/pallas_call | solution.py:373
  182.6 0.0 reduce-scatter.3.cloned.1.call-update
  182.6 20.6 %reduce-scatter.5.cloned.1.call-done = bf16[256,2176]{1,0:T(8,128)(2,1)} async-done(((bf16[1024,2176]{1,0:T(8,128)(2,1)}), bf16[256,2176]{1,0:T(8,128)(2,1)}) %reduce-scatter.5.cloned.1.call-update) | async-done | bytes 1114128 | tf_op jit(solution)/shard_map/reduce_scatter | solution.py:516
  203.2 2.9 %collective-permute-start.11 = (bf16[256,2176]{1,0:T(8,128)(2,1)}, bf16[256,2176]{1,0:T(8,128)(2,1)}, u32[]{:S(2)}, u32[]{:S(2)}) collective-permute-start(bf16[256,2176]{1,0:T(8,128)(2,1)} %reduce-scatter.5.cloned.1.call-done), channel_id=1, source_target_pairs={{0,4},{4,0},{1,5},{5,1},{2,6},{6,2},{3,7},{7,3},{8,12},{12,8},{9,1... | collective-permute-start | bytes 3342344 | tf_op jit(solution)/shard_map/ppermute | solution.py:517
  206.1 24.6 %all-to-all-done.2.back = bf16[32,28,2176]{2,1,0:T(8,128)(2,1)} async-done(((bf16[32,28,2176]{2,1,0:T(8,128)(2,1)}), bf16[32,28,2176]{2,1,0:T(8,128)(2,1)}, u32[]{:S(2)}, u32[]{:S(2)}) %all-to-all-start.2) | async-done | bytes 3899424 | tf_op jit(solution)/shard_map/all_to_all | solution.py:520
  230.7 4.0 %shard_map.98 = (bf16[128,2048]{1,0:T(8,128)(2,1)}, f32[6,128]{1,0:T(8,128)}) custom-call(bf16[32,28,2176]{2,1,0:T(8,128)(2,1)} %all-to-all-done.2.back, s32[6,128]{1,0:T(8,128)} %bitcast.12, f32[6,128]{1,0:T(8,128)} %bitcast.14), custom_call_target="tpu_custom_call" | custom-call | flops 99999997952 | bytes 8388608 | tf_op jit(solution)/shard_map/pallas_call | solution.py:431
  234.7 19.5 %reduce-scatter.3.cloned.1.call-done.own = bf16[256,2176]{1,0:T(8,128)(2,1)} async-done(((bf16[1024,2176]{1,0:T(8,128)(2,1)}), bf16[256,2176]{1,0:T(8,128)(2,1)}) %reduce-scatter.3.cloned.1.call-update) | async-done | bytes 1114128 | tf_op jit(solution)/shard_map/reduce_scatter | solution.py:516
  254.2 0.7 collective-permute-done.11.oth
  254.9 3.0 %shard_map.100 = (bf16[2,256,1408]{2,1,0:T(8,128)(2,1)}, bf16[2,704,256]{2,1,0:T(8,128)(2,1)}) custom-call(s32[5]{0:T(128)} %stack.23.sc, bf16[256,2176]{1,0:T(8,128)(2,1)} %reduce-scatter.3.cloned.1.call-done.own, bf16[256,2176]{1,0:T(8,128)(2,1)} %collective-permute-done.11.oth), custom_call_target="tpu_custom_call" | custom-call | bytes 5242880 | tf_op jit(solution)/shard_map/pallas_call | solution.py:463
  (11 shorter events, 0.0 us)
Async XLA Ops:
  7.2 122.8 %all-gather.3.cloned.1.call-start = ((), (), s32[]{:S(2)}) async-start(), calls=%async_computation.5 | async-start | bytes 5570560 | tf_op jit(solution)/shard_map/all_gather | solution.py:502
  12.3 5.2 %copy-start.1 = (bf16[256,2176]{1,0:T(8,128)(2,1)S(1)}, bf16[256,2176]{1,0:T(8,128)(2,1)}, u32[]{:S(2)}) copy-start(bf16[256,2176]{1,0:T(8,128)(2,1)} %get-tuple-element.38) | copy-start | bytes 3342340
  12.4 9.2 %copy-start.2 = (bf16[128,2176]{1,0:T(8,128)(2,1)S(1)}, bf16[128,2176]{1,0:T(8,128)(2,1)}, u32[]{:S(2)}) copy-start(bf16[128,2176]{1,0:T(8,128)(2,1)} %get-tuple-element.27.refs_2_.refs_6_) | copy-start | bytes 1671172
  12.4 58.2 %all-to-all-start = ((bf16[4,128,2176]{2,1,0:T(8,128)(2,1)}), bf16[4,128,2176]{2,1,0:T(8,128)(2,1)}, u32[]{:S(2)}, u32[]{:S(2)}) async-start(bf16[4,128,2176]{2,1,0:T(8,128)(2,1)} %get-tuple-element.26), calls=%async_computation | async-start | bytes 4456448 | tf_op jit(solution)/shard_map/all_to_all | solution.py:500
  17.5 112.5 %all-gather.5.cloned.1.call-start = ((), (), s32[]{:S(2)}) async-start(), calls=%async_computation.6 | async-start | bytes 5570560 | tf_op jit(solution)/shard_map/all_gather | solution.py:502
  17.5 53.1 %collective-permute-start.10 = (bf16[256,2176]{1,0:T(8,128)(2,1)S(1)}, bf16[256,2176]{1,0:T(8,128)(2,1)}, u32[]{:S(2)}, u32[]{:S(2)}) collective-permute-start(bf16[256,2176]{1,0:T(8,128)(2,1)S(1)} %copy-done.1), channel_id=1, source_target_pairs={{0,4},{4,0},{1,5},{5,1},{2,6},{6,2},{3,7},{7,3},{8,12},{12,8},{9,1... | collective-permute-start | bytes 3342344 | tf_op jit(solution)/shard_map/ppermute | solution.py:503
  21.6 37.1 %collective-permute-start.2 = (bf16[128,2176]{1,0:T(8,128)(2,1)S(1)}, bf16[128,2176]{1,0:T(8,128)(2,1)S(1)}, u32[]{:S(2)}, u32[]{:S(2)}) collective-permute-start(bf16[128,2176]{1,0:T(8,128)(2,1)S(1)} %copy-done.2), channel_id=1, source_target_pairs={{0,20},{16,0},{4,16},{20,4},{1,21},{17,1},{5,17},{21,5},{2,22},{18... | collective-permute-start | bytes 1671176 | tf_op jit(solution)/shard_map/ppermute | solution.py:499
  22.0 36.6 %collective-permute-start.1 = (bf16[128,2176]{1,0:T(8,128)(2,1)S(1)}, bf16[128,2176]{1,0:T(8,128)(2,1)}, u32[]{:S(2)}, u32[]{:S(2)}) collective-permute-start(bf16[128,2176]{1,0:T(8,128)(2,1)S(1)} %copy-done.2), channel_id=1, source_target_pairs={{0,4},{16,20},{4,0},{20,16},{1,5},{17,21},{5,1},{21,17},{2,6},{18,... | collective-permute-start | bytes 1671176 | tf_op jit(solution)/shard_map/ppermute | solution.py:499
  24.1 46.5 %collective-permute-start = (bf16[128,2176]{1,0:T(8,128)(2,1)S(1)}, bf16[128,2176]{1,0:T(8,128)(2,1)}, u32[]{:S(2)}, u32[]{:S(2)}) collective-permute-start(bf16[128,2176]{1,0:T(8,128)(2,1)S(1)} %copy-done.2), channel_id=1, source_target_pairs={{0,16},{16,4},{4,20},{20,0},{1,17},{17,5},{5,21},{21,1},{2,18},{18... | collective-permute-start | bytes 1671176 | tf_op jit(solution)/shard_map/ppermute | solution.py:499
  58.6 12.0 %copy-start = (bf16[128,2176]{1,0:T(8,128)(2,1)}, bf16[128,2176]{1,0:T(8,128)(2,1)S(1)}, u32[]{:S(2)}) copy-start(bf16[128,2176]{1,0:T(8,128)(2,1)S(1)} %collective-permute-done.2.refs_5_.refs_9_.rest_3_) | copy-start | bytes 1671172
  79.3 11.3 %copy-start.9 = (bf16[112,2048]{1,0:T(8,128)(2,1)S(1)}, bf16[112,2048]{1,0:T(8,128)(2,1)}, u32[]{:S(2)}) copy-start(bf16[112,2048]{1,0:T(8,128)(2,1)} %get-tuple-element.33) | copy-start | bytes 1376260
  79.3 19.0 %copy-start.7 = (bf16[112,2048]{1,0:T(8,128)(2,1)S(1)}, bf16[112,2048]{1,0:T(8,128)(2,1)}, u32[]{:S(2)}) copy-start(bf16[112,2048]{1,0:T(8,128)(2,1)} %get-tuple-element.34) | copy-start | bytes 1376260
  79.4 31.6 %copy-start.5 = (bf16[112,2048]{1,0:T(8,128)(2,1)S(1)}, bf16[112,2048]{1,0:T(8,128)(2,1)}, u32[]{:S(2)}) copy-start(bf16[112,2048]{1,0:T(8,128)(2,1)} %get-tuple-element.35) | copy-start | bytes 1376260
  79.4 50.6 %all-to-all-start.1 = ((bf16[8,112,2048]{2,1,0:T(8,128)(2,1)}), bf16[8,112,2048]{2,1,0:T(8,128)(2,1)}, u32[]{:S(2)}, u32[]{:S(2)}) async-start(bf16[8,112,2048]{2,1,0:T(8,128)(2,1)} %bitcast.10), calls=%async_computation.1 | async-start | bytes 7340032 | tf_op jit(solution)/shard_map/all_to_all | solution.py:507
  84.7 118.5 %reduce-scatter.5.cloned.1.call-start = ((), (), s32[]{:S(2)}) async-start(), calls=%async_computation.8 | async-start | bytes 5570560 | tf_op jit(solution)/shard_map/reduce_scatter | solution.py:516
  84.7 13.6 %collective-permute-start.3 = (bf16[112,2048]{1,0:T(8,128)(2,1)}, bf16[112,2048]{1,0:T(8,128)(2,1)S(1)}, u32[]{:S(2)}, u32[]{:S(2)}) collective-permute-start(bf16[112,2048]{1,0:T(8,128)(2,1)} %get-tuple-element.29), channel_id=1, source_target_pairs={{0,32},{8,40},{32,64},{40,72},{64,96},{72,104},{96,0},{104,8},{1,3... | collective-permute-start | bytes 1376264 | tf_op jit(solution)/shard_map/ppermute | solution.py:511
  86.1 24.9 %collective-permute-start.4 = (bf16[112,2048]{1,0:T(8,128)(2,1)}, bf16[112,2048]{1,0:T(8,128)(2,1)S(1)}, u32[]{:S(2)}, u32[]{:S(2)}) collective-permute-start(bf16[112,2048]{1,0:T(8,128)(2,1)} %get-tuple-element.30), channel_id=1, source_target_pairs={{0,64},{8,72},{32,96},{40,104},{64,0},{72,8},{96,32},{104,40},{1,6... | collective-permute-start | bytes 1376264 | tf_op jit(solution)/shard_map/ppermute | solution.py:511
  88.7 22.6 %collective-permute-start.5 = (bf16[112,2048]{1,0:T(8,128)(2,1)}, bf16[112,2048]{1,0:T(8,128)(2,1)S(1)}, u32[]{:S(2)}, u32[]{:S(2)}) collective-permute-start(bf16[112,2048]{1,0:T(8,128)(2,1)} %get-tuple-element.31), channel_id=1, source_target_pairs={{0,96},{8,104},{32,0},{40,8},{64,32},{72,40},{96,64},{104,72},{1,9... | collective-permute-start | bytes 1376264 | tf_op jit(solution)/shard_map/ppermute | solution.py:511
  89.7 21.6 %collective-permute-start.6 = (bf16[112,2048]{1,0:T(8,128)(2,1)}, bf16[112,2048]{1,0:T(8,128)(2,1)S(1)}, u32[]{:S(2)}, u32[]{:S(2)}) collective-permute-start(bf16[112,2048]{1,0:T(8,128)(2,1)} %get-tuple-element.32), channel_id=1, source_target_pairs={{0,8},{8,0},{32,40},{40,32},{64,72},{72,64},{96,104},{104,96},{1,9... | collective-permute-start | bytes 1376264 | tf_op jit(solution)/shard_map/ppermute | solution.py:511
  90.6 27.9 %collective-permute-start.7 = (bf16[112,2048]{1,0:T(8,128)(2,1)S(1)}, bf16[112,2048]{1,0:T(8,128)(2,1)S(1)}, u32[]{:S(2)}, u32[]{:S(2)}) collective-permute-start(bf16[112,2048]{1,0:T(8,128)(2,1)S(1)} %copy-done.9), channel_id=1, source_target_pairs={{0,40},{8,32},{32,72},{40,64},{64,104},{72,96},{96,8},{104,0},{1,4... | collective-permute-start | bytes 1376264 | tf_op jit(solution)/shard_map/ppermute | solution.py:511
  98.4 31.7 %copy-start.3 = (bf16[112,2048]{1,0:T(8,128)(2,1)}, bf16[112,2048]{1,0:T(8,128)(2,1)S(1)}, u32[]{:S(2)}) copy-start(bf16[112,2048]{1,0:T(8,128)(2,1)S(1)} %collective-permute-done.3.refs_1_) | copy-start | bytes 1376260
  98.4 30.8 %collective-permute-start.8 = (bf16[112,2048]{1,0:T(8,128)(2,1)S(1)}, bf16[112,2048]{1,0:T(8,128)(2,1)S(1)}, u32[]{:S(2)}, u32[]{:S(2)}) collective-permute-start(bf16[112,2048]{1,0:T(8,128)(2,1)S(1)} %copy-done.7), channel_id=1, source_target_pairs={{0,72},{8,64},{32,104},{40,96},{64,8},{72,0},{96,40},{104,32},{1,7... | collective-permute-start | bytes 1376264 | tf_op jit(solution)/shard_map/ppermute | solution.py:511
  111.0 19.0 %copy-start.4 = (bf16[112,2048]{1,0:T(8,128)(2,1)}, bf16[112,2048]{1,0:T(8,128)(2,1)S(1)}, u32[]{:S(2)}) copy-start(bf16[112,2048]{1,0:T(8,128)(2,1)S(1)} %collective-permute-done.4.refs_2_) | copy-start | bytes 1376260
  111.0 19.0 %collective-permute-start.9 = (bf16[112,2048]{1,0:T(8,128)(2,1)S(1)}, bf16[112,2048]{1,0:T(8,128)(2,1)}, u32[]{:S(2)}, u32[]{:S(2)}) collective-permute-start(bf16[112,2048]{1,0:T(8,128)(2,1)S(1)} %copy-done.5), channel_id=1, source_target_pairs={{0,104},{8,96},{32,8},{40,0},{64,40},{72,32},{96,72},{104,64},{1,1... | collective-permute-start | bytes 1376264 | tf_op jit(solution)/shard_map/ppermute | solution.py:511
  111.3 18.7 %copy-start.6 = (bf16[112,2048]{1,0:T(8,128)(2,1)}, bf16[112,2048]{1,0:T(8,128)(2,1)S(1)}, u32[]{:S(2)}) copy-start(bf16[112,2048]{1,0:T(8,128)(2,1)S(1)} %collective-permute-done.5.refs_3_) | copy-start | bytes 1376260
  111.3 18.7 %copy-start.8 = (bf16[112,2048]{1,0:T(8,128)(2,1)}, bf16[112,2048]{1,0:T(8,128)(2,1)S(1)}, u32[]{:S(2)}) copy-start(bf16[112,2048]{1,0:T(8,128)(2,1)S(1)} %collective-permute-done.6.refs_4_) | copy-start | bytes 1376260
  118.5 10.7 %copy-start.10 = (bf16[112,2048]{1,0:T(8,128)(2,1)}, bf16[112,2048]{1,0:T(8,128)(2,1)S(1)}, u32[]{:S(2)}) copy-start(bf16[112,2048]{1,0:T(8,128)(2,1)S(1)} %collective-permute-done.7.refs_5_) | copy-start | bytes 1376260
  129.2 0.8 copy-start.11
  165.7 65.0 %all-to-all-start.2 = ((bf16[32,28,2176]{2,1,0:T(8,128)(2,1)}), bf16[32,28,2176]{2,1,0:T(8,128)(2,1)}, u32[]{:S(2)}, u32[]{:S(2)}) async-start(bf16[32,28,2176]{2,1,0:T(8,128)(2,1)} %shard_map.97), calls=%async_computation.2 | async-start | bytes 8912896 | tf_op jit(solution)/shard_map/all_to_all | solution.py:520
  172.4 81.8 %reduce-scatter.3.cloned.1.call-start = ((), (), s32[]{:S(2)}) async-start(), calls=%async_computation.7 | async-start | bytes 5570560 | tf_op jit(solution)/shard_map/reduce_scatter | solution.py:516
  203.2 51.7 %collective-permute-start.11 = (bf16[256,2176]{1,0:T(8,128)(2,1)}, bf16[256,2176]{1,0:T(8,128)(2,1)}, u32[]{:S(2)}, u32[]{:S(2)}) collective-permute-start(bf16[256,2176]{1,0:T(8,128)(2,1)} %reduce-scatter.5.cloned.1.call-done), channel_id=1, source_target_pairs={{0,4},{4,0},{1,5},{5,1},{2,6},{6,2},{3,7},{7,3},{8,12},{12,8},{9,1... | collective-permute-start | bytes 3342344 | tf_op jit(solution)/shard_map/ppermute | solution.py:517
Sparse Core Ops, SparseCore 0:
  12.5 53.6 all-gather.2
  70.8 51.9 all-gather.4
  154.0 49.1 reduce-scatter.4
  205.5 48.6 reduce-scatter.2

commit v4 on v3

--- a/solution.py
+++ b/solution.py
@@ -38,7 +38,15 @@
     return pl.CostEstimate(flops=flops, bytes_accessed=moved, transcendentals=0)
 
 
-def prepare_kernel(sc, tok, cot, routes, probs, gate_up, down, out_tok, out_cot, own, oth):
+def prepare_kernel(sc, tok, cot, routes, probs, gate_up, down, *refs):
+    out_tok, out_cot, own, oth, tok_row, cot_row, packed, sems = refs
+    copies = []
+
+    def put(src, dst):
+        copy = pltpu.make_async_copy(src, dst, sems.at[len(copies)])
+        copy.start()
+        copies.append(copy)
+
     z_hi = sc[3]
     line = lax.broadcasted_iota(jnp.int32, (128, TOK), 0)
     meta = jnp.zeros((128, TOK), F32)
@@ -48,15 +56,20 @@
         meta = jnp.where(line == k, chosen[k : k + 1, :], meta)
         meta = jnp.where(line == 8 + k, weight[k : k + 1, :], meta)
     meta = meta.T.astype(BF)
+    tok_row[:, :D] = tok[...]
+    tok_row[:, D:] = meta
     for n in range(4):
-        out_tok[n, :, :D] = tok[...]
-        out_tok[n, :, D:] = meta
-    out_cot[:, :D] = cot[...]
-    out_cot[:, D:] = meta
-    for out, which in ((own, z_hi), (oth, 1 - z_hi)):
-        out[:, : 2 * F] = gate_up[which]
-        out[:, 2 * F : 3 * F] = down[which].T
-        out[:, 3 * F :] = jnp.zeros((256, PACK - 3 * F), BF)
+        put(tok_row, out_tok.at[n])
+    cot_row[:, :D] = cot[...]
+    cot_row[:, D:] = meta
+    put(cot_row, out_cot)
+    for i, (out, which) in enumerate(((own, z_hi), (oth, 1 - z_hi))):
+        packed[i, :, : 2 * F] = gate_up[which]
+        packed[i, :, 2 * F : 3 * F] = down[which].T
+        packed[i, :, 3 * F :] = jnp.zeros((256, PACK - 3 * F), BF)
+        put(packed.at[i], out)
+    for copy in copies:
+        copy.wait()
 
 
 def prepare(sc, tokens, cotangent, routes, probs, w_gate_up, w_down):
@@ -66,8 +79,14 @@
     return pl.pallas_call(
         prepare_kernel,
         in_specs=[pl.BlockSpec(memory_space=pltpu.SMEM)] + [vmem] * 6,
-        out_specs=[vmem] * 4,
+        out_specs=[pl.BlockSpec(memory_space=pl.ANY)] * 4,
         out_shape=(jax.ShapeDtypeStruct((4, TOK, WIDE), BF), wide, shard, shard),
+        scratch_shapes=[
+            pltpu.VMEM((TOK, WIDE), BF),
+            pltpu.VMEM((TOK, WIDE), BF),
+            pltpu.VMEM((2, 256, PACK), BF),
+            pltpu.SemaphoreType.DMA((7,)),
+        ],
         compiler_params=params(),
         cost_estimate=cost(0, 8 * MIB),
     )(sc, tokens, cotangent, routes, probs, w_gate_up, w_down)
@@ -127,7 +146,7 @@
 
 
 def pick(sc, toks, cots):
-    step = 512
+    step = 1024
     column = lambda n, sc: (0, n)
     tables = [
         pl.BlockSpec((4, TOK, step), lambda n, sc: (0, 0, n)),
@@ -291,36 +310,41 @@
     oth = pl.multiple_of((1 - z_hi) * 1024, 1024)
     pairs = (
         (d_both_in, d_both),
-        (w_own.at[:, pl.ds(0, 2 * F)], w.at[pl.ds(own, 1024)]),
-        (w_oth.at[:, pl.ds(0, 2 * F)], w.at[pl.ds(oth, 1024)]),
+        (w_own.at[:, pl.ds(0, 2 * F)], w.at[0]),
+        (w_oth.at[:, pl.ds(0, 2 * F)], w.at[1]),
     )
     loads = [pltpu.make_async_copy(*pair, sem_in.at[i]) for i, pair in enumerate(pairs)]
     stores = []
     for copy in loads:
         copy.start()
     extra = q[...].astype(F32)
-    for copy in loads:
-        copy.wait()
-    for m in range(2):
-        part = slice(m * tile, (m + 1) * tile)
-        rows = mm(d_both[part, :], w[...], 1, 1)
-        for to_y in range(4):
-            for j in range(4):
-                first, block = j * BLK + to_y * CAP, to_y * 8 + m * 4 + j
-                dx[block, :, :D] = rows[first : first + CAP, :].astype(BF)
-                first += m * tile
-                dx[block, :, D:] = extra[first : first + CAP, :].astype(BF)
-            span = pl.ds(to_y * 8 + m * 4, 4)
-            copy = pltpu.make_async_copy(dx.at[span], dx_out.at[span], sem_out.at[len(stores)])
-            copy.start()
-            stores.append(copy)
+    loads[0].wait()
+    for side, start in enumerate((own, oth)):
+        loads[1 + side].wait()
+        for m in range(2):
+            part = slice(m * tile, (m + 1) * tile)
+            rows = mm(d_both[part, :], w[side], 1, 1)
+            for to_y in range(4):
+                for j in range(4):
+                    first, block = j * BLK + to_y * CAP, to_y * 8 + m * 4 + j
+                    dx[block, :, pl.ds(start, 1024)] = rows[first : first + CAP, :].astype(BF)
+                    if side:
+                        first += m * tile
+                        dx[block, :, D:] = extra[first : first + CAP, :].astype(BF)
+                if side:
+                    span = pl.ds(to_y * 8 + m * 4, 4)
+                    copy = pltpu.make_async_copy(
+                        dx.at[span], dx_out.at[span], sem_out.at[len(stores)]
+                    )
+                    copy.start()
+                    stores.append(copy)
     for copy in stores:
         copy.wait()
 
 
 def input_grads(sc, d_both, q, w_own, w_oth):
     anywhere = pl.BlockSpec(memory_space=pl.ANY)
-    scratch = [(ROWS, 2 * F), (D, 2 * F), (EXPERTS, CAP, WIDE)]
+    scratch = [(ROWS, 2 * F), (2, 1024, 2 * F), (EXPERTS, CAP, WIDE)]
     return pl.pallas_call(
         inputs_kernel,
         in_specs=[

time: 265 us -> 264 us (level)
  transfers between devices with their start and end apart: 19 -> 19, of which waited for: 9 -> 8; matrix products, arithmetic and copies ran while one was open for 0% -> 0% of each run, Pallas kernels for 13% -> 13%
where the time goes in v4:
time: 264 us
  waiting for transfers between devices  137 us (52%)
  Pallas kernels  65.2 us (25%)
  starting transfers between devices  45.8 us (17%)
  between operations  14 us (5%)
    ppermute x3, waiting for transfers between devices, body(): lax.ppermute(cot, ('zl', 'zh'), along_z(k))  46.5 us
    reduce_scatter x2, waiting for transfers between devices, body(): lax.psum_scatter(g, 'x', scatter_dimension=0, tiled=True)  41.4 us
    ppermute x7, waiting for transfers between devices, body(): lax.ppermute(sent[j], ('y', 'c'), along_yc(j % 4, j // 4))  25.3 us
    all_to_all x1, waiting for transfers between devices, body(): lax.all_to_all(dx, ('y', 'zl', 'c', 'zh'), split_axis=0, concat_axis=0, t...  23.9 us
    pallas_call x1, Pallas kernels, expert_pass(): pl.pallas_call(expert_kernel, in_specs=[pl.BlockSpec(memory_space=pltpu.S...  23.8 us
    ppermute x7, starting transfers between devices, body(): lax.ppermute(sent[j], ('y', 'c'), along_yc(j % 4, j // 4))  19.1 us
    pallas_call x1, Pallas kernels, input_grads(): pl.pallas_call(inputs_kernel, in_specs=[pl.BlockSpec(memory_space=pltpu.S...  11.1 us
    pallas_call x1, Pallas kernels, own_grads(): pl.pallas_call(grads_kernel, in_specs=[pl.BlockSpec(memory_space=pltpu.SM...  10.2 us
  transfers between devices with their start and end apart: 19, of which 8 were waited for; matrix products, arithmetic and copies ran while one was open for 0% of the time, Pallas kernels for 13%

profile of v4, /device:TPU:1, one launch (start us, length us, event | category | flops | bytes accessed | tf_op | source)
XLA Modules:
  0.0 263.6 jit_solution(1306809405333840174)
XLA Ops:
  7.2 0.0 all-gather.3.cloned.1.call-start
  7.2 0.6 stack.23.sc
  7.8 4.4 %shard_map.93 = (bf16[4,128,2176]{2,1,0:T(8,128)(2,1)}, bf16[128,2176]{1,0:T(8,128)(2,1)}, bf16[256,2176]{1,0:T(8,128)(2,1)}, bf16[256,2176]{1,0:T(8,128)(2,1)}) custom-call(s32[5]{0:T(128)} %stack.23.sc, bf16[128,2048]{1,0:T(8,128)(2,1)} %tok.1, bf16[128,2048]{1,0:T(8,128)(2,1)} %cot.1, s32[6,128]{1,0:T(8,128)} %bitcast.11, f32[6,128]{1,0:T(8,128)} %bitcast.13, ...), custom_call_target="tpu_custom_call" | custom-call | bytes 8388608 | tf_op jit(solution)/shard_map/pallas_call | solution.py:79
  12.3 0.0 all-gather.3.cloned.1.call-update
  12.3 0.0 copy-start.1
  12.3 0.0 copy-start.2
  12.3 5.2 %all-to-all-start = ((bf16[4,128,2176]{2,1,0:T(8,128)(2,1)}), bf16[4,128,2176]{2,1,0:T(8,128)(2,1)}, u32[]{:S(2)}, u32[]{:S(2)}) async-start(bf16[4,128,2176]{2,1,0:T(8,128)(2,1)} %get-tuple-element.26), calls=%async_computation | async-start | bytes 4456448 | tf_op jit(solution)/shard_map/all_to_all | solution.py:524
  17.5 0.0 all-gather.5.cloned.1.call-start
  17.5 0.0 copy-done.1
  17.5 4.1 %collective-permute-start.10 = (bf16[256,2176]{1,0:T(8,128)(2,1)S(1)}, bf16[256,2176]{1,0:T(8,128)(2,1)}, u32[]{:S(2)}, u32[]{:S(2)}) collective-permute-start(bf16[256,2176]{1,0:T(8,128)(2,1)S(1)} %copy-done.1), channel_id=1, source_target_pairs={{0,4},{4,0},{1,5},{5,1},{2,6},{6,2},{3,7},{7,3},{8,12},{12,8},{9,1... | collective-permute-start | bytes 3342344 | tf_op jit(solution)/shard_map/ppermute | solution.py:527
  21.5 0.0 copy-done.2
  21.5 0.4 collective-permute-start.2
  22.0 2.1 collective-permute-start.1
  24.1 0.0 collective-permute-start
  24.1 34.5 %collective-permute-done.2.refs_5_.refs_9_.rest_3_ = bf16[128,2176]{1,0:T(8,128)(2,1)S(1)} collective-permute-done((bf16[128,2176]{1,0:T(8,128)(2,1)S(1)}, bf16[128,2176]{1,0:T(8,128)(2,1)S(1)}, u32[]{:S(2)}, u32[]{:S(2)}) %collective-permute-start.2) | collective-permute-done | bytes 557088 | tf_op jit(solution)/shard_map/ppermute | solution.py:523
  58.6 0.0 collective-permute-done.1.refs_4_.refs_8_.rest_2_
  58.6 11.9 %collective-permute-done.refs_3_.refs_7_.rest_1_ = bf16[128,2176]{1,0:T(8,128)(2,1)} collective-permute-done((bf16[128,2176]{1,0:T(8,128)(2,1)S(1)}, bf16[128,2176]{1,0:T(8,128)(2,1)}, u32[]{:S(2)}, u32[]{:S(2)}) %collective-permute-start) | collective-permute-done | bytes 557088 | tf_op jit(solution)/shard_map/ppermute | solution.py:523
  70.6 0.0 collective-permute-done.10.value
  70.6 0.0 all-to-all-done.refs_0_.refs_1_.rest_0_
  70.6 0.0 copy-done
  70.6 0.0 all-gather.5.cloned.1.call-update
  70.6 8.6 %shard_map.94 = (bf16[896,2048]{1,0:T(8,128)(2,1)}, bf16[112,2048]{1,0:T(8,128)(2,1)}, bf16[112,2048]{1,0:T(8,128)(2,1)}, bf16[112,2048]{1,0:T(8,128)(2,1)}, bf1...) custom-call(s32[5]{0:T(128)} %stack.23.sc, ...), custom_call_target="tpu_custom_call" | custom-call | flops 3758096384 | bytes 16777216 | tf_op jit(solution)/shard_map/pallas_call | solution.py:157
  79.3 0.0 copy-start.9
  79.3 0.0 copy-start.7
  79.3 0.0 copy-start.5
  79.3 5.4 %all-to-all-start.1 = ((bf16[8,112,2048]{2,1,0:T(8,128)(2,1)}), bf16[8,112,2048]{2,1,0:T(8,128)(2,1)}, u32[]{:S(2)}, u32[]{:S(2)}) async-start(bf16[8,112,2048]{2,1,0:T(8,128)(2,1)} %bitcast.10), calls=%async_computation.1 | async-start | bytes 7340032 | tf_op jit(solution)/shard_map/all_to_all | solution.py:531
  84.6 0.0 reduce-scatter.5.cloned.1.call-start
  84.7 1.3 collective-permute-start.3
  86.0 2.6 collective-permute-start.4
  88.6 1.1 collective-permute-start.5
  89.6 0.9 collective-permute-start.6
  90.6 0.0 copy-done.9
  90.6 0.3 collective-permute-start.7
  90.8 7.4 %collective-permute-done.3.refs_1_ = bf16[112,2048]{1,0:T(8,128)(2,1)S(1)} collective-permute-done((bf16[112,2048]{1,0:T(8,128)(2,1)}, bf16[112,2048]{1,0:T(8,128)(2,1)S(1)}, u32[]{:S(2)}, u32[]{:S(2)}) %collective-permute-start.3) | collective-permute-done | bytes 458784 | tf_op jit(solution)/shard_map/ppermute | solution.py:535
  98.3 0.0 copy-done.7
  98.3 12.6 %collective-permute-start.8 = (bf16[112,2048]{1,0:T(8,128)(2,1)S(1)}, bf16[112,2048]{1,0:T(8,128)(2,1)S(1)}, u32[]{:S(2)}, u32[]{:S(2)}) collective-permute-start(bf16[112,2048]{1,0:T(8,128)(2,1)S(1)} %copy-done.7), channel_id=1, source_target_pairs={{0,72},{8,64},{32,104},{40,96},{64,8},{72,0},{96,40},{104,32},{1,7... | collective-permute-start | bytes 1376264 | tf_op jit(solution)/shard_map/ppermute | solution.py:535
  110.9 0.0 collective-permute-done.4.refs_2_
  110.9 0.0 copy-done.5
  110.9 0.3 collective-permute-start.9
  111.2 0.0 collective-permute-done.5.refs_3_
  111.2 0.0 collective-permute-done.6.refs_4_
  111.2 7.2 %collective-permute-done.7.refs_5_ = bf16[112,2048]{1,0:T(8,128)(2,1)S(1)} collective-permute-done((bf16[112,2048]{1,0:T(8,128)(2,1)S(1)}, bf16[112,2048]{1,0:T(8,128)(2,1)S(1)}, u32[]{:S(2)}, u32[]{:S(2)}) %collective-permute-start.7) | collective-permute-done | bytes 458784 | tf_op jit(solution)/shard_map/ppermute | solution.py:535
  118.4 10.7 %collective-permute-done.8.refs_6_ = bf16[112,2048]{1,0:T(8,128)(2,1)S(1)} collective-permute-done((bf16[112,2048]{1,0:T(8,128)(2,1)S(1)}, bf16[112,2048]{1,0:T(8,128)(2,1)S(1)}, u32[]{:S(2)}, u32[]{:S(2)}) %collective-permute-start.8) | collective-permute-done | bytes 458784 | tf_op jit(solution)/shard_map/ppermute | solution.py:535
  129.1 0.8 copy-done.11
  129.9 0.0 collective-permute-done.9.refs_7_
  129.9 0.0 all-to-all-done.1
  129.9 0.0 all-gather.3.cloned.1.call-done.refs_9_.w_own
  129.9 0.0 all-gather.5.cloned.1.call-done.refs_10_.w_oth
  129.9 0.0 copy-done.3
  129.9 0.0 copy-done.4
  130.0 23.8 %shard_map.96 = (bf16[896,2048]{1,0:T(8,128)(2,1)}, bf16[896,1408]{1,0:T(8,128)(2,1)}, bf16[896,704]{1,0:T(8,128)(2,1)}, bf16[896,128]{1,0:T(8,128)(2,1)}, bf16[1024,2176]{1,0:T(8,128)(2,1)}) custom-call(s32[5]{0:T(128)} %stack.23.sc, bf16[112,2048]{1,0:T(8,128)(2,1)} %get-tuple-element.28.refs_0_, bf16[112,2048]{1,0:T(8,128)(2,1)} %copy-done.3, ...), custom_call_target="tpu_custom_call" | custom-call | flops 15502147584 | bytes 33554432 | tf_op jit(solution)/shard_map/pallas_call | solution.py:294
  153.8 0.0 reduce-scatter.5.cloned.1.call-update
  153.8 11.1 %shard_map.97 = bf16[32,28,2176]{2,1,0:T(8,128)(2,1)} custom-call(s32[5]{0:T(128)} %stack.23.sc, bf16[896,1408]{1,0:T(8,128)(2,1)} %get-tuple-element.39.d_both_in, bf16[896,128]{1,0:T(8,128)(2,1)} %get-tuple-element.40.q, bf16[1024,2176]{1,0:T(8,128)(2,1)} %all-gather.3.cloned.1.call-done.refs_9_.w_own, ...), custom_call_target="tpu_custom_call" | custom-call | flops 5167382528 | bytes 16777216 | tf_op jit(solution)/shard_map/pallas_call | solution.py:348
  164.9 6.7 %all-to-all-start.2 = ((bf16[32,28,2176]{2,1,0:T(8,128)(2,1)}), bf16[32,28,2176]{2,1,0:T(8,128)(2,1)}, u32[]{:S(2)}, u32[]{:S(2)}) async-start(bf16[32,28,2176]{2,1,0:T(8,128)(2,1)} %shard_map.97), calls=%async_computation.2 | async-start | bytes 8912896 | tf_op jit(solution)/shard_map/all_to_all | solution.py:544
  171.6 0.0 reduce-scatter.3.cloned.1.call-start
  171.6 10.2 %shard_map.99 = bf16[1024,2176]{1,0:T(8,128)(2,1)} custom-call(s32[5]{0:T(128)} %stack.23.sc, bf16[896,2048]{1,0:T(8,128)(2,1)} %bitcast.8.refs_8_.x_in, bf16[896,2048]{1,0:T(8,128)(2,1)} %get-tuple-element.43.scaled_in, bf16[896,1408]{1,0:T(8,128)(2,1)} %get-tuple-element.39.d_both_in, bf16[896,704]{1,0:T(8,128)(2,1)} %get-tuple-element.44.hidden_in), custom_call_target="tpu_custom_call" | custom-call | flops 3875536896 | bytes 12582912 | tf_op jit(solution)/shard_map/pallas_call | solution.py:397
  181.8 0.0 reduce-scatter.3.cloned.1.call-update
  181.9 21.3 %reduce-scatter.5.cloned.1.call-done = bf16[256,2176]{1,0:T(8,128)(2,1)} async-done(((bf16[1024,2176]{1,0:T(8,128)(2,1)}), bf16[256,2176]{1,0:T(8,128)(2,1)}) %reduce-scatter.5.cloned.1.call-update) | async-done | bytes 1114128 | tf_op jit(solution)/shard_map/reduce_scatter | solution.py:540
  203.1 2.9 %collective-permute-start.11 = (bf16[256,2176]{1,0:T(8,128)(2,1)}, bf16[256,2176]{1,0:T(8,128)(2,1)}, u32[]{:S(2)}, u32[]{:S(2)}) collective-permute-start(bf16[256,2176]{1,0:T(8,128)(2,1)} %reduce-scatter.5.cloned.1.call-done), channel_id=1, source_target_pairs={{0,4},{4,0},{1,5},{5,1},{2,6},{6,2},{3,7},{7,3},{8,12},{12,8},{9,1... | collective-permute-start | bytes 3342344 | tf_op jit(solution)/shard_map/ppermute | solution.py:541
  206.0 23.9 %all-to-all-done.2.back = bf16[32,28,2176]{2,1,0:T(8,128)(2,1)} async-done(((bf16[32,28,2176]{2,1,0:T(8,128)(2,1)}), bf16[32,28,2176]{2,1,0:T(8,128)(2,1)}, u32[]{:S(2)}, u32[]{:S(2)}) %all-to-all-start.2) | async-done | bytes 3899424 | tf_op jit(solution)/shard_map/all_to_all | solution.py:544
  229.9 4.0 %shard_map.98 = (bf16[128,2048]{1,0:T(8,128)(2,1)}, f32[6,128]{1,0:T(8,128)}) custom-call(bf16[32,28,2176]{2,1,0:T(8,128)(2,1)} %all-to-all-done.2.back, s32[6,128]{1,0:T(8,128)} %bitcast.12, f32[6,128]{1,0:T(8,128)} %bitcast.14), custom_call_target="tpu_custom_call" | custom-call | flops 99999997952 | bytes 8388608 | tf_op jit(solution)/shard_map/pallas_call | solution.py:455
  233.9 20.2 %reduce-scatter.3.cloned.1.call-done.own = bf16[256,2176]{1,0:T(8,128)(2,1)} async-done(((bf16[1024,2176]{1,0:T(8,128)(2,1)}), bf16[256,2176]{1,0:T(8,128)(2,1)}) %reduce-scatter.3.cloned.1.call-update) | async-done | bytes 1114128 | tf_op jit(solution)/shard_map/reduce_scatter | solution.py:540
  254.1 0.0 collective-permute-done.11.oth
  254.1 3.0 %shard_map.100 = (bf16[2,256,1408]{2,1,0:T(8,128)(2,1)}, bf16[2,704,256]{2,1,0:T(8,128)(2,1)}) custom-call(s32[5]{0:T(128)} %stack.23.sc, bf16[256,2176]{1,0:T(8,128)(2,1)} %reduce-scatter.3.cloned.1.call-done.own, bf16[256,2176]{1,0:T(8,128)(2,1)} %collective-permute-done.11.oth), custom_call_target="tpu_custom_call" | custom-call | bytes 5242880 | tf_op jit(solution)/shard_map/pallas_call | solution.py:487
  (11 shorter events, 0.0 us)
Async XLA Ops:
  7.2 122.7 %all-gather.3.cloned.1.call-start = ((), (), s32[]{:S(2)}) async-start(), calls=%async_computation.5 | async-start | bytes 5570560 | tf_op jit(solution)/shard_map/all_gather | solution.py:526
  12.3 5.2 %copy-start.1 = (bf16[256,2176]{1,0:T(8,128)(2,1)S(1)}, bf16[256,2176]{1,0:T(8,128)(2,1)}, u32[]{:S(2)}) copy-start(bf16[256,2176]{1,0:T(8,128)(2,1)} %get-tuple-element.38) | copy-start | bytes 3342340
  12.3 9.2 %copy-start.2 = (bf16[128,2176]{1,0:T(8,128)(2,1)S(1)}, bf16[128,2176]{1,0:T(8,128)(2,1)}, u32[]{:S(2)}) copy-start(bf16[128,2176]{1,0:T(8,128)(2,1)} %get-tuple-element.27.refs_2_.refs_6_) | copy-start | bytes 1671172
  12.3 58.2 %all-to-all-start = ((bf16[4,128,2176]{2,1,0:T(8,128)(2,1)}), bf16[4,128,2176]{2,1,0:T(8,128)(2,1)}, u32[]{:S(2)}, u32[]{:S(2)}) async-start(bf16[4,128,2176]{2,1,0:T(8,128)(2,1)} %get-tuple-element.26), calls=%async_computation | async-start | bytes 4456448 | tf_op jit(solution)/shard_map/all_to_all | solution.py:524
  17.5 112.4 %all-gather.5.cloned.1.call-start = ((), (), s32[]{:S(2)}) async-start(), calls=%async_computation.6 | async-start | bytes 5570560 | tf_op jit(solution)/shard_map/all_gather | solution.py:526
  17.5 53.1 %collective-permute-start.10 = (bf16[256,2176]{1,0:T(8,128)(2,1)S(1)}, bf16[256,2176]{1,0:T(8,128)(2,1)}, u32[]{:S(2)}, u32[]{:S(2)}) collective-permute-start(bf16[256,2176]{1,0:T(8,128)(2,1)S(1)} %copy-done.1), channel_id=1, source_target_pairs={{0,4},{4,0},{1,5},{5,1},{2,6},{6,2},{3,7},{7,3},{8,12},{12,8},{9,1... | collective-permute-start | bytes 3342344 | tf_op jit(solution)/shard_map/ppermute | solution.py:527
  21.5 37.1 %collective-permute-start.2 = (bf16[128,2176]{1,0:T(8,128)(2,1)S(1)}, bf16[128,2176]{1,0:T(8,128)(2,1)S(1)}, u32[]{:S(2)}, u32[]{:S(2)}) collective-permute-start(bf16[128,2176]{1,0:T(8,128)(2,1)S(1)} %copy-done.2), channel_id=1, source_target_pairs={{0,20},{16,0},{4,16},{20,4},{1,21},{17,1},{5,17},{21,5},{2,22},{18... | collective-permute-start | bytes 1671176 | tf_op jit(solution)/shard_map/ppermute | solution.py:523
  22.0 36.6 %collective-permute-start.1 = (bf16[128,2176]{1,0:T(8,128)(2,1)S(1)}, bf16[128,2176]{1,0:T(8,128)(2,1)}, u32[]{:S(2)}, u32[]{:S(2)}) collective-permute-start(bf16[128,2176]{1,0:T(8,128)(2,1)S(1)} %copy-done.2), channel_id=1, source_target_pairs={{0,4},{16,20},{4,0},{20,16},{1,5},{17,21},{5,1},{21,17},{2,6},{18,... | collective-permute-start | bytes 1671176 | tf_op jit(solution)/shard_map/ppermute | solution.py:523
  24.1 46.5 %collective-permute-start = (bf16[128,2176]{1,0:T(8,128)(2,1)S(1)}, bf16[128,2176]{1,0:T(8,128)(2,1)}, u32[]{:S(2)}, u32[]{:S(2)}) collective-permute-start(bf16[128,2176]{1,0:T(8,128)(2,1)S(1)} %copy-done.2), channel_id=1, source_target_pairs={{0,16},{16,4},{4,20},{20,0},{1,17},{17,5},{5,21},{21,1},{2,18},{18... | collective-permute-start | bytes 1671176 | tf_op jit(solution)/shard_map/ppermute | solution.py:523
  58.6 12.0 %copy-start = (bf16[128,2176]{1,0:T(8,128)(2,1)}, bf16[128,2176]{1,0:T(8,128)(2,1)S(1)}, u32[]{:S(2)}) copy-start(bf16[128,2176]{1,0:T(8,128)(2,1)S(1)} %collective-permute-done.2.refs_5_.refs_9_.rest_3_) | copy-start | bytes 1671172
  79.3 11.3 %copy-start.9 = (bf16[112,2048]{1,0:T(8,128)(2,1)S(1)}, bf16[112,2048]{1,0:T(8,128)(2,1)}, u32[]{:S(2)}) copy-start(bf16[112,2048]{1,0:T(8,128)(2,1)} %get-tuple-element.33) | copy-start | bytes 1376260
  79.3 19.0 %copy-start.7 = (bf16[112,2048]{1,0:T(8,128)(2,1)S(1)}, bf16[112,2048]{1,0:T(8,128)(2,1)}, u32[]{:S(2)}) copy-start(bf16[112,2048]{1,0:T(8,128)(2,1)} %get-tuple-element.34) | copy-start | bytes 1376260
  79.3 31.6 %copy-start.5 = (bf16[112,2048]{1,0:T(8,128)(2,1)S(1)}, bf16[112,2048]{1,0:T(8,128)(2,1)}, u32[]{:S(2)}) copy-start(bf16[112,2048]{1,0:T(8,128)(2,1)} %get-tuple-element.35) | copy-start | bytes 1376260
  79.3 50.6 %all-to-all-start.1 = ((bf16[8,112,2048]{2,1,0:T(8,128)(2,1)}), bf16[8,112,2048]{2,1,0:T(8,128)(2,1)}, u32[]{:S(2)}, u32[]{:S(2)}) async-start(bf16[8,112,2048]{2,1,0:T(8,128)(2,1)} %bitcast.10), calls=%async_computation.1 | async-start | bytes 7340032 | tf_op jit(solution)/shard_map/all_to_all | solution.py:531
  84.6 118.5 %reduce-scatter.5.cloned.1.call-start = ((), (), s32[]{:S(2)}) async-start(), calls=%async_computation.8 | async-start | bytes 5570560 | tf_op jit(solution)/shard_map/reduce_scatter | solution.py:540
  84.7 13.6 %collective-permute-start.3 = (bf16[112,2048]{1,0:T(8,128)(2,1)}, bf16[112,2048]{1,0:T(8,128)(2,1)S(1)}, u32[]{:S(2)}, u32[]{:S(2)}) collective-permute-start(bf16[112,2048]{1,0:T(8,128)(2,1)} %get-tuple-element.29), channel_id=1, source_target_pairs={{0,32},{8,40},{32,64},{40,72},{64,96},{72,104},{96,0},{104,8},{1,3... | collective-permute-start | bytes 1376264 | tf_op jit(solution)/shard_map/ppermute | solution.py:535
  86.0 24.9 %collective-permute-start.4 = (bf16[112,2048]{1,0:T(8,128)(2,1)}, bf16[112,2048]{1,0:T(8,128)(2,1)S(1)}, u32[]{:S(2)}, u32[]{:S(2)}) collective-permute-start(bf16[112,2048]{1,0:T(8,128)(2,1)} %get-tuple-element.30), channel_id=1, source_target_pairs={{0,64},{8,72},{32,96},{40,104},{64,0},{72,8},{96,32},{104,40},{1,6... | collective-permute-start | bytes 1376264 | tf_op jit(solution)/shard_map/ppermute | solution.py:535
  88.6 22.6 %collective-permute-start.5 = (bf16[112,2048]{1,0:T(8,128)(2,1)}, bf16[112,2048]{1,0:T(8,128)(2,1)S(1)}, u32[]{:S(2)}, u32[]{:S(2)}) collective-permute-start(bf16[112,2048]{1,0:T(8,128)(2,1)} %get-tuple-element.31), channel_id=1, source_target_pairs={{0,96},{8,104},{32,0},{40,8},{64,32},{72,40},{96,64},{104,72},{1,9... | collective-permute-start | bytes 1376264 | tf_op jit(solution)/shard_map/ppermute | solution.py:535
  89.6 21.6 %collective-permute-start.6 = (bf16[112,2048]{1,0:T(8,128)(2,1)}, bf16[112,2048]{1,0:T(8,128)(2,1)S(1)}, u32[]{:S(2)}, u32[]{:S(2)}) collective-permute-start(bf16[112,2048]{1,0:T(8,128)(2,1)} %get-tuple-element.32), channel_id=1, source_target_pairs={{0,8},{8,0},{32,40},{40,32},{64,72},{72,64},{96,104},{104,96},{1,9... | collective-permute-start | bytes 1376264 | tf_op jit(solution)/shard_map/ppermute | solution.py:535
  90.6 27.9 %collective-permute-start.7 = (bf16[112,2048]{1,0:T(8,128)(2,1)S(1)}, bf16[112,2048]{1,0:T(8,128)(2,1)S(1)}, u32[]{:S(2)}, u32[]{:S(2)}) collective-permute-start(bf16[112,2048]{1,0:T(8,128)(2,1)S(1)} %copy-done.9), channel_id=1, source_target_pairs={{0,40},{8,32},{32,72},{40,64},{64,104},{72,96},{96,8},{104,0},{1,4... | collective-permute-start | bytes 1376264 | tf_op jit(solution)/shard_map/ppermute | solution.py:535
  98.3 31.7 %copy-start.3 = (bf16[112,2048]{1,0:T(8,128)(2,1)}, bf16[112,2048]{1,0:T(8,128)(2,1)S(1)}, u32[]{:S(2)}) copy-start(bf16[112,2048]{1,0:T(8,128)(2,1)S(1)} %collective-permute-done.3.refs_1_) | copy-start | bytes 1376260
  98.3 30.8 %collective-permute-start.8 = (bf16[112,2048]{1,0:T(8,128)(2,1)S(1)}, bf16[112,2048]{1,0:T(8,128)(2,1)S(1)}, u32[]{:S(2)}, u32[]{:S(2)}) collective-permute-start(bf16[112,2048]{1,0:T(8,128)(2,1)S(1)} %copy-done.7), channel_id=1, source_target_pairs={{0,72},{8,64},{32,104},{40,96},{64,8},{72,0},{96,40},{104,32},{1,7... | collective-permute-start | bytes 1376264 | tf_op jit(solution)/shard_map/ppermute | solution.py:535
  110.9 19.0 %copy-start.4 = (bf16[112,2048]{1,0:T(8,128)(2,1)}, bf16[112,2048]{1,0:T(8,128)(2,1)S(1)}, u32[]{:S(2)}) copy-start(bf16[112,2048]{1,0:T(8,128)(2,1)S(1)} %collective-permute-done.4.refs_2_) | copy-start | bytes 1376260
  110.9 19.0 %collective-permute-start.9 = (bf16[112,2048]{1,0:T(8,128)(2,1)S(1)}, bf16[112,2048]{1,0:T(8,128)(2,1)}, u32[]{:S(2)}, u32[]{:S(2)}) collective-permute-start(bf16[112,2048]{1,0:T(8,128)(2,1)S(1)} %copy-done.5), channel_id=1, source_target_pairs={{0,104},{8,96},{32,8},{40,0},{64,40},{72,32},{96,72},{104,64},{1,1... | collective-permute-start | bytes 1376264 | tf_op jit(solution)/shard_map/ppermute | solution.py:535
  111.2 18.7 %copy-start.6 = (bf16[112,2048]{1,0:T(8,128)(2,1)}, bf16[112,2048]{1,0:T(8,128)(2,1)S(1)}, u32[]{:S(2)}) copy-start(bf16[112,2048]{1,0:T(8,128)(2,1)S(1)} %collective-permute-done.5.refs_3_) | copy-start | bytes 1376260
  111.2 18.7 %copy-start.8 = (bf16[112,2048]{1,0:T(8,128)(2,1)}, bf16[112,2048]{1,0:T(8,128)(2,1)S(1)}, u32[]{:S(2)}) copy-start(bf16[112,2048]{1,0:T(8,128)(2,1)S(1)} %collective-permute-done.6.refs_4_) | copy-start | bytes 1376260
  118.4 10.7 %copy-start.10 = (bf16[112,2048]{1,0:T(8,128)(2,1)}, bf16[112,2048]{1,0:T(8,128)(2,1)S(1)}, u32[]{:S(2)}) copy-start(bf16[112,2048]{1,0:T(8,128)(2,1)S(1)} %collective-permute-done.7.refs_5_) | copy-start | bytes 1376260
  129.1 0.8 copy-start.11
  164.9 65.0 %all-to-all-start.2 = ((bf16[32,28,2176]{2,1,0:T(8,128)(2,1)}), bf16[32,28,2176]{2,1,0:T(8,128)(2,1)}, u32[]{:S(2)}, u32[]{:S(2)}) async-start(bf16[32,28,2176]{2,1,0:T(8,128)(2,1)} %shard_map.97), calls=%async_computation.2 | async-start | bytes 8912896 | tf_op jit(solution)/shard_map/all_to_all | solution.py:544
  171.6 82.5 %reduce-scatter.3.cloned.1.call-start = ((), (), s32[]{:S(2)}) async-start(), calls=%async_computation.7 | async-start | bytes 5570560 | tf_op jit(solution)/shard_map/reduce_scatter | solution.py:540
  203.1 51.0 %collective-permute-start.11 = (bf16[256,2176]{1,0:T(8,128)(2,1)}, bf16[256,2176]{1,0:T(8,128)(2,1)}, u32[]{:S(2)}, u32[]{:S(2)}) collective-permute-start(bf16[256,2176]{1,0:T(8,128)(2,1)} %reduce-scatter.5.cloned.1.call-done), channel_id=1, source_target_pairs={{0,4},{4,0},{1,5},{5,1},{2,6},{6,2},{3,7},{7,3},{8,12},{12,8},{9,1... | collective-permute-start | bytes 3342344 | tf_op jit(solution)/shard_map/ppermute | solution.py:541
Sparse Core Ops, SparseCore 0:
  12.4 53.6 all-gather.2
  70.7 51.9 all-gather.4
  153.9 49.1 reduce-scatter.4
  205.4 48.6 reduce-scatter.2
